TPU v7x, 32 devices: a whole 2x2x4 slice. The times are simulated.
32 devices in a mesh: groups: 2 (over x), grid: 8 (over z, y), rep: 2 (over core).
Axes of the slice: x: 2, y: 2, z: 4, core: 2. Of those that a mesh axis runs over, the one named last changes fastest.
Arguments:
- feats: bfloat16 [14336, 256], P(('groups', 'grid')), parts along dimension 0, may hold values from -6 to 6
- msg_weight: bfloat16 [256, 256], replicated, may hold values from -0.375 to 0.375
- tiles: bfloat16 [16, 2, 1, 896, 896], P(('groups', 'grid'), 'rep'), parts along dimension 0, may hold values from -0.1875 to 0.1875
- tile_step: int32 [16, 2, 1], P(('groups', 'grid'), 'rep'), parts along dimension 0, may hold values from 0 to 3, as said below
- tile_count: int32 [16, 2, 1], P(('groups', 'grid'), 'rep'), parts along dimension 0, may hold values from 0 to 63, as said below
- node_type: int32 [14336], P(('groups', 'grid')), parts along dimension 0, may hold values from 0 to 7
- expert_up: bfloat16 [8, 256, 512], replicated, may hold values from -0.375 to 0.375
- expert_down: bfloat16 [8, 512, 256], replicated, may hold values from -0.25 to 0.25
- out_grad: bfloat16 [14336, 256], P(('groups', 'grid', 'rep')), parts along dimension 0, may hold values from -6 to 6
Outputs:
- updated: bfloat16 [14336, 256], P(('groups', 'grid', 'rep')), parts along dimension 0
- feats_grad: bfloat16 [14336, 256], P(('groups', 'grid', 'rep')), parts along dimension 0
- msg_weight_grad: float32 [512, 256], P('groups'), parts along dimension 0
There are 2 independent parts, one for each index of `groups`. A program takes and returns all parts, laid end to end along the dimension named above; an argument that names none is the same for every part. Nothing has to cross between parts.
Inputs may be any that keep to these rules, and one draw needn't show every extreme that they name: `tile_step`: the 1 local steps of one block row and replica are distinct. `tile_count`: slot 0 of replica 0 is never empty, so every degree is positive.
All inputs are finite; a program needn't handle non-finite values.
Results may differ from a plain program's by a relative error of at most 0.0063.
Values may be sent and summed in bfloat16 or wider, within the bound.
No kernel may reach another device: no remote copies, remote signals or barrier semaphores. Data moves between devices by JAX's collectives and lax.ppermute only.
A program may use at most 64 MiB of HBM per device.

v0:
```python
import jax
import jax.numpy as jnp
from jax import lax
from jax.sharding import PartitionSpec as P


def from_behind(block, axis, distance):
    devices = range(lax.axis_size(axis))
    route = [((i - distance) % len(devices), i) for i in devices]
    return lax.ppermute(block, axis, route)


def ragged_product(rows, weights, group_sizes):
    return lax.ragged_dot(rows, weights, group_sizes, preferred_element_type=jnp.float32)


def per_device(
    feats, msg_weight, tiles, tile_step, tile_count, node_type, expert_up, expert_down, out_grad
):
    loop_size = lax.axis_size("grid")
    half_steps = loop_size // 2
    rep_index = lax.axis_index("rep")
    tile_stack = tiles[0, 0]
    step_table = tile_step[0, 0]
    count_table = tile_count[0, 0].astype(jnp.float32)
    slot_ids = jnp.arange(step_table.shape[0], dtype=jnp.int32)
    block_rows = feats.shape[0]
    share_rows = block_rows // 2
    row_start = rep_index * share_rows

    def pick(step_now):
        matches = step_table == step_now
        weight = jnp.sum(jnp.where(matches, count_table, jnp.float32(0.0)))
        slot_index = jnp.sum(jnp.where(matches, slot_ids, 0))
        return (weight, lax.dynamic_index_in_dim(tile_stack, slot_index, 0, keepdims=False))

    def forward_term(tile_now, holding):
        return jnp.dot(tile_now, holding, preferred_element_type=jnp.float32)

    def backward_term(tile_now, holding):
        return lax.dot_general(
            tile_now, holding, (((0,), (0,)), ((), ())), preferred_element_type=jnp.float32
        )

    def contribute(partial_value, step_now, holding, product_fn):
        weight, tile_now = pick(step_now)
        return partial_value + weight * product_fn(tile_now, holding)

    message = jnp.dot(feats, msg_weight, preferred_element_type=jnp.float32).astype(jnp.bfloat16)
    opposite = from_behind(message, "grid", half_steps)
    holding = jnp.where(rep_index == 0, message, opposite)
    zero_rows = jnp.zeros((block_rows, message.shape[1]), jnp.float32)

    def forward_step(step_now, carry):
        partial_value, current = carry
        partial_value = contribute(partial_value, step_now, current, forward_term)
        current = from_behind(current, "grid", 1)
        return (partial_value, current)

    partial_value, holding = lax.fori_loop(0, half_steps - 1, forward_step, (zero_rows, holding))
    partial_value = contribute(partial_value, half_steps - 1, holding, forward_term)
    count_sum = jnp.sum(count_table)
    total, degree = lax.psum((partial_value, count_sum), "rep")
    aggregate = lax.dynamic_slice_in_dim(total, row_start, share_rows, 0)
    aggregate = aggregate / degree
    inv_rms = lax.rsqrt(jnp.mean(aggregate * aggregate, axis=-1, keepdims=True) + 1e-06)
    normed = aggregate * inv_rms
    normed_bf = normed.astype(jnp.bfloat16)
    row_types = lax.dynamic_slice_in_dim(node_type, row_start, share_rows, 0)
    own_feats = lax.dynamic_slice_in_dim(feats, row_start, share_rows, 0)
    expert_count = expert_up.shape[0]
    ordering = jnp.argsort(row_types, stable=True)
    group_sizes = jnp.sum(
        row_types[None, :] == jnp.arange(expert_count, dtype=jnp.int32)[:, None], axis=1
    )
    up_act = ragged_product(normed_bf[ordering], expert_up, group_sizes)
    hidden = jax.nn.silu(up_act).astype(jnp.bfloat16)
    expert_sorted = ragged_product(hidden, expert_down, group_sizes)
    expert_out = jnp.zeros_like(expert_sorted).at[ordering].set(expert_sorted)
    updated = (own_feats.astype(jnp.float32) + expert_out).astype(jnp.bfloat16)
    grad_hidden = ragged_product(out_grad[ordering], jnp.swapaxes(expert_down, 1, 2), group_sizes)
    sigmoid_act = jax.nn.sigmoid(up_act)
    grad_act = (grad_hidden * sigmoid_act * (1.0 + up_act * (1.0 - sigmoid_act))).astype(
        jnp.bfloat16
    )
    grad_sorted = ragged_product(grad_act, jnp.swapaxes(expert_up, 1, 2), group_sizes)
    grad_pre = jnp.zeros_like(grad_sorted).at[ordering].set(grad_sorted)
    grad_agg = inv_rms * (grad_pre - normed * jnp.mean(grad_pre * normed, axis=-1, keepdims=True))
    grad_scaled = (grad_agg / degree).astype(jnp.bfloat16)
    grad_full = lax.all_gather(grad_scaled, "rep", axis=0, tiled=True)

    def upward_step(step_now, sums_now):
        sums_now = contribute(sums_now, step_now, grad_full, backward_term)
        return from_behind(sums_now, "grid", 1)

    sums_now = lax.fori_loop(0, half_steps, upward_step, zero_rows)
    needs_return = rep_index == 0
    returned = from_behind(sums_now, "grid", half_steps)
    sums_now = jnp.where(needs_return, returned, sums_now)
    grad_msg = lax.psum_scatter(sums_now, "rep", scatter_dimension=0, tiled=True).astype(
        jnp.bfloat16
    )
    back_proj = lax.dot_general(
        grad_msg, msg_weight, (((1,), (1,)), ((), ())), preferred_element_type=jnp.float32
    )
    feats_grad = (out_grad.astype(jnp.float32) + back_proj).astype(jnp.bfloat16)
    weight_term = lax.dot_general(
        own_feats, grad_msg, (((0,), (0,)), ((), ())), preferred_element_type=jnp.float32
    )
    msg_weight_grad = lax.psum(weight_term, ("grid", "rep"))
    return (updated, feats_grad, msg_weight_grad)


def solution(mesh):
    return jax.shard_map(
        per_device,
        mesh=mesh,
        in_specs=(
            P(("groups", "grid"), None),
            P(),
            P(("groups", "grid"), "rep", None, None, None),
            P(("groups", "grid"), "rep", None),
            P(("groups", "grid"), "rep", None),
            P(("groups", "grid")),
            P(),
            P(),
            P(("groups", "grid", "rep"), None),
        ),
        out_specs=(
            P(("groups", "grid", "rep"), None),
            P(("groups", "grid", "rep"), None),
            P("groups", None),
        ),
        check_vma=False,
    )
```

profile of v0, /device:TPU:0, one launch (start us, length us, event | category | flops | bytes accessed | tf_op | source)
XLA Modules:
  0.0 408.6 jit_solution(2685881161554237189)
XLA Ops:
  7.2 0.8 copy-done
  8.1 1.3 convolution_convert_fusion
  9.4 4.1 %collective-permute-start.2 = (bf16[896,256]{1,0:T(8,128)(2,1)S(1)}, bf16[896,256]{1,0:T(8,128)(2,1)}, u32[]{:S(2)}, u32[]{:S(2)}) collective-permute-start(bf16[896,256]{1,0:T(8,128)(2,1)S(1)} %convolution_convert_fusion), channel_id=1, source_target_pairs={{8,0},{10,2},{12,4},{14,6},{0,8},{2,10},{4,12},{6,14},{9,1},{11,3}... | collective-permute-start | bytes 1376264 | tf_op jit(solution)/shard_map/ppermute | solution.py:10
  14.8 19.1 %collective-permute-done.2 = bf16[896,256]{1,0:T(8,128)(2,1)} collective-permute-done((bf16[896,256]{1,0:T(8,128)(2,1)S(1)}, bf16[896,256]{1,0:T(8,128)(2,1)}, u32[]{:S(2)}, u32[]{:S(2)}) %collective-permute-start.2) | collective-permute-done | bytes 458784 | tf_op jit(solution)/shard_map/ppermute | solution.py:10
  33.9 0.8 broadcast_select_fusion.1
  34.8 49.0 %while.32 = (s32[]{:T(128)}, f32[896,256]{1,0:T(8,128)S(1)}, bf16[896,256]{1,0:T(8,128)(2,1)}, s32[1]{0:T(128)}, f32[1]{0:T(128)}, /*index=5*/bf16[1,896,896]{2,1,0:T(8,128)(2,1)S(1)}, s32[]{:T(128)}, f32[1]{0:T(128)}, s32[]{:T(128)}) while((s32[]{:T(128)}, f32[896,256]{1,0:T(8,128)S(1)}, bf16[896,256]{1,0:T(8,128)(2,1)}, ...), condition=%wide.region_2.3_spmd.clone, body=%wide.region_1.2_spmd.clone.sunk | while | flops 411729920 | bytes 6652081 | solution.py:60
  34.8 1.0 copy.52
  35.8 1.6 collective-permute-start.1
  38.0 1.0 fusion.42
  39.0 12.9 %collective-permute-done.1 = bf16[896,256]{1,0:T(8,128)(2,1)} collective-permute-done((bf16[896,256]{1,0:T(8,128)(2,1)S(1)}, bf16[896,256]{1,0:T(8,128)(2,1)}, u32[]{:S(2)}, u32[]{:S(2)}) %collective-permute-start.1) | collective-permute-done | bytes 458784 | tf_op jit(solution)/shard_map/while/body/eval_jaxpr/ppermute | solution.py:10
  51.9 1.0 copy.52
  53.5 1.0 fusion.42
  54.5 13.7 %collective-permute-done.1 = bf16[896,256]{1,0:T(8,128)(2,1)} collective-permute-done((bf16[896,256]{1,0:T(8,128)(2,1)S(1)}, bf16[896,256]{1,0:T(8,128)(2,1)}, u32[]{:S(2)}, u32[]{:S(2)}) %collective-permute-start.1) | collective-permute-done | bytes 458784 | tf_op jit(solution)/shard_map/while/body/eval_jaxpr/ppermute | solution.py:10
  68.2 1.0 copy.52
  69.9 1.0 fusion.42
  70.9 12.9 %collective-permute-done.1 = bf16[896,256]{1,0:T(8,128)(2,1)} collective-permute-done((bf16[896,256]{1,0:T(8,128)(2,1)S(1)}, bf16[896,256]{1,0:T(8,128)(2,1)}, u32[]{:S(2)}, u32[]{:S(2)}) %collective-permute-start.1) | collective-permute-done | bytes 458784 | tf_op jit(solution)/shard_map/while/body/eval_jaxpr/ppermute | solution.py:10
  83.7 1.7 fusion.15
  85.4 1.1 add.108
  86.5 0.0 reduce-scatter.2.cloned.1.call-start
  86.6 3.6 psum.22
  90.2 0.1 dynamic_slice.18
  90.2 3.8 sort.17
  94.0 0.6 convert_reduce_fusion
  94.6 1.5 ragged-dot-metadata
  96.2 4.0 copy.43
  100.1 4.0 copy.44
  104.2 2.6 gather_fusion.1
  106.7 11.1 %ragged-dot-none.1 = f32[448,512]{1,0:T(8,128)} custom-call(s32[1]{0:T(128)} %get-tuple-element.272, s32[9]{0:T(128)} %get-tuple-element.273, s32[14]{0:T(128)} %get-tuple-element.274, s32[14]{0:T(128)} %get-tuple-element.275, s32[1]{0:T(128)} %get-tuple-element.272, bf16[448,256]{1,0:T(8,128)(2,1)} %gather_fusion.1, bf16[8,256,512]{2,1,0:T(8,128)(2,1)} %bitcast.56), custom_call_target="tpu_custom_call" | custom-call | flops 117440512 | bytes 3244064 | tf_op jit(solution)/shard_map/ragged_dot_general/ragged-dot-none
  117.9 1.7 multiply_reduce_fusion.1
  119.6 1.7 multiply_convert_fusion.2
  121.3 2.6 gather_fusion
  123.9 11.2 %ragged-dot-none.3 = f32[448,512]{1,0:T(8,128)} custom-call(s32[1]{0:T(128)} %get-tuple-element.272, s32[9]{0:T(128)} %get-tuple-element.273, s32[14]{0:T(128)} %get-tuple-element.274, s32[14]{0:T(128)} %get-tuple-element.275, s32[1]{0:T(128)} %get-tuple-element.272, bf16[448,256]{1,0:T(8,128)(2,1)} %gather_fusion, bf16[8,256,512]{2,1,0:T(8,128)(2,1)} %param.19), custom_call_target="tpu_custom_call" | custom-call | flops 117440512 | bytes 3244064 | tf_op jit(solution)/shard_map/ragged_dot_general/ragged-dot-none
  135.1 2.5 multiply_convert_fusion
  137.6 11.2 %ragged-dot-none = f32[448,256]{1,0:T(8,128)} custom-call(s32[1]{0:T(128)} %get-tuple-element.272, s32[9]{0:T(128)} %get-tuple-element.273, s32[14]{0:T(128)} %get-tuple-element.274, s32[14]{0:T(128)} %get-tuple-element.275, s32[1]{0:T(128)} %get-tuple-element.272, bf16[448,512]{1,0:T(8,128)(2,1)} %get-tuple-element.351, bf16[8,512,256]{2,1,0:T(8,128)(2,1)} %bitcast.55), custom_call_target="tpu_custom_call" | custom-call | flops 117440512 | bytes 3014688 | tf_op jit(solution)/shard_map/ragged_dot_general/ragged-dot-none
  148.7 2.6 scatter_custom_fusion.1
  151.4 1.8 multiply_reduce_fusion
  153.2 1.8 divide_convert_fusion
  154.9 2.1 all_gather.3
  157.1 0.7 fusion.18
  157.8 0.3 copy.45
  158.1 0.1 broadcast_in_dim.35
  158.2 101.5 %while.31 = (s32[]{:T(128)}, f32[896,256]{1,0:T(8,128)S(1)}, s32[1]{0:T(128)}, f32[1]{0:T(128)}, f32[896,256]{1,0:T(8,128)S(1)}, /*index=5*/s32[]{:T(128)}, f32[1]{0:T(128)}) while((s32[]{:T(128)}, f32[896,256]{1,0:T(8,128)S(1)}, s32[1]{0:T(128)}, f32[1]{0:T(128)}, f32[896,256]{1,0:T(8,128)S(1)}, /*index=5*/s32[]{:T(128)}, ...), condition=%wide.region_11.12_spmd, body=%wide.region_10.11_spmd.sunk | while | flops 458756 | bytes 6422671 | solution.py:96
  158.8 0.1 multiply_add_fusion.2
  158.9 0.1 collective-permute-start
  159.0 25.1 %collective-permute-done = f32[896,256]{1,0:T(8,128)S(1)} collective-permute-done((f32[896,256]{1,0:T(8,128)S(1)}, f32[896,256]{1,0:T(8,128)S(1)}, u32[]{:S(2)}, u32[]{:S(2)}) %collective-permute-start) | collective-permute-done | bytes 917536 | tf_op jit(solution)/shard_map/while/body/eval_jaxpr/ppermute | solution.py:10
  184.7 0.1 multiply_add_fusion.2
  184.9 0.1 collective-permute-start
  184.9 24.2 %collective-permute-done = f32[896,256]{1,0:T(8,128)S(1)} collective-permute-done((f32[896,256]{1,0:T(8,128)S(1)}, f32[896,256]{1,0:T(8,128)S(1)}, u32[]{:S(2)}, u32[]{:S(2)}) %collective-permute-start) | collective-permute-done | bytes 917536 | tf_op jit(solution)/shard_map/while/body/eval_jaxpr/ppermute | solution.py:10
  209.8 0.1 multiply_add_fusion.2
  210.0 0.1 collective-permute-start
  210.0 23.3 %collective-permute-done = f32[896,256]{1,0:T(8,128)S(1)} collective-permute-done((f32[896,256]{1,0:T(8,128)S(1)}, f32[896,256]{1,0:T(8,128)S(1)}, u32[]{:S(2)}, u32[]{:S(2)}) %collective-permute-start) | collective-permute-done | bytes 917536 | tf_op jit(solution)/shard_map/while/body/eval_jaxpr/ppermute | solution.py:10
  234.0 0.1 multiply_add_fusion.2
  234.1 0.1 collective-permute-start
  234.2 25.5 %collective-permute-done = f32[896,256]{1,0:T(8,128)S(1)} collective-permute-done((f32[896,256]{1,0:T(8,128)S(1)}, f32[896,256]{1,0:T(8,128)S(1)}, u32[]{:S(2)}, u32[]{:S(2)}) %collective-permute-start) | collective-permute-done | bytes 917536 | tf_op jit(solution)/shard_map/while/body/eval_jaxpr/ppermute | solution.py:10
  259.7 31.2 %collective-permute-done.3 = f32[896,256]{1,0:T(8,128)S(1)} collective-permute-done((f32[896,256]{1,0:T(8,128)S(1)}, f32[896,256]{1,0:T(8,128)S(1)}, u32[]{:S(2)}, u32[]{:S(2)}) %collective-permute-start.3) | collective-permute-done | bytes 917536 | tf_op jit(solution)/shard_map/ppermute | solution.py:10
  290.9 1.0 broadcast_select_fusion
  291.9 0.0 all-reduce.5.cloned.1.call-start
  292.0 11.2 %ragged-dot-none.2 = f32[448,256]{1,0:T(8,128)} custom-call(s32[1]{0:T(128)} %get-tuple-element.272, s32[9]{0:T(128)} %get-tuple-element.273, s32[14]{0:T(128)} %get-tuple-element.274, s32[14]{0:T(128)} %get-tuple-element.275, s32[1]{0:T(128)} %get-tuple-element.272, bf16[448,512]{1,0:T(8,128)(2,1)} %get-tuple-element.352, bf16[8,512,256]{2,1,0:T(8,128)(2,1)} %param.20), custom_call_target="tpu_custom_call" | custom-call | flops 117440512 | bytes 3014688 | tf_op jit(solution)/shard_map/ragged_dot_general/ragged-dot-none
  303.2 2.6 scatter_custom_fusion
  305.9 0.7 add_convert_fusion
  306.6 2.0 fusion.26
  308.6 2.0 fusion.21
  310.6 89.8 %all-reduce.5.cloned.1.call-done = f32[256,256]{1,0:T(8,128)} async-done(((f32[256,256]{1,0:T(8,128)}), f32[256,256]{1,0:T(8,128)}) %all-reduce.5.cloned.1.call-update) | async-done | bytes 262160 | tf_op jit(solution)/shard_map/psum | solution.py:110
  400.4 1.7 copy.68
  (26 shorter events, 0.2 us)
Async XLA Ops:
  7.2 0.9 copy-start
  7.2 27.6 %copy-start.1 = (bf16[1,1,1,896,896]{4,3,2,1,0:T(8,128)(2,1)S(1)}, bf16[1,1,1,896,896]{4,3,2,1,0:T(8,128)(2,1)}, u32[]{:S(2)}) copy-start(bf16[1,1,1,896,896]{4,3,2,1,0:T(8,128)(2,1)} %param.15) | copy-start | bytes 4816900
  7.2 110.7 %all-reduce.3.cloned.1.call-start = ((), (), s32[]{:S(2)}) async-start(), calls=%async_computation.1 | async-start | bytes 1835008 | tf_op jit(solution)/shard_map/psum | solution.py:63
  9.4 24.6 %collective-permute-start.2 = (bf16[896,256]{1,0:T(8,128)(2,1)S(1)}, bf16[896,256]{1,0:T(8,128)(2,1)}, u32[]{:S(2)}, u32[]{:S(2)}) collective-permute-start(bf16[896,256]{1,0:T(8,128)(2,1)S(1)} %convolution_convert_fusion), channel_id=1, source_target_pairs={{8,0},{10,2},{12,4},{14,6},{0,8},{2,10},{4,12},{6,14},{9,1},{11,3}... | collective-permute-start | bytes 1376264 | tf_op jit(solution)/shard_map/ppermute | solution.py:10
  35.8 16.1 %collective-permute-start.1 = (bf16[896,256]{1,0:T(8,128)(2,1)S(1)}, bf16[896,256]{1,0:T(8,128)(2,1)}, u32[]{:S(2)}, u32[]{:S(2)}) collective-permute-start(bf16[896,256]{1,0:T(8,128)(2,1)S(1)} %copy.52), channel_id=1, source_target_pairs={{14,0},{0,2},{2,4},{4,6},{6,8},{8,10},{10,12},{12,14},{15,1},{1,3}... | collective-permute-start | bytes 1376264 | tf_op jit(solution)/shard_map/while/body/eval_jaxpr/ppermute | solution.py:10
  52.9 15.3 %collective-permute-start.1 = (bf16[896,256]{1,0:T(8,128)(2,1)S(1)}, bf16[896,256]{1,0:T(8,128)(2,1)}, u32[]{:S(2)}, u32[]{:S(2)}) collective-permute-start(bf16[896,256]{1,0:T(8,128)(2,1)S(1)} %copy.52), channel_id=1, source_target_pairs={{14,0},{0,2},{2,4},{4,6},{6,8},{8,10},{10,12},{12,14},{15,1},{1,3}... | collective-permute-start | bytes 1376264 | tf_op jit(solution)/shard_map/while/body/eval_jaxpr/ppermute | solution.py:10
  69.2 14.5 %collective-permute-start.1 = (bf16[896,256]{1,0:T(8,128)(2,1)S(1)}, bf16[896,256]{1,0:T(8,128)(2,1)}, u32[]{:S(2)}, u32[]{:S(2)}) collective-permute-start(bf16[896,256]{1,0:T(8,128)(2,1)S(1)} %copy.52), channel_id=1, source_target_pairs={{14,0},{0,2},{2,4},{4,6},{6,8},{8,10},{10,12},{12,14},{15,1},{1,3}... | collective-permute-start | bytes 1376264 | tf_op jit(solution)/shard_map/while/body/eval_jaxpr/ppermute | solution.py:10
  85.4 4.7 %copy-start.5 = (s32[896]{0:T(1024)S(1)}, s32[896]{0:T(1024)}, u32[]{:S(2)}) copy-start(s32[896]{0:T(1024)} %param.18) | copy-start | bytes 10756
  86.5 220.1 %reduce-scatter.2.cloned.1.call-start = ((), (), s32[]{:S(2)}) async-start(), calls=%async_computation.2 | async-start | bytes 1376256 | tf_op jit(solution)/shard_map/reduce_scatter | solution.py:100
  100.1 4.0 copy-start.2
  123.9 11.2 %copy-start.3 = (f32[448,512]{1,0:T(8,128)S(1)}, f32[448,512]{1,0:T(8,128)}, u32[]{:S(2)}) copy-start(f32[448,512]{1,0:T(8,128)} %ragged-dot-none.1) | copy-start | bytes 2752516
  158.9 25.1 %collective-permute-start = (f32[896,256]{1,0:T(8,128)S(1)}, f32[896,256]{1,0:T(8,128)S(1)}, u32[]{:S(2)}, u32[]{:S(2)}) collective-permute-start(f32[896,256]{1,0:T(8,128)S(1)} %multiply_add_fusion.2), channel_id=1, source_target_pairs={{14,0},{0,2},{2,4},{4,6},{6,8},{8,10},{10,12},{12,14},{15,1},{1,3}... | collective-permute-start | bytes 2752520 | tf_op jit(solution)/shard_map/while/body/eval_jaxpr/ppermute | solution.py:10
  184.9 24.3 %collective-permute-start = (f32[896,256]{1,0:T(8,128)S(1)}, f32[896,256]{1,0:T(8,128)S(1)}, u32[]{:S(2)}, u32[]{:S(2)}) collective-permute-start(f32[896,256]{1,0:T(8,128)S(1)} %multiply_add_fusion.2), channel_id=1, source_target_pairs={{14,0},{0,2},{2,4},{4,6},{6,8},{8,10},{10,12},{12,14},{15,1},{1,3}... | collective-permute-start | bytes 2752520 | tf_op jit(solution)/shard_map/while/body/eval_jaxpr/ppermute | solution.py:10
  210.0 23.4 %collective-permute-start = (f32[896,256]{1,0:T(8,128)S(1)}, f32[896,256]{1,0:T(8,128)S(1)}, u32[]{:S(2)}, u32[]{:S(2)}) collective-permute-start(f32[896,256]{1,0:T(8,128)S(1)} %multiply_add_fusion.2), channel_id=1, source_target_pairs={{14,0},{0,2},{2,4},{4,6},{6,8},{8,10},{10,12},{12,14},{15,1},{1,3}... | collective-permute-start | bytes 2752520 | tf_op jit(solution)/shard_map/while/body/eval_jaxpr/ppermute | solution.py:10
  234.1 25.6 %collective-permute-start = (f32[896,256]{1,0:T(8,128)S(1)}, f32[896,256]{1,0:T(8,128)S(1)}, u32[]{:S(2)}, u32[]{:S(2)}) collective-permute-start(f32[896,256]{1,0:T(8,128)S(1)} %multiply_add_fusion.2), channel_id=1, source_target_pairs={{14,0},{0,2},{2,4},{4,6},{6,8},{8,10},{10,12},{12,14},{15,1},{1,3}... | collective-permute-start | bytes 2752520 | tf_op jit(solution)/shard_map/while/body/eval_jaxpr/ppermute | solution.py:10
  259.7 31.2 %collective-permute-start.3 = (f32[896,256]{1,0:T(8,128)S(1)}, f32[896,256]{1,0:T(8,128)S(1)}, u32[]{:S(2)}, u32[]{:S(2)}) collective-permute-start(f32[896,256]{1,0:T(8,128)S(1)} %get-tuple-element.263), channel_id=1, source_target_pairs={{8,0},{10,2},{12,4},{14,6},{0,8},{2,10},{4,12},{6,14},{9,1},{11,3}... | collective-permute-start | bytes 2752520 | tf_op jit(solution)/shard_map/ppermute | solution.py:10
  291.9 108.5 %all-reduce.5.cloned.1.call-start = ((), (), s32[]{:S(2)}) async-start(), calls=%async_computation.3 | async-start | bytes 524288 | tf_op jit(solution)/shard_map/psum | solution.py:110
  292.0 13.9 %copy-start.4 = (bf16[896,256]{1,0:T(8,128)(2,1)S(1)}, bf16[896,256]{1,0:T(8,128)(2,1)}, u32[]{:S(2)}) copy-start(bf16[896,256]{1,0:T(8,128)(2,1)} %param.13) | copy-start | bytes 1376260
Sparse Core Ops, SparseCore 0:
  86.6 16.7 all-reduce.2
  292.1 11.3 reduce-scatter.1
  308.8 91.5 all-reduce.4
where the time goes:
time: 411 us; the launch traced here: 409 us
  waiting for transfers between devices  278 us (68%)
  Pallas kernels  46.3 us (11%)
  local copies, waits for them, and re-layouts  24.4 us (6%)
  other arithmetic  18 us (4%)
  between operations  15.2 us (4%)
  matrix products  10.5 us (3%)
  starting transfers between devices  6.04 us (1%)
  blocking collectives  5.72 us (1%)
  loops' own time  4.71 us (1%)
    ppermute x9, waiting for transfers between devices, from_behind(): return lax.ppermute(block, axis, route)  188 us
    psum x1, waiting for transfers between devices, per_device(): msg_weight_grad = lax.psum(weight_term, ('grid', 'rep'))  89.8 us
    another operation x4, Pallas kernels  44.8 us
    unnamed x15, local copies, waits for them, and re-layouts  10.5 us
  transfers between devices with their start and end apart: 12, of which 10 were waited for; matrix products, arithmetic and copies ran while one was open for 6% of the time, Pallas kernels for 6%

commit v1 on v0

v1 whole, which is shorter than its diff:
```python
import functools

import jax
import jax.numpy as jnp
from jax import lax
from jax.experimental import pallas as pl
from jax.experimental.pallas import tpu as pltpu
from jax.sharding import PartitionSpec as P

BF16 = jnp.bfloat16
F32 = jnp.float32
NT = (((1,), (1,)), ((), ()))
TN = (((0,), (0,)), ((), ()))
VMEM_LIMIT = 30 * 1024 * 1024


def ring_order(size):
    if size <= 8:
        return list(range(0, size, 2)) + list(range(1, size, 2))[::-1]
    return list(range(size))


def along_ring(block, order, hop):
    size = len(order)
    route = [(order[place], order[(place + hop) % size]) for place in range(size)]
    return lax.ppermute(block, "grid", route)


def other_core(block):
    return lax.ppermute(block, "rep", [(0, 1), (1, 0)])


def call(kernel, out_shape, smem, vmem, scratch=(), flops=0):
    return pl.pallas_call(
        kernel,
        out_shape=out_shape,
        in_specs=[pl.BlockSpec(memory_space=pltpu.SMEM)] * len(smem)
        + [pl.BlockSpec(memory_space=pltpu.VMEM)] * len(vmem),
        out_specs=jax.tree.map(lambda _: pl.BlockSpec(memory_space=pltpu.VMEM), out_shape),
        scratch_shapes=list(scratch),
        compiler_params=pltpu.CompilerParams(vmem_limit_bytes=VMEM_LIMIT),
        cost_estimate=pl.CostEstimate(flops=flops, bytes_accessed=1 << 20, transcendentals=0),
    )(*smem, *vmem)


def struct(shape, dtype):
    return jax.ShapeDtypeStruct(shape, dtype)


def pick_kernel(offsets, slots, parts, *refs):
    weight = refs[parts]
    rows_out, message_out = refs[parts + 1], refs[parts + 2]
    part_offsets, part_rows = offsets
    chosen = refs[0]
    blocks = refs[1:parts]
    for slot in range(slots):
        for block, offset, start in zip(blocks, part_offsets, part_rows, strict=True):

            @pl.when(chosen[slot] == offset)
            def _(slot=slot, block=block, start=start):
                rows_out[slot, pl.ds(start, block.shape[0]), :] = block[...]

        message_out[slot] = jnp.dot(
            rows_out[slot], weight[...], preferred_element_type=F32
        ).astype(BF16)


def hidden_grad_kernel(mask, out_grad, down, grad_hidden):
    experts = down.shape[0]
    total = lax.dot_general(out_grad[...] * mask[0], down[0], NT, preferred_element_type=F32)
    for expert in range(1, experts):
        total += lax.dot_general(
            out_grad[...] * mask[expert], down[expert], NT, preferred_element_type=F32
        )
    grad_hidden[...] = total


def middle_kernel(
    place,
    counts,
    own_rows,
    other_rows,
    own_message,
    other_message,
    mask,
    up,
    grad_hidden,
    hidden,
    grad_scaled,
    message,
    wide,
):
    slots = own_rows.shape[0]
    experts, width, inner = up.shape
    half = own_message.shape[1]
    core = place[0]
    own_start = pl.multiple_of(core * half, half)
    other_start = pl.multiple_of((1 - core) * half, half)
    for slot in range(2 * slots):
        message[slot, pl.ds(own_start, half), :] = own_message[slot]
        message[slot, pl.ds(other_start, half), :] = other_message[slot]
    total = jnp.zeros((half, width), F32)
    edges = jnp.float32(0.0)
    for slot in range(slots):
        for tile_rows, which in ((own_rows, core), (other_rows, 1 - core)):
            index = which * slots + slot
            count = counts[index].astype(F32)
            edges = edges + count
            total += count * jnp.dot(tile_rows[slot], message[index], preferred_element_type=F32)
    aggregate = total / jnp.full((1, 1), edges, F32)
    inv_rms = lax.rsqrt(jnp.mean(aggregate * aggregate, axis=-1, keepdims=True) + 1e-06)
    normed = aggregate * inv_rms
    normed_bf = normed.astype(BF16)
    for expert in range(experts):
        wide[:, expert * width : (expert + 1) * width] = normed_bf * mask[expert]
    up_act = jnp.dot(
        wide[...], up[...].reshape(experts * width, inner), preferred_element_type=F32
    )
    gate = 1.0 / (1.0 + jnp.exp(-up_act))
    hidden[...] = (up_act * gate).astype(BF16)
    grad_act = (grad_hidden[...] * gate * (1.0 + up_act * (1.0 - gate))).astype(BF16)
    grad_pre = jnp.zeros((half, width), F32)
    for expert in range(experts):
        masked = jnp.concatenate(
            [
                grad_act[:, start : start + width] * mask[expert]
                for start in range(0, inner, width)
            ],
            axis=1,
        )
        grad_pre += lax.dot_general(masked, up[expert], NT, preferred_element_type=F32)
    grad_agg = inv_rms * (
        grad_pre - normed * jnp.mean(grad_pre * normed, axis=-1, keepdims=True)
    )
    grad_scaled[...] = (grad_agg / jnp.full((1, 1), edges, F32)).astype(BF16)


def spread_kernel(
    offsets, place, counts, chosen, own_columns, other_columns, own_grad, other_grad, *refs
):
    terms, grads, full_grad = refs[:-2], refs[-2], refs[-1]
    slots, half, _ = own_columns.shape
    core = place[0]
    full_grad[pl.ds(pl.multiple_of(core * half, half), half), :] = own_grad[...]
    full_grad[pl.ds(pl.multiple_of((1 - core) * half, half), half), :] = other_grad[...]
    products, distances = [], []
    for columns, which in ((own_columns, core), (other_columns, 1 - core)):
        for slot in range(slots):
            index = which * slots + slot
            product = counts[index].astype(F32) * jnp.dot(
                columns[slot], full_grad[...], preferred_element_type=F32
            )
            grads[index] = product.astype(BF16)
            products.append(product)
            distances.append(chosen[index])
    for term, (offset, start) in zip(terms, offsets, strict=True):
        length = term.shape[0]
        total = None
        for product, distance in zip(products, distances, strict=True):
            piece = jnp.where(distance == offset, product[start : start + length], 0.0)
            total = piece if total is None else total + piece
        term[...] = total.astype(term.dtype)


def weight_kernel(rows, grads, total):
    slots = rows.shape[0]
    total[...] = sum(
        lax.dot_general(rows[slot], grads[slot], TN, preferred_element_type=F32)
        for slot in range(slots)
    )


def update_kernel(mask, hidden, down, feats, updated):
    experts, inner, width = down.shape
    total = feats[...].astype(F32)
    for expert in range(experts):
        masked = jnp.concatenate(
            [
                hidden[:, start : start + width] * mask[expert]
                for start in range(0, inner, width)
            ],
            axis=1,
        )
        total += jnp.dot(masked, down[expert], preferred_element_type=F32)
    updated[...] = total.astype(BF16)


def finish_kernel(own, up_first, up_second, down_first, down_second, weight, out_grad, result):
    cut = up_first.shape[0]
    for start, pair in ((0, (up_first, down_first)), (cut, (up_second, down_second))):
        length = pair[0].shape[0]
        grad_msg = (
            own[start : start + length] + pair[0][...].astype(F32) + pair[1][...].astype(F32)
        ).astype(BF16)
        back = lax.dot_general(grad_msg, weight[...], NT, preferred_element_type=F32)
        result[start : start + length] = (
            out_grad[start : start + length].astype(F32) + back
        ).astype(BF16)


def sum_over_all(term, size, core):
    half = term.shape[0] // 2
    kept = lax.dynamic_slice_in_dim(term, core * half, half, 0)
    total = kept + other_core(lax.dynamic_slice_in_dim(term, (1 - core) * half, half, 0))
    step = 1
    while step < size:
        total = total + lax.ppermute(total, "grid", [(i, i ^ step) for i in range(size)])
        step *= 2
    received = other_core(total)
    first = jnp.where(core == 0, total, received)
    second = jnp.where(core == 0, received, total)
    return jnp.concatenate([first, second], axis=0)


def per_device(
    feats, msg_weight, tiles, tile_step, tile_count, node_type, expert_up, expert_down, out_grad
):
    size = lax.axis_size("grid")
    core = lax.axis_index("rep")
    chip = lax.axis_index("grid")
    order = ring_order(size)
    far = size // 2
    slots = tiles.shape[2]
    block, width = feats.shape
    half = block // 2
    cut = half // 2
    experts, _, inner = expert_up.shape

    first = lax.dynamic_slice_in_dim(feats, core * half, cut, 0)
    second = lax.dynamic_slice_in_dim(feats, core * half + cut, half - cut, 0)
    arrived = [(0, 0, first), (0, cut, second)]
    up_a = down_a = first
    up_b = down_b = second
    for step in range(1, far):
        up_a = along_ring(up_a, order, 1)
        down_b = along_ring(down_b, order, -1)
        up_b = along_ring(up_b, order, 1)
        down_a = along_ring(down_a, order, -1)
        arrived += [(size - step, 0, up_a), (size - step, cut, up_b)]
        arrived += [(step, 0, down_a), (step, cut, down_b)]
    arrived += [(far, 0, along_ring(up_a, order, 1)), (far, cut, along_ring(down_b, order, -1))]

    tile_own = tiles[0, 0]
    table_own = jnp.stack([tile_step[0, 0], tile_count[0, 0]])
    table_other = other_core(table_own)
    tile_other = other_core(tile_own)
    table = jnp.where(
        core == 0, jnp.stack([table_own, table_other]), jnp.stack([table_other, table_own])
    )
    counts = table[:, 1].reshape(2 * slots)
    half_loop = jnp.arange(2, dtype=jnp.int32)[:, None] * far
    source = jnp.mod(chip - half_loop - table[:, 0], size)
    ring_place = jnp.array([order.index(i) for i in range(size)], jnp.int32)
    distance = jnp.mod(ring_place[source] - ring_place[chip], size).reshape(2 * slots)
    place = core.astype(jnp.int32).reshape(1)

    def rows_of(tile):
        return lax.dynamic_slice_in_dim(tile, core * half, half, 1)

    def columns_of(tile):
        return lax.dynamic_slice_in_dim(jnp.swapaxes(tile, 1, 2), core * half, half, 1)

    types = lax.dynamic_slice_in_dim(node_type, core * half, half, 0)
    mask = (types[None, :] == jnp.arange(experts, dtype=jnp.int32)[:, None]).astype(BF16)
    mask = jnp.broadcast_to(mask[:, :, None], (experts, half, width))
    grad_hidden = call(
        hidden_grad_kernel, struct((half, inner), F32), (), (mask, out_grad, expert_down)
    )

    pieces = [piece for _, _, piece in arrived]
    offsets = ([offset for offset, _, _ in arrived], [start for _, start, _ in arrived])
    source_rows, own_message = call(
        functools.partial(pick_kernel, offsets, 2 * slots, len(pieces) + 1),
        [struct((2 * slots, half, width), BF16)] * 2,
        (distance,),
        (*pieces, msg_weight),
    )
    other_message = other_core(own_message)

    hidden, grad_scaled = call(
        middle_kernel,
        [struct((half, inner), BF16), struct((half, width), BF16)],
        (place, counts),
        (
            rows_of(tile_own),
            rows_of(tile_other),
            own_message,
            other_message,
            mask,
            expert_up,
            grad_hidden,
        ),
        (
            pltpu.VMEM((2 * slots, block, width), BF16),
            pltpu.VMEM((half, experts * width), BF16),
        ),
    )
    other_grad = other_core(grad_scaled)

    keys = [(0, 0), (far, 0), (far, cut)]
    shapes = [struct((half, width), F32), struct((cut, width), BF16)]
    shapes += [struct((half - cut, width), BF16)]
    for step in range(1, far):
        for offset in (step, size - step):
            keys += [(offset, 0), (offset, cut)]
            shapes += [struct((cut, width), BF16), struct((half - cut, width), BF16)]
    *terms, grads = call(
        functools.partial(spread_kernel, keys),
        [*shapes, struct((2 * slots, half, width), BF16)],
        (place, counts, distance),
        (columns_of(tile_own), columns_of(tile_other), grad_scaled, other_grad),
        (pltpu.VMEM((block, width), BF16),),
    )
    terms = dict(zip(keys, terms, strict=True))

    def joined(received, term):
        return (received.astype(F32) + term.astype(F32)).astype(BF16)

    up_a = along_ring(terms[far, 0], order, 1)
    down_b = along_ring(terms[far, cut], order, -1)
    up_b = down_a = None
    for step in range(far - 1, 0, -1):
        up_a = along_ring(joined(up_a, terms[step, 0]), order, 1)
        down_b = along_ring(joined(down_b, terms[size - step, cut]), order, -1)
        ready_b, ready_a = terms[step, cut], terms[size - step, 0]
        up_b = along_ring(ready_b if up_b is None else joined(up_b, ready_b), order, 1)
        down_a = along_ring(ready_a if down_a is None else joined(down_a, ready_a), order, -1)

    weight_term = call(
        weight_kernel, struct((width, width), F32), (), (source_rows, grads)
    )
    msg_weight_grad = sum_over_all(weight_term, size, core)

    own_feats = jnp.concatenate([first, second], axis=0)
    updated = call(
        update_kernel,
        struct((half, width), BF16),
        (),
        (mask, hidden, expert_down, own_feats),
    )
    feats_grad = call(
        finish_kernel,
        struct((half, width), BF16),
        (),
        (terms[0, 0], up_a, up_b, down_a, down_b, msg_weight, out_grad),
    )
    return (updated, feats_grad, msg_weight_grad)


def solution(mesh):
    return jax.shard_map(
        per_device,
        mesh=mesh,
        in_specs=(
            P(("groups", "grid"), None),
            P(),
            P(("groups", "grid"), "rep", None, None, None),
            P(("groups", "grid"), "rep", None),
            P(("groups", "grid"), "rep", None),
            P(("groups", "grid")),
            P(),
            P(),
            P(("groups", "grid", "rep"), None),
        ),
        out_specs=(
            P(("groups", "grid", "rep"), None),
            P(("groups", "grid", "rep"), None),
            P("groups", None),
        ),
        check_vma=False,
    )
```

time: 411 us -> 97.2 us (0.24)
  waiting for transfers between devices: 278 us -> 22.1 us
  Pallas kernels: 46.3 us -> 14.8 us
  starting transfers between devices: 6.04 us -> 35.5 us
  other arithmetic: 18 us -> 2.79 us
  between operations: 15.2 us -> 2.4 us
  matrix products: 10.5 us -> 0 us
  blocking collectives: 5.72 us -> 0 us
  local copies, waits for them, and re-layouts: 24.4 us -> 19.2 us
  loops' own time: 4.71 us -> 0 us
    ppermute x9 -> x37, waiting for transfers between devices: 188 us -> 22.1 us  [the longest x28 12.6 us: along_ring(): return lax.ppermute(block, 'grid', route)]
    psum x2 -> x0, waiting for transfers between devices: 89.8 us -> none  [the longest x1 89.8 us: per_device(): msg_weight_grad = lax.psum(weight_term, ('grid', 'rep'))]
    another operation x4 -> x0, Pallas kernels: 44.8 us -> none
    ppermute x9 -> x37, starting transfers between devices: 5.92 us -> 35.5 us  [the longest x28 32.8 us: along_ring(): return lax.ppermute(block, 'grid', route)]
    pallas_call x0 -> x7, Pallas kernels: none -> 14.8 us  [call(): pl.pallas_call(kernel, out_shape=out_shape, in_specs=[pl.BlockSpec(memory...]
    dot_general x8 -> x0, matrix products: 10.5 us -> none  [the longest x4 4.56 us: forward_term(): return jnp.dot(tile_now, holding, preferred_element_type=jnp.float32)]
    dynamic_slice x1 -> x8, local copies, waits for them, and re-layouts: 0.07 us -> 6.86 us  [the longest x3 4.82 us: rows_of(): return lax.dynamic_slice_in_dim(tile, core * half, half, 1)]
    convert_element_type x4 -> x11, other arithmetic: 6.68 us -> 0.3 us  [the longest x10 0.3 us: joined(): return (received.astype(F32) + term.astype(F32)).astype(BF16)]
  transfers between devices with their start and end apart: 12 -> 37, of which waited for: 10 -> 14; matrix products, arithmetic and copies ran while one was open for 6% -> 14% of each run, Pallas kernels for 6% -> 7%
where the time goes in v1:
time: 97.2 us; the launch traced here: 96.7 us
  starting transfers between devices  35.5 us (37%)
  waiting for transfers between devices  22.1 us (23%)
  local copies, waits for them, and re-layouts  19.2 us (20%)
  Pallas kernels  14.8 us (15%)
  other arithmetic  2.79 us (3%)
  between operations  2.4 us (2%)
    ppermute x28, starting transfers between devices, along_ring(): return lax.ppermute(block, 'grid', route)  32.8 us
    pallas_call x7, Pallas kernels, call(): pl.pallas_call(kernel, out_shape=out_shape, in_specs=[pl.BlockSpec(memory...  14.8 us
    ppermute x28, waiting for transfers between devices, along_ring(): return lax.ppermute(block, 'grid', route)  12.6 us
    ppermute x3, waiting for transfers between devices, sum_over_all(): lax.ppermute(total, 'grid', [(i, i ^ step) for i in range(size)])  8.35 us
    unnamed x51, local copies, waits for them, and re-layouts  8.12 us
    dynamic_slice x3, local copies, waits for them, and re-layouts, rows_of(): return lax.dynamic_slice_in_dim(tile, core * half, half, 1)  4.82 us
    another operation x2, local copies, waits for them, and re-layouts  3.04 us
  transfers between devices with their start and end apart: 37, of which 14 were waited for; matrix products, arithmetic and copies ran while one was open for 14% of the time, Pallas kernels for 7%

profile of v1, /device:TPU:0, one launch (start us, length us, event | category | flops | bytes accessed | tf_op | source)
XLA Modules:
  0.0 96.7 jit_solution(4345359285927625465)
XLA Ops:
  0.7 3.7 %copy.16 = bf16[1,1,1,896,896]{3,4,2,1,0:T(8,128)(2,1)} copy(bf16[1,1,1,896,896]{4,3,2,1,0:T(8,128)(2,1)} %param.12) | data formatting | bytes 3211264 | tf_op args[2]
  4.3 0.5 collective-permute-start.1
  4.8 2.6 %collective-permute-start.2 = (bf16[224,256]{1,0:T(8,128)(2,1)S(1)}, bf16[224,256]{1,0:T(8,128)(2,1)S(1)}, u32[]{:S(2)}, u32[]{:S(2)}) collective-permute-start(bf16[224,256]{1,0:T(8,128)(2,1)S(1)} %get-tuple-element.46.refs_1_), channel_id=1, source_target_pairs={{0,4},{4,8},{8,12},{12,14},{14,10},{10,6},{6,2},{2,0},{1,5},{5,9},... | collective-permute-start | bytes 344072 | tf_op jit(solution)/shard_map/ppermute | solution.py:26
  7.5 2.0 %collective-permute-start.3 = (bf16[224,256]{1,0:T(8,128)(2,1)S(1)}, bf16[224,256]{1,0:T(8,128)(2,1)S(1)}, u32[]{:S(2)}, u32[]{:S(2)}) collective-permute-start(bf16[224,256]{1,0:T(8,128)(2,1)S(1)} %get-tuple-element.45.refs_2_), channel_id=1, source_target_pairs={{0,4},{4,8},{8,12},{12,14},{14,10},{10,6},{6,2},{2,0},{1,5},{5,9},... | collective-permute-start | bytes 344072 | tf_op jit(solution)/shard_map/ppermute | solution.py:26
  10.9 1.1 %collective-permute-done = s32[2,1]{1,0:T(2,128)S(1)} collective-permute-done((s32[2,1]{1,0:T(2,128)S(1)}, s32[2,1]{1,0:T(2,128)S(1)}, u32[]{:S(2)}, u32[]{:S(2)}) %collective-permute-start) | collective-permute-done | bytes 40 | tf_op jit(solution)/shard_map/ppermute | solution.py:30
  12.0 2.0 %collective-permute-start.6 = (bf16[224,256]{1,0:T(8,128)(2,1)S(1)}, bf16[224,256]{1,0:T(8,128)(2,1)S(1)}, u32[]{:S(2)}, u32[]{:S(2)}) collective-permute-start(bf16[224,256]{1,0:T(8,128)(2,1)S(1)} %collective-permute-done.2.refs_3_), channel_id=1, source_target_pairs={{0,4},{4,8},{8,12},{12,14},{14,10},{10,6},{6,2},{2,0},{1,5},{5,9},... | collective-permute-start | bytes 344072 | tf_op jit(solution)/shard_map/ppermute | solution.py:26
  14.1 0.7 dynamic_slice.36
  14.8 0.1 fusion.4
  14.9 0.1 reduce.1
  15.0 2.1 %collective-permute-start.7 = (bf16[224,256]{1,0:T(8,128)(2,1)S(1)}, bf16[224,256]{1,0:T(8,128)(2,1)S(1)}, u32[]{:S(2)}, u32[]{:S(2)}) collective-permute-start(bf16[224,256]{1,0:T(8,128)(2,1)S(1)} %collective-permute-done.3.refs_4_), channel_id=1, source_target_pairs={{0,4},{4,8},{8,12},{12,14},{14,10},{10,6},{6,2},{2,0},{1,5},{5,9},... | collective-permute-start | bytes 344072 | tf_op jit(solution)/shard_map/ppermute | solution.py:26
  17.1 0.9 collective-permute-done.4.refs_5_
  18.0 2.0 %collective-permute-start.10 = (bf16[224,256]{1,0:T(8,128)(2,1)S(1)}, bf16[224,256]{1,0:T(8,128)(2,1)S(1)}, u32[]{:S(2)}, u32[]{:S(2)}) collective-permute-start(bf16[224,256]{1,0:T(8,128)(2,1)S(1)} %collective-permute-done.6.refs_7_), channel_id=1, source_target_pairs={{0,4},{4,8},{8,12},{12,14},{14,10},{10,6},{6,2},{2,0},{1,5},{5,9},... | collective-permute-start | bytes 344072 | tf_op jit(solution)/shard_map/ppermute | solution.py:26
  20.0 0.1 collective-permute-done.9.refs_10_
  20.1 0.7 fusion.2
  20.9 0.6 gather_fusion
  21.5 2.0 %collective-permute-start.11 = (bf16[224,256]{1,0:T(8,128)(2,1)S(1)}, bf16[224,256]{1,0:T(8,128)(2,1)S(1)}, u32[]{:S(2)}, u32[]{:S(2)}) collective-permute-start(bf16[224,256]{1,0:T(8,128)(2,1)S(1)} %collective-permute-done.7.refs_8_), channel_id=1, source_target_pairs={{0,4},{4,8},{8,12},{12,14},{14,10},{10,6},{6,2},{2,0},{1,5},{5,9},... | collective-permute-start | bytes 344072 | tf_op jit(solution)/shard_map/ppermute | solution.py:26
  23.5 0.4 collective-permute-done.8.refs_9_
  23.9 2.0 %collective-permute-start.14 = (bf16[224,256]{1,0:T(8,128)(2,1)S(1)}, bf16[224,256]{1,0:T(8,128)(2,1)S(1)}, u32[]{:S(2)}, u32[]{:S(2)}) collective-permute-start(bf16[224,256]{1,0:T(8,128)(2,1)S(1)} %collective-permute-done.10.refs_11_), channel_id=1, source_target_pairs={{0,4},{4,8},{8,12},{12,14},{14,10},{10,6},{6,2},{2,0},{1,5},{5,9},... | collective-permute-start | bytes 344072 | tf_op jit(solution)/shard_map/ppermute | solution.py:26
  25.9 0.7 and_select_fusion.1.refs_0_.chosen
  26.7 0.6 collective-permute-done.11.refs_12_
  27.3 2.0 %collective-permute-done.12.refs_13_ = bf16[224,256]{1,0:T(8,128)(2,1)S(1)} collective-permute-done((bf16[224,256]{1,0:T(8,128)(2,1)S(1)}, bf16[224,256]{1,0:T(8,128)(2,1)S(1)}, u32[]{:S(2)}, u32[]{:S(2)}) %collective-permute-start.12) | collective-permute-done | bytes 114720 | tf_op jit(solution)/shard_map/ppermute | solution.py:26
  29.3 1.4 %collective-permute-done.15.refs_16_ = bf16[224,256]{1,0:T(8,128)(2,1)S(1)} collective-permute-done((bf16[224,256]{1,0:T(8,128)(2,1)S(1)}, bf16[224,256]{1,0:T(8,128)(2,1)S(1)}, u32[]{:S(2)}, u32[]{:S(2)}) %collective-permute-start.15) | collective-permute-done | bytes 114720 | tf_op jit(solution)/shard_map/ppermute | solution.py:26
  30.7 2.1 %shard_map.121 = (bf16[2,448,256]{2,1,0:T(8,128)(2,1)S(1)}, bf16[2,448,256]{2,1,0:T(8,128)(2,1)}) custom-call(s32[2]{0:T(128)S(1)} %and_select_fusion.1.refs_0_.chosen, bf16[224,256]{1,0:T(8,128)(2,1)S(1)} %get-tuple-element.46.refs_1_, bf16[224,256]{1,0:T(8,128)(2,1)S(1)} %get-tuple-element.45.refs_2_, bf16[224,256]{1,0:T(8,128)(2,1)S(1)} %collective-permute-done.2.refs_3_, ...), custom_call_target="tpu_custom_call" | custom-call | bytes 1048576 | tf_op jit(solution)/shard_map/pallas_call | solution.py:34
  32.9 0.5 broadcast_in_dim.2.mask
  33.5 1.1 %shard_map.122.grad_hidden = f32[448,512]{1,0:T(8,128)S(1)} custom-call(bf16[8,448,256]{2,1,0:T(8,128)(2,1)S(1)} %broadcast_in_dim.2.mask, bf16[448,256]{1,0:T(8,128)(2,1)S(1)} %copy-done.8, bf16[8,512,256]{2,1,0:T(8,128)(2,1)S(1)} %copy-done), custom_call_target="tpu_custom_call" | custom-call | bytes 1048576 | tf_op jit(solution)/shard_map/pallas_call | solution.py:34
  34.6 0.2 copy-done.21
  35.0 2.6 %constant_dynamic-slice_fusion.4 = bf16[1,448,896]{1,2,0:T(8,128)(2,1)} fusion(bf16[1,896,896]{1,2,0:T(8,128)(2,1)} %collective-permute-done.1, s32[]{:T(128)S(6)} %select_n.71), kind=kLoop, calls=%fused_computation.31 | loop fusion | bytes 1605636 | tf_op jit(solution)/shard_map/dynamic_slice | solution.py:258
  37.5 2.2 %copy.17.other_rows = bf16[1,448,896]{2,1,0:T(8,128)(2,1)} copy(bf16[1,448,896]{1,2,0:T(8,128)(2,1)} %constant_dynamic-slice_fusion.4) | data formatting | bytes 1605632 | tf_op jit(solution)/shard_map/dynamic_slice | solution.py:258
  39.7 1.1 %copy-done.2 = bf16[1,448,896]{2,1,0:T(8,128)(2,1)S(1)} copy-done((bf16[1,448,896]{2,1,0:T(8,128)(2,1)S(1)}, bf16[1,448,896]{2,1,0:T(8,128)(2,1)}, u32[]{:S(2)}) %copy-start.2) | copy-done | bytes 802840
  40.9 1.6 %copy-done.3 = bf16[8,256,512]{2,1,0:T(8,128)(2,1)S(1)} copy-done((bf16[8,256,512]{2,1,0:T(8,128)(2,1)S(1)}, bf16[8,256,512]{2,1,0:T(8,128)(2,1)}, u32[]{:S(2)}) %copy-start.3) | copy-done | bytes 2097176
  42.5 0.6 copy-done.16
  43.0 6.4 %shard_map.123 = (bf16[448,512]{1,0:T(8,128)(2,1)S(1)}, bf16[448,256]{1,0:T(8,128)(2,1)}) custom-call(s32[1]{0:T(128)} %bitcast.place, s32[2]{0:T(128)S(1)} %copy-done.16, bf16[1,448,896]{2,1,0:T(8,128)(2,1)S(1)} %dynamic-slice_bitcast_fusion.1.own_rows, bf16[1,448,896]{2,1,0:T(8,128)(2,1)S(1)} %copy-done.2, ...), custom_call_target="tpu_custom_call" | custom-call | bytes 1048576 | tf_op jit(solution)/shard_map/pallas_call | solution.py:34
  49.5 0.8 copy-done.12
  50.3 0.4 collective-permute-start.17
  50.7 1.3 %constant_dynamic-slice_fusion.1 = bf16[1,1,1,896,448]{4,3,2,1,0:T(8,128)(2,1)} fusion(bf16[1,1,1,896,896]{4,3,2,1,0:T(8,128)(2,1)S(1)} %copy-done.22, s32[]{:T(128)S(6)} %select_n.71), kind=kLoop, calls=%fused_computation.28 | loop fusion | bytes 1605636 | tf_op jit(solution)/shard_map/dynamic-slice.3
  52.0 1.7 %copy.18 = bf16[1,1,1,896,448]{3,4,2,1,0:T(8,128)(2,1)S(1)} copy(bf16[1,1,1,896,448]{4,3,2,1,0:T(8,128)(2,1)} %constant_dynamic-slice_fusion.1) | data formatting | bytes 1605632 | tf_op jit(solution)/shard_map/dynamic-slice.3
  53.7 1.3 %dynamic-slice_bitcast_fusion.other_columns = bf16[1,448,896]{2,1,0:T(8,128)(2,1)S(1)} fusion(bf16[1,896,896]{1,2,0:T(8,128)(2,1)} %collective-permute-done.1, s32[]{:T(128)S(6)} %select_n.71), kind=kLoop, calls=%fused_computation.1 | loop fusion | bytes 1605636 | tf_op jit(solution)/shard_map/dynamic_slice | solution.py:261
  55.0 2.0 %shard_map.125 = (f32[448,256]{1,0:T(8,128)S(1)}, bf16[224,256]{1,0:T(8,128)(2,1)S(1)}, bf16[224,256]{1,0:T(8,128)(2,1)S(1)}, bf16[224,256]{1,0:T(8,128)(2,1)S(1...) custom-call(s32[1]{0:T(128)} %bitcast.place, ...), custom_call_target="tpu_custom_call" | custom-call | bytes 1048576 | tf_op jit(solution)/shard_map/pallas_call | solution.py:34
  57.0 0.1 collective-permute-start.28
  57.2 0.3 shard_map.127
  57.5 0.1 collective-permute-start.32
  57.7 1.9 %collective-permute-start.25 = (bf16[224,256]{1,0:T(8,128)(2,1)S(1)}, bf16[224,256]{1,0:T(8,128)(2,1)S(1)}, u32[]{:S(2)}, u32[]{:S(2)}) collective-permute-start(bf16[224,256]{1,0:T(8,128)(2,1)S(1)} %get-tuple-element.34), channel_id=1, source_target_pairs={{0,2},{4,0},{8,4},{12,8},{14,12},{10,14},{6,10},{2,6},{1,3},{5,1},... | collective-permute-start | bytes 344072 | tf_op jit(solution)/shard_map/ppermute | solution.py:26
  59.6 0.1 collective-permute-start.22
  59.7 1.9 %collective-permute-start.18 = (bf16[224,256]{1,0:T(8,128)(2,1)S(1)}, bf16[224,256]{1,0:T(8,128)(2,1)S(1)}, u32[]{:S(2)}, u32[]{:S(2)}) collective-permute-start(bf16[224,256]{1,0:T(8,128)(2,1)S(1)} %get-tuple-element.27), channel_id=1, source_target_pairs={{0,4},{4,8},{8,12},{12,14},{14,10},{10,6},{6,2},{2,0},{1,5},{5,9},... | collective-permute-start | bytes 344072 | tf_op jit(solution)/shard_map/ppermute | solution.py:26
  61.7 1.4 %collective-permute-done.28 = bf16[224,256]{1,0:T(8,128)(2,1)S(1)} collective-permute-done((bf16[224,256]{1,0:T(8,128)(2,1)S(1)}, bf16[224,256]{1,0:T(8,128)(2,1)S(1)}, u32[]{:S(2)}, u32[]{:S(2)}) %collective-permute-start.28) | collective-permute-done | bytes 114720 | tf_op jit(solution)/shard_map/ppermute | solution.py:26
  63.2 2.0 %collective-permute-done.25 = bf16[224,256]{1,0:T(8,128)(2,1)S(1)} collective-permute-done((bf16[224,256]{1,0:T(8,128)(2,1)S(1)}, bf16[224,256]{1,0:T(8,128)(2,1)S(1)}, u32[]{:S(2)}, u32[]{:S(2)}) %collective-permute-start.25) | collective-permute-done | bytes 114720 | tf_op jit(solution)/shard_map/ppermute | solution.py:26
  65.2 0.3 collective-permute-start.26
  65.4 0.1 collective-permute-done.22
  65.6 1.7 %collective-permute-start.23 = (bf16[224,256]{1,0:T(8,128)(2,1)S(1)}, bf16[224,256]{1,0:T(8,128)(2,1)S(1)}, u32[]{:S(2)}, u32[]{:S(2)}) collective-permute-start(bf16[224,256]{1,0:T(8,128)(2,1)S(1)} %add_convert_fusion.6), channel_id=1, source_target_pairs={{0,4},{4,8},{8,12},{12,14},{14,10},{10,6},{6,2},{2,0},{1,5},{5,9},... | collective-permute-start | bytes 344072 | tf_op jit(solution)/shard_map/ppermute | solution.py:26
  67.4 1.6 %collective-permute-start.19 = (bf16[224,256]{1,0:T(8,128)(2,1)S(1)}, bf16[224,256]{1,0:T(8,128)(2,1)S(1)}, u32[]{:S(2)}, u32[]{:S(2)}) collective-permute-start(bf16[224,256]{1,0:T(8,128)(2,1)S(1)} %add_convert_fusion.9), channel_id=1, source_target_pairs={{0,4},{4,8},{8,12},{12,14},{14,10},{10,6},{6,2},{2,0},{1,5},{5,9},... | collective-permute-start | bytes 344072 | tf_op jit(solution)/shard_map/ppermute | solution.py:26
  69.0 0.5 collective-permute-start.33
  69.6 1.6 %collective-permute-start.30 = (bf16[224,256]{1,0:T(8,128)(2,1)S(1)}, bf16[224,256]{1,0:T(8,128)(2,1)S(1)}, u32[]{:S(2)}, u32[]{:S(2)}) collective-permute-start(bf16[224,256]{1,0:T(8,128)(2,1)S(1)} %add_convert_fusion.1), channel_id=1, source_target_pairs={{0,2},{4,0},{8,4},{12,8},{14,12},{10,14},{6,10},{2,6},{1,3},{5,1},... | collective-permute-start | bytes 344072 | tf_op jit(solution)/shard_map/ppermute | solution.py:26
  71.3 1.6 %collective-permute-start.27 = (bf16[224,256]{1,0:T(8,128)(2,1)S(1)}, bf16[224,256]{1,0:T(8,128)(2,1)S(1)}, u32[]{:S(2)}, u32[]{:S(2)}) collective-permute-start(bf16[224,256]{1,0:T(8,128)(2,1)S(1)} %add_convert_fusion.3), channel_id=1, source_target_pairs={{0,2},{4,0},{8,4},{12,8},{14,12},{10,14},{6,10},{2,6},{1,3},{5,1},... | collective-permute-start | bytes 344072 | tf_op jit(solution)/shard_map/ppermute | solution.py:26
  72.9 0.5 collective-permute-start.24
  73.4 3.4 %collective-permute-done.33 = f32[128,256]{1,0:T(8,128)S(1)} collective-permute-done((f32[128,256]{1,0:T(8,128)S(1)}, f32[128,256]{1,0:T(8,128)S(1)}, u32[]{:S(2)}, u32[]{:S(2)}) %collective-permute-start.33) | collective-permute-done | bytes 131104 | tf_op jit(solution)/shard_map/ppermute | solution.py:207
  77.0 2.1 %collective-permute-start.20 = (bf16[224,256]{1,0:T(8,128)(2,1)S(1)}, bf16[224,256]{1,0:T(8,128)(2,1)S(1)}, u32[]{:S(2)}, u32[]{:S(2)}) collective-permute-start(bf16[224,256]{1,0:T(8,128)(2,1)S(1)} %add_convert_fusion.8), channel_id=1, source_target_pairs={{0,4},{4,8},{8,12},{12,14},{14,10},{10,6},{6,2},{2,0},{1,5},{5,9},... | collective-permute-start | bytes 344072 | tf_op jit(solution)/shard_map/ppermute | solution.py:26
  79.1 2.9 %collective-permute-done.34 = f32[128,256]{1,0:T(8,128)S(1)} collective-permute-done((f32[128,256]{1,0:T(8,128)S(1)}, f32[128,256]{1,0:T(8,128)S(1)}, u32[]{:S(2)}, u32[]{:S(2)}) %collective-permute-start.34) | collective-permute-done | bytes 131104 | tf_op jit(solution)/shard_map/ppermute | solution.py:207
  82.0 0.9 collective-permute-start.35
  82.9 4.3 %collective-permute-start.31 = (bf16[224,256]{1,0:T(8,128)(2,1)S(1)}, bf16[224,256]{1,0:T(8,128)(2,1)S(1)}, u32[]{:S(2)}, u32[]{:S(2)}) collective-permute-start(bf16[224,256]{1,0:T(8,128)(2,1)S(1)} %add_convert_fusion), channel_id=1, source_target_pairs={{0,2},{4,0},{8,4},{12,8},{14,12},{10,14},{6,10},{2,6},{1,3},{5,1},... | collective-permute-start | bytes 344072 | tf_op jit(solution)/shard_map/ppermute | solution.py:26
  87.2 2.0 %collective-permute-done.35 = f32[128,256]{1,0:T(8,128)S(1)} collective-permute-done((f32[128,256]{1,0:T(8,128)S(1)}, f32[128,256]{1,0:T(8,128)S(1)}, u32[]{:S(2)}, u32[]{:S(2)}) %collective-permute-start.35) | collective-permute-done | bytes 131104 | tf_op jit(solution)/shard_map/ppermute | solution.py:207
  89.6 1.8 %shard_map.124 = bf16[448,256]{1,0:T(8,128)(2,1)} custom-call(bf16[8,448,256]{2,1,0:T(8,128)(2,1)S(1)} %broadcast_in_dim.2.mask, bf16[448,512]{1,0:T(8,128)(2,1)S(1)} %copy-done.13, bf16[8,512,256]{2,1,0:T(8,128)(2,1)S(1)} %copy-done.1, bf16[448,256]{1,0:T(8,128)(2,1)S(1)} %pad_maximum_fusion.1.feats), custom_call_target="tpu_custom_call" | custom-call | bytes 1048576 | tf_op jit(solution)/shard_map/pallas_call | solution.py:34
  91.4 3.6 %collective-permute-done.21.up_first = bf16[224,256]{1,0:T(8,128)(2,1)S(1)} collective-permute-done((bf16[224,256]{1,0:T(8,128)(2,1)S(1)}, bf16[224,256]{1,0:T(8,128)(2,1)S(1)}, u32[]{:S(2)}, u32[]{:S(2)}) %collective-permute-start.21) | collective-permute-done | bytes 114720 | tf_op jit(solution)/shard_map/ppermute | solution.py:26
  95.0 1.0 shard_map.126
  96.0 0.7 pad_maximum_fusion
  (105 shorter events, 1.1 us)
Async XLA Ops:
  0.6 13.5 %copy-start.20 = (s32[8]{0:T(128)S(1)}, s32[8]{0:T(128)}, u32[]{:S(2)}) copy-start(s32[8]{0:T(128)} %constant.51.clone) | copy-start | bytes 100
  0.6 4.1 %copy-start.23 = (bf16[896,256]{1,0:T(8,128)(2,1)S(1)}, bf16[896,256]{1,0:T(8,128)(2,1)}, u32[]{:S(2)}) copy-start(bf16[896,256]{1,0:T(8,128)(2,1)} %param.10) | copy-start | bytes 1376260
  0.7 13.4 %copy-start.24 = (s32[896]{0:T(1024)S(1)}, s32[896]{0:T(1024)}, u32[]{:S(2)}) copy-start(s32[896]{0:T(1024)} %param.15) | copy-start | bytes 10756
  0.7 30.1 %copy-start.10 = (bf16[256,256]{1,0:T(8,128)(2,1)S(1)}, bf16[256,256]{1,0:T(8,128)(2,1)}, u32[]{:S(2)}) copy-start(bf16[256,256]{1,0:T(8,128)(2,1)} %weight.1) | copy-start | bytes 393220
  4.3 30.6 %collective-permute-start.1 = (bf16[1,896,896]{1,2,0:T(8,128)(2,1)}, bf16[1,896,896]{1,2,0:T(8,128)(2,1)}, u32[]{:S(2)}, u32[]{:S(2)}) collective-permute-start(bf16[1,896,896]{1,2,0:T(8,128)(2,1)} %bitcast.4), channel_id=1, source_target_pairs={{0,1},{1,0},{2,3},{3,2},{4,5},{5,4},{6,7},{7,6},{8,9},{9,8},{10,11... | collective-permute-start | bytes 4816904 | tf_op jit(solution)/shard_map/ppermute | solution.py:30
  4.8 28.0 %copy-start.4 = (bf16[224,256]{1,0:T(8,128)(2,1)}, bf16[224,256]{1,0:T(8,128)(2,1)S(1)}, u32[]{:S(2)}) copy-start(bf16[224,256]{1,0:T(8,128)(2,1)S(1)} %get-tuple-element.45.refs_2_) | copy-start | bytes 344068
  4.8 28.0 %copy-start.6 = (bf16[224,256]{1,0:T(8,128)(2,1)}, bf16[224,256]{1,0:T(8,128)(2,1)S(1)}, u32[]{:S(2)}) copy-start(bf16[224,256]{1,0:T(8,128)(2,1)S(1)} %get-tuple-element.46.refs_1_) | copy-start | bytes 344068
  4.8 7.2 %collective-permute-start.2 = (bf16[224,256]{1,0:T(8,128)(2,1)S(1)}, bf16[224,256]{1,0:T(8,128)(2,1)S(1)}, u32[]{:S(2)}, u32[]{:S(2)}) collective-permute-start(bf16[224,256]{1,0:T(8,128)(2,1)S(1)} %get-tuple-element.46.refs_1_), channel_id=1, source_target_pairs={{0,4},{4,8},{8,12},{12,14},{14,10},{10,6},{6,2},{2,0},{1,5},{5,9},... | collective-permute-start | bytes 344072 | tf_op jit(solution)/shard_map/ppermute | solution.py:26
  7.5 6.6 %collective-permute-start.5 = (bf16[224,256]{1,0:T(8,128)(2,1)S(1)}, bf16[224,256]{1,0:T(8,128)(2,1)S(1)}, u32[]{:S(2)}, u32[]{:S(2)}) collective-permute-start(bf16[224,256]{1,0:T(8,128)(2,1)S(1)} %get-tuple-element.45.refs_2_), channel_id=1, source_target_pairs={{0,2},{4,0},{8,4},{12,8},{14,12},{10,14},{6,10},{2,6},{1,3},{5,1},... | collective-permute-start | bytes 344072 | tf_op jit(solution)/shard_map/ppermute | solution.py:26
  7.5 7.6 %collective-permute-start.3 = (bf16[224,256]{1,0:T(8,128)(2,1)S(1)}, bf16[224,256]{1,0:T(8,128)(2,1)S(1)}, u32[]{:S(2)}, u32[]{:S(2)}) collective-permute-start(bf16[224,256]{1,0:T(8,128)(2,1)S(1)} %get-tuple-element.45.refs_2_), channel_id=1, source_target_pairs={{0,4},{4,8},{8,12},{12,14},{14,10},{10,6},{6,2},{2,0},{1,5},{5,9},... | collective-permute-start | bytes 344072 | tf_op jit(solution)/shard_map/ppermute | solution.py:26
  10.8 1.2 %collective-permute-start = (s32[2,1]{1,0:T(2,128)S(1)}, s32[2,1]{1,0:T(2,128)S(1)}, u32[]{:S(2)}, u32[]{:S(2)}) collective-permute-start(s32[2,1]{1,0:T(2,128)S(1)} %pad_add_fusion), channel_id=1, source_target_pairs={{0,1},{1,0},{2,3},{3,2},{4,5},{5,4},{6,7},{7,6},{8,9},{9,8},{10,11... | collective-permute-start | bytes 32 | tf_op jit(solution)/shard_map/ppermute | solution.py:30
  12.0 6.0 %collective-permute-start.4 = (bf16[224,256]{1,0:T(8,128)(2,1)S(1)}, bf16[224,256]{1,0:T(8,128)(2,1)S(1)}, u32[]{:S(2)}, u32[]{:S(2)}) collective-permute-start(bf16[224,256]{1,0:T(8,128)(2,1)S(1)} %get-tuple-element.46.refs_1_), channel_id=1, source_target_pairs={{0,2},{4,0},{8,4},{12,8},{14,12},{10,14},{6,10},{2,6},{1,3},{5,1},... | collective-permute-start | bytes 344072 | tf_op jit(solution)/shard_map/ppermute | solution.py:26
  12.0 6.0 %collective-permute-start.6 = (bf16[224,256]{1,0:T(8,128)(2,1)S(1)}, bf16[224,256]{1,0:T(8,128)(2,1)S(1)}, u32[]{:S(2)}, u32[]{:S(2)}) collective-permute-start(bf16[224,256]{1,0:T(8,128)(2,1)S(1)} %collective-permute-done.2.refs_3_), channel_id=1, source_target_pairs={{0,4},{4,8},{8,12},{12,14},{14,10},{10,6},{6,2},{2,0},{1,5},{5,9},... | collective-permute-start | bytes 344072 | tf_op jit(solution)/shard_map/ppermute | solution.py:26
  14.0 6.1 %collective-permute-start.9 = (bf16[224,256]{1,0:T(8,128)(2,1)S(1)}, bf16[224,256]{1,0:T(8,128)(2,1)S(1)}, u32[]{:S(2)}, u32[]{:S(2)}) collective-permute-start(bf16[224,256]{1,0:T(8,128)(2,1)S(1)} %collective-permute-done.5.refs_6_), channel_id=1, source_target_pairs={{0,2},{4,0},{8,4},{12,8},{14,12},{10,14},{6,10},{2,6},{1,3},{5,1},... | collective-permute-start | bytes 344072 | tf_op jit(solution)/shard_map/ppermute | solution.py:26
  15.0 6.4 %collective-permute-start.7 = (bf16[224,256]{1,0:T(8,128)(2,1)S(1)}, bf16[224,256]{1,0:T(8,128)(2,1)S(1)}, u32[]{:S(2)}, u32[]{:S(2)}) collective-permute-start(bf16[224,256]{1,0:T(8,128)(2,1)S(1)} %collective-permute-done.3.refs_4_), channel_id=1, source_target_pairs={{0,4},{4,8},{8,12},{12,14},{14,10},{10,6},{6,2},{2,0},{1,5},{5,9},... | collective-permute-start | bytes 344072 | tf_op jit(solution)/shard_map/ppermute | solution.py:26
  18.0 5.9 %collective-permute-start.8 = (bf16[224,256]{1,0:T(8,128)(2,1)S(1)}, bf16[224,256]{1,0:T(8,128)(2,1)S(1)}, u32[]{:S(2)}, u32[]{:S(2)}) collective-permute-start(bf16[224,256]{1,0:T(8,128)(2,1)S(1)} %collective-permute-done.4.refs_5_), channel_id=1, source_target_pairs={{0,2},{4,0},{8,4},{12,8},{14,12},{10,14},{6,10},{2,6},{1,3},{5,1},... | collective-permute-start | bytes 344072 | tf_op jit(solution)/shard_map/ppermute | solution.py:26
  18.0 5.9 %collective-permute-start.10 = (bf16[224,256]{1,0:T(8,128)(2,1)S(1)}, bf16[224,256]{1,0:T(8,128)(2,1)S(1)}, u32[]{:S(2)}, u32[]{:S(2)}) collective-permute-start(bf16[224,256]{1,0:T(8,128)(2,1)S(1)} %collective-permute-done.6.refs_7_), channel_id=1, source_target_pairs={{0,4},{4,8},{8,12},{12,14},{14,10},{10,6},{6,2},{2,0},{1,5},{5,9},... | collective-permute-start | bytes 344072 | tf_op jit(solution)/shard_map/ppermute | solution.py:26
  20.1 5.8 %collective-permute-start.13 = (bf16[224,256]{1,0:T(8,128)(2,1)S(1)}, bf16[224,256]{1,0:T(8,128)(2,1)S(1)}, u32[]{:S(2)}, u32[]{:S(2)}) collective-permute-start(bf16[224,256]{1,0:T(8,128)(2,1)S(1)} %collective-permute-done.9.refs_10_), channel_id=1, source_target_pairs={{0,2},{4,0},{8,4},{12,8},{14,12},{10,14},{6,10},{2,6},{1,3},{5,1},... | collective-permute-start | bytes 344072 | tf_op jit(solution)/shard_map/ppermute | solution.py:26
  21.5 5.8 %collective-permute-start.11 = (bf16[224,256]{1,0:T(8,128)(2,1)S(1)}, bf16[224,256]{1,0:T(8,128)(2,1)S(1)}, u32[]{:S(2)}, u32[]{:S(2)}) collective-permute-start(bf16[224,256]{1,0:T(8,128)(2,1)S(1)} %collective-permute-done.7.refs_8_), channel_id=1, source_target_pairs={{0,4},{4,8},{8,12},{12,14},{14,10},{10,6},{6,2},{2,0},{1,5},{5,9},... | collective-permute-start | bytes 344072 | tf_op jit(solution)/shard_map/ppermute | solution.py:26
  23.9 5.4 %collective-permute-start.12 = (bf16[224,256]{1,0:T(8,128)(2,1)S(1)}, bf16[224,256]{1,0:T(8,128)(2,1)S(1)}, u32[]{:S(2)}, u32[]{:S(2)}) collective-permute-start(bf16[224,256]{1,0:T(8,128)(2,1)S(1)} %collective-permute-done.8.refs_9_), channel_id=1, source_target_pairs={{0,2},{4,0},{8,4},{12,8},{14,12},{10,14},{6,10},{2,6},{1,3},{5,1},... | collective-permute-start | bytes 344072 | tf_op jit(solution)/shard_map/ppermute | solution.py:26
  23.9 5.4 %collective-permute-start.14 = (bf16[224,256]{1,0:T(8,128)(2,1)S(1)}, bf16[224,256]{1,0:T(8,128)(2,1)S(1)}, u32[]{:S(2)}, u32[]{:S(2)}) collective-permute-start(bf16[224,256]{1,0:T(8,128)(2,1)S(1)} %collective-permute-done.10.refs_11_), channel_id=1, source_target_pairs={{0,4},{4,8},{8,12},{12,14},{14,10},{10,6},{6,2},{2,0},{1,5},{5,9},... | collective-permute-start | bytes 344072 | tf_op jit(solution)/shard_map/ppermute | solution.py:26
  25.9 4.8 %collective-permute-start.15 = (bf16[224,256]{1,0:T(8,128)(2,1)S(1)}, bf16[224,256]{1,0:T(8,128)(2,1)S(1)}, u32[]{:S(2)}, u32[]{:S(2)}) collective-permute-start(bf16[224,256]{1,0:T(8,128)(2,1)S(1)} %collective-permute-done.13.refs_14_), channel_id=1, source_target_pairs={{0,2},{4,0},{8,4},{12,8},{14,12},{10,14},{6,10},{2,6},{1,3},{5,1},... | collective-permute-start | bytes 344072 | tf_op jit(solution)/shard_map/ppermute | solution.py:26
  26.6 6.8 %copy-start.18 = (s32[2]{0:T(128)}, s32[2]{0:T(128)S(1)}, u32[]{:S(2)}) copy-start(s32[2]{0:T(128)S(1)} %and_select_fusion.1.refs_0_.chosen) | copy-start | bytes 28
  26.7 6.8 %copy-start = (bf16[8,512,256]{2,1,0:T(8,128)(2,1)S(1)}, bf16[8,512,256]{2,1,0:T(8,128)(2,1)}, u32[]{:S(2)}) copy-start(bf16[8,512,256]{2,1,0:T(8,128)(2,1)} %down.3) | copy-start | bytes 6291460
  26.7 6.8 %copy-start.8 = (bf16[448,256]{1,0:T(8,128)(2,1)S(1)}, bf16[448,256]{1,0:T(8,128)(2,1)}, u32[]{:S(2)}) copy-start(bf16[448,256]{1,0:T(8,128)(2,1)} %out_grad.3) | copy-start | bytes 688132
  32.8 1.8 %copy-start.14 = (bf16[2,448,256]{2,1,0:T(8,128)(2,1)}, bf16[2,448,256]{2,1,0:T(8,128)(2,1)S(1)}, u32[]{:S(2)}) copy-start(bf16[2,448,256]{2,1,0:T(8,128)(2,1)S(1)} %get-tuple-element.41.rows) | copy-start | bytes 1376260
  32.9 6.9 %collective-permute-start.16 = (bf16[2,448,256]{2,1,0:T(8,128)(2,1)}, bf16[2,448,256]{2,1,0:T(8,128)(2,1)}, u32[]{:S(2)}, u32[]{:S(2)}) collective-permute-start(bf16[2,448,256]{2,1,0:T(8,128)(2,1)} %get-tuple-element.23.own_message), channel_id=1, source_target_pairs={{0,1},{1,0},{2,3},{3,2},{4,5},{5,4},{6,7},{7,6},{8,9},{9,8},{10,11... | collective-permute-start | bytes 1376264 | tf_op jit(solution)/shard_map/ppermute | solution.py:30
  33.5 1.4 %copy-start.21 = (bf16[1,1,1,896,896]{4,3,2,1,0:T(8,128)(2,1)S(1)}, bf16[1,1,1,896,896]{4,3,2,1,0:T(8,128)(2,1)}, u32[]{:S(2)}) copy-start(bf16[1,1,1,896,896]{4,3,2,1,0:T(8,128)(2,1)} %param.12) | copy-start | bytes 4816900
  39.7 1.1 %copy-start.2 = (bf16[1,448,896]{2,1,0:T(8,128)(2,1)S(1)}, bf16[1,448,896]{2,1,0:T(8,128)(2,1)}, u32[]{:S(2)}) copy-start(bf16[1,448,896]{2,1,0:T(8,128)(2,1)} %copy.17.other_rows) | copy-start | bytes 2408452
  40.9 1.6 %copy-start.3 = (bf16[8,256,512]{2,1,0:T(8,128)(2,1)S(1)}, bf16[8,256,512]{2,1,0:T(8,128)(2,1)}, u32[]{:S(2)}) copy-start(bf16[8,256,512]{2,1,0:T(8,128)(2,1)} %up.1) | copy-start | bytes 6291460
  42.5 0.6 copy-start.16
  43.0 7.6 %copy-start.22 = (bf16[1,1,1,896,896]{4,3,2,1,0:T(8,128)(2,1)S(1)}, bf16[1,1,1,896,896]{4,3,2,1,0:T(8,128)(2,1)}, u32[]{:S(2)}) copy-start(bf16[1,1,1,896,896]{4,3,2,1,0:T(8,128)(2,1)} %param.12) | copy-start | bytes 4816900
  49.5 0.8 copy-start.12
  50.3 4.8 %collective-permute-start.17 = (bf16[448,256]{1,0:T(8,128)(2,1)}, bf16[448,256]{1,0:T(8,128)(2,1)S(1)}, u32[]{:S(2)}, u32[]{:S(2)}) collective-permute-start(bf16[448,256]{1,0:T(8,128)(2,1)} %get-tuple-element.25.own_grad), channel_id=1, source_target_pairs={{0,1},{1,0},{2,3},{3,2},{4,5},{5,4},{6,7},{7,6},{8,9},{9,8},{10,11... | collective-permute-start | bytes 688136 | tf_op jit(solution)/shard_map/ppermute | solution.py:30
  52.0 3.0 %copy-start.17 = (s32[2]{0:T(128)S(1)}, s32[2]{0:T(128)}, u32[]{:S(2)}) copy-start(s32[2]{0:T(128)} %get-tuple-element.44.counts) | copy-start | bytes 28
  52.0 3.0 %copy-start.19 = (s32[2]{0:T(128)S(1)}, s32[2]{0:T(128)}, u32[]{:S(2)}) copy-start(s32[2]{0:T(128)} %copy-done.18) | copy-start | bytes 28
  53.7 3.4 %copy-start.15 = (bf16[2,448,256]{2,1,0:T(8,128)(2,1)S(1)}, bf16[2,448,256]{2,1,0:T(8,128)(2,1)}, u32[]{:S(2)}) copy-start(bf16[2,448,256]{2,1,0:T(8,128)(2,1)} %copy-done.14) | copy-start | bytes 1376260
  57.0 6.0 %collective-permute-start.28 = (bf16[224,256]{1,0:T(8,128)(2,1)S(1)}, bf16[224,256]{1,0:T(8,128)(2,1)S(1)}, u32[]{:S(2)}, u32[]{:S(2)}) collective-permute-start(bf16[224,256]{1,0:T(8,128)(2,1)S(1)} %get-tuple-element.37), channel_id=1, source_target_pairs={{0,2},{4,0},{8,4},{12,8},{14,12},{10,14},{6,10},{2,6},{1,3},{5,1},... | collective-permute-start | bytes 344072 | tf_op jit(solution)/shard_map/ppermute | solution.py:26
  57.5 11.5 %collective-permute-start.32 = (f32[128,256]{1,0:T(8,128)S(1)}, f32[128,256]{1,0:T(8,128)S(1)}, u32[]{:S(2)}, u32[]{:S(2)}) collective-permute-start(f32[128,256]{1,0:T(8,128)S(1)} %constant_dynamic-slice_fusion), channel_id=1, source_target_pairs={{0,1},{1,0},{2,3},{3,2},{4,5},{5,4},{6,7},{7,6},{8,9},{9,8},{10,11... | collective-permute-start | bytes 393224 | tf_op jit(solution)/shard_map/ppermute | solution.py:30
  57.7 7.5 %collective-permute-start.25 = (bf16[224,256]{1,0:T(8,128)(2,1)S(1)}, bf16[224,256]{1,0:T(8,128)(2,1)S(1)}, u32[]{:S(2)}, u32[]{:S(2)}) collective-permute-start(bf16[224,256]{1,0:T(8,128)(2,1)S(1)} %get-tuple-element.34), channel_id=1, source_target_pairs={{0,2},{4,0},{8,4},{12,8},{14,12},{10,14},{6,10},{2,6},{1,3},{5,1},... | collective-permute-start | bytes 344072 | tf_op jit(solution)/shard_map/ppermute | solution.py:26
  59.6 6.0 %collective-permute-start.22 = (bf16[224,256]{1,0:T(8,128)(2,1)S(1)}, bf16[224,256]{1,0:T(8,128)(2,1)S(1)}, u32[]{:S(2)}, u32[]{:S(2)}) collective-permute-start(bf16[224,256]{1,0:T(8,128)(2,1)S(1)} %get-tuple-element.31), channel_id=1, source_target_pairs={{0,4},{4,8},{8,12},{12,14},{14,10},{10,6},{6,2},{2,0},{1,5},{5,9},... | collective-permute-start | bytes 344072 | tf_op jit(solution)/shard_map/ppermute | solution.py:26
  59.7 7.6 %collective-permute-start.18 = (bf16[224,256]{1,0:T(8,128)(2,1)S(1)}, bf16[224,256]{1,0:T(8,128)(2,1)S(1)}, u32[]{:S(2)}, u32[]{:S(2)}) collective-permute-start(bf16[224,256]{1,0:T(8,128)(2,1)S(1)} %get-tuple-element.27), channel_id=1, source_target_pairs={{0,4},{4,8},{8,12},{12,14},{14,10},{10,6},{6,2},{2,0},{1,5},{5,9},... | collective-permute-start | bytes 344072 | tf_op jit(solution)/shard_map/ppermute | solution.py:26
  63.1 6.4 %collective-permute-start.29 = (bf16[224,256]{1,0:T(8,128)(2,1)S(1)}, bf16[224,256]{1,0:T(8,128)(2,1)S(1)}, u32[]{:S(2)}, u32[]{:S(2)}) collective-permute-start(bf16[224,256]{1,0:T(8,128)(2,1)S(1)} %add_convert_fusion.2), channel_id=1, source_target_pairs={{0,2},{4,0},{8,4},{12,8},{14,12},{10,14},{6,10},{2,6},{1,3},{5,1},... | collective-permute-start | bytes 344072 | tf_op jit(solution)/shard_map/ppermute | solution.py:26
  65.2 6.1 %collective-permute-start.26 = (bf16[224,256]{1,0:T(8,128)(2,1)S(1)}, bf16[224,256]{1,0:T(8,128)(2,1)S(1)}, u32[]{:S(2)}, u32[]{:S(2)}) collective-permute-start(bf16[224,256]{1,0:T(8,128)(2,1)S(1)} %add_convert_fusion.4), channel_id=1, source_target_pairs={{0,2},{4,0},{8,4},{12,8},{14,12},{10,14},{6,10},{2,6},{1,3},{5,1},... | collective-permute-start | bytes 344072 | tf_op jit(solution)/shard_map/ppermute | solution.py:26
  65.6 7.3 %collective-permute-start.23 = (bf16[224,256]{1,0:T(8,128)(2,1)S(1)}, bf16[224,256]{1,0:T(8,128)(2,1)S(1)}, u32[]{:S(2)}, u32[]{:S(2)}) collective-permute-start(bf16[224,256]{1,0:T(8,128)(2,1)S(1)} %add_convert_fusion.6), channel_id=1, source_target_pairs={{0,4},{4,8},{8,12},{12,14},{14,10},{10,6},{6,2},{2,0},{1,5},{5,9},... | collective-permute-start | bytes 344072 | tf_op jit(solution)/shard_map/ppermute | solution.py:26
  67.4 9.6 %collective-permute-start.19 = (bf16[224,256]{1,0:T(8,128)(2,1)S(1)}, bf16[224,256]{1,0:T(8,128)(2,1)S(1)}, u32[]{:S(2)}, u32[]{:S(2)}) collective-permute-start(bf16[224,256]{1,0:T(8,128)(2,1)S(1)} %add_convert_fusion.9), channel_id=1, source_target_pairs={{0,4},{4,8},{8,12},{12,14},{14,10},{10,6},{6,2},{2,0},{1,5},{5,9},... | collective-permute-start | bytes 344072 | tf_op jit(solution)/shard_map/ppermute | solution.py:26
  69.0 7.8 %collective-permute-start.33 = (f32[128,256]{1,0:T(8,128)S(1)}, f32[128,256]{1,0:T(8,128)S(1)}, u32[]{:S(2)}, u32[]{:S(2)}) collective-permute-start(f32[128,256]{1,0:T(8,128)S(1)} %dynamic-slice_add_fusion), channel_id=1, source_target_pairs={{0,2},{2,0},{4,6},{6,4},{8,10},{10,8},{12,14},{14,12},{1,3},{3,1},... | collective-permute-start | bytes 393224 | tf_op jit(solution)/shard_map/ppermute | solution.py:207
  69.6 19.9 %copy-start.5 = (bf16[224,256]{1,0:T(8,128)(2,1)S(1)}, bf16[224,256]{1,0:T(8,128)(2,1)}, u32[]{:S(2)}) copy-start(bf16[224,256]{1,0:T(8,128)(2,1)} %copy-done.4) | copy-start | bytes 344068
  69.6 19.9 %copy-start.7 = (bf16[224,256]{1,0:T(8,128)(2,1)S(1)}, bf16[224,256]{1,0:T(8,128)(2,1)}, u32[]{:S(2)}) copy-start(bf16[224,256]{1,0:T(8,128)(2,1)} %copy-done.6) | copy-start | bytes 344068
  69.6 13.3 %collective-permute-start.30 = (bf16[224,256]{1,0:T(8,128)(2,1)S(1)}, bf16[224,256]{1,0:T(8,128)(2,1)S(1)}, u32[]{:S(2)}, u32[]{:S(2)}) collective-permute-start(bf16[224,256]{1,0:T(8,128)(2,1)S(1)} %add_convert_fusion.1), channel_id=1, source_target_pairs={{0,2},{4,0},{8,4},{12,8},{14,12},{10,14},{6,10},{2,6},{1,3},{5,1},... | collective-permute-start | bytes 344072 | tf_op jit(solution)/shard_map/ppermute | solution.py:26
  71.2 18.3 %copy-start.1 = (bf16[8,512,256]{2,1,0:T(8,128)(2,1)S(1)}, bf16[8,512,256]{2,1,0:T(8,128)(2,1)}, u32[]{:S(2)}) copy-start(bf16[8,512,256]{2,1,0:T(8,128)(2,1)} %down.3) | copy-start | bytes 6291460
  71.2 18.3 %copy-start.13 = (bf16[448,512]{1,0:T(8,128)(2,1)S(1)}, bf16[448,512]{1,0:T(8,128)(2,1)}, u32[]{:S(2)}) copy-start(bf16[448,512]{1,0:T(8,128)(2,1)} %copy-done.12) | copy-start | bytes 1376260
  71.3 20.1 %collective-permute-start.27 = (bf16[224,256]{1,0:T(8,128)(2,1)S(1)}, bf16[224,256]{1,0:T(8,128)(2,1)S(1)}, u32[]{:S(2)}, u32[]{:S(2)}) collective-permute-start(bf16[224,256]{1,0:T(8,128)(2,1)S(1)} %add_convert_fusion.3), channel_id=1, source_target_pairs={{0,2},{4,0},{8,4},{12,8},{14,12},{10,14},{6,10},{2,6},{1,3},{5,1},... | collective-permute-start | bytes 344072 | tf_op jit(solution)/shard_map/ppermute | solution.py:26
  72.9 18.5 %collective-permute-start.24 = (bf16[224,256]{1,0:T(8,128)(2,1)S(1)}, bf16[224,256]{1,0:T(8,128)(2,1)S(1)}, u32[]{:S(2)}, u32[]{:S(2)}) collective-permute-start(bf16[224,256]{1,0:T(8,128)(2,1)S(1)} %add_convert_fusion.5), channel_id=1, source_target_pairs={{0,4},{4,8},{8,12},{12,14},{14,10},{10,6},{6,2},{2,0},{1,5},{5,9},... | collective-permute-start | bytes 344072 | tf_op jit(solution)/shard_map/ppermute | solution.py:26
  76.9 5.0 %collective-permute-start.34 = (f32[128,256]{1,0:T(8,128)S(1)}, f32[128,256]{1,0:T(8,128)S(1)}, u32[]{:S(2)}, u32[]{:S(2)}) collective-permute-start(f32[128,256]{1,0:T(8,128)S(1)} %add.109), channel_id=1, source_target_pairs={{0,4},{2,6},{4,0},{6,2},{8,12},{10,14},{12,8},{14,10},{1,5},{3,7},... | collective-permute-start | bytes 393224 | tf_op jit(solution)/shard_map/ppermute | solution.py:207
  77.0 12.3 %collective-permute-start.20 = (bf16[224,256]{1,0:T(8,128)(2,1)S(1)}, bf16[224,256]{1,0:T(8,128)(2,1)S(1)}, u32[]{:S(2)}, u32[]{:S(2)}) collective-permute-start(bf16[224,256]{1,0:T(8,128)(2,1)S(1)} %add_convert_fusion.8), channel_id=1, source_target_pairs={{0,4},{4,8},{8,12},{12,14},{14,10},{10,6},{6,2},{2,0},{1,5},{5,9},... | collective-permute-start | bytes 344072 | tf_op jit(solution)/shard_map/ppermute | solution.py:26
  82.0 7.3 %collective-permute-start.35 = (f32[128,256]{1,0:T(8,128)S(1)}, f32[128,256]{1,0:T(8,128)S(1)}, u32[]{:S(2)}, u32[]{:S(2)}) collective-permute-start(f32[128,256]{1,0:T(8,128)S(1)} %add.110), channel_id=1, source_target_pairs={{0,8},{2,10},{4,12},{6,14},{8,0},{10,2},{12,4},{14,6},{1,9},{3,11}... | collective-permute-start | bytes 393224 | tf_op jit(solution)/shard_map/ppermute | solution.py:207
  82.9 8.5 %collective-permute-start.31 = (bf16[224,256]{1,0:T(8,128)(2,1)S(1)}, bf16[224,256]{1,0:T(8,128)(2,1)S(1)}, u32[]{:S(2)}, u32[]{:S(2)}) collective-permute-start(bf16[224,256]{1,0:T(8,128)(2,1)S(1)} %add_convert_fusion), channel_id=1, source_target_pairs={{0,2},{4,0},{8,4},{12,8},{14,12},{10,14},{6,10},{2,6},{1,3},{5,1},... | collective-permute-start | bytes 344072 | tf_op jit(solution)/shard_map/ppermute | solution.py:26
  89.3 6.7 %collective-permute-start.36 = (f32[128,256]{1,0:T(8,128)S(1)}, f32[128,256]{1,0:T(8,128)S(1)}, u32[]{:S(2)}, u32[]{:S(2)}) collective-permute-start(f32[128,256]{1,0:T(8,128)S(1)} %add.111), channel_id=1, source_target_pairs={{0,1},{1,0},{2,3},{3,2},{4,5},{5,4},{6,7},{7,6},{8,9},{9,8},{10,11... | collective-permute-start | bytes 393224 | tf_op jit(solution)/shard_map/ppermute | solution.py:30
  89.4 5.6 %collective-permute-start.21 = (bf16[224,256]{1,0:T(8,128)(2,1)S(1)}, bf16[224,256]{1,0:T(8,128)(2,1)S(1)}, u32[]{:S(2)}, u32[]{:S(2)}) collective-permute-start(bf16[224,256]{1,0:T(8,128)(2,1)S(1)} %add_convert_fusion.7), channel_id=1, source_target_pairs={{0,4},{4,8},{8,12},{12,14},{14,10},{10,6},{6,2},{2,0},{1,5},{5,9},... | collective-permute-start | bytes 344072 | tf_op jit(solution)/shard_map/ppermute | solution.py:26
  89.6 5.5 %copy-start.9 = (bf16[448,256]{1,0:T(8,128)(2,1)S(1)}, bf16[448,256]{1,0:T(8,128)(2,1)}, u32[]{:S(2)}) copy-start(bf16[448,256]{1,0:T(8,128)(2,1)} %out_grad.3) | copy-start | bytes 688132
  89.6 5.5 %copy-start.11 = (bf16[256,256]{1,0:T(8,128)(2,1)S(1)}, bf16[256,256]{1,0:T(8,128)(2,1)}, u32[]{:S(2)}) copy-start(bf16[256,256]{1,0:T(8,128)(2,1)} %weight.1) | copy-start | bytes 393220

commit v2 on v1

v2 whole, which is shorter than its diff:
```python
import functools

import jax
import jax.numpy as jnp
from jax import lax
from jax.experimental import pallas as pl
from jax.experimental.pallas import tpu as pltpu
from jax.sharding import PartitionSpec as P

BF16 = jnp.bfloat16
F32 = jnp.float32
NT = (((1,), (1,)), ((), ()))
TN = (((0,), (0,)), ((), ()))
VMEM_LIMIT = 30 * 1024 * 1024


def ring_order(size):
    if size <= 8:
        return list(range(0, size, 2)) + list(range(1, size, 2))[::-1]
    return list(range(size))


def along_ring(block, order, hop):
    size = len(order)
    route = [(order[place], order[(place + hop) % size]) for place in range(size)]
    return lax.ppermute(block, "grid", route)


def other_core(block):
    return lax.ppermute(block, "rep", [(0, 1), (1, 0)])


def swapped(block, distance, across=False):
    axes, flip = ("grid", "rep"), 2 * distance + int(across)
    route = [(device, device ^ flip) for device in range(2 * lax.axis_size("grid"))]
    return lax.ppermute(block, axes, route)


def call(kernel, out_shape, smem, vmem, scratch=(), flops=0):
    moved = sum(item.size * item.dtype.itemsize for item in (*vmem, *jax.tree.leaves(out_shape)))
    return pl.pallas_call(
        kernel,
        out_shape=out_shape,
        in_specs=[pl.BlockSpec(memory_space=pltpu.SMEM)] * len(smem)
        + [pl.BlockSpec(memory_space=pltpu.VMEM)] * len(vmem),
        out_specs=jax.tree.map(lambda _: pl.BlockSpec(memory_space=pltpu.VMEM), out_shape),
        scratch_shapes=list(scratch),
        compiler_params=pltpu.CompilerParams(vmem_limit_bytes=VMEM_LIMIT),
        cost_estimate=pl.CostEstimate(flops=flops, bytes_accessed=moved, transcendentals=0),
    )(*smem, *vmem)


def struct(shape, dtype):
    return jax.ShapeDtypeStruct(shape, dtype)


def ring_place(chip, size):
    if size <= 8:
        return jnp.where(lax.rem(chip, 2) == 0, lax.div(chip, 2), size - 1 - lax.div(chip, 2))
    return chip


def distances(place, own_table, other_table, size):
    core, chip = place[0], place[1]
    slots = own_table.shape[1]
    found = []
    for replica in range(2):
        for slot in range(slots):
            step = jnp.where(core == replica, own_table[0, slot], other_table[0, slot])
            source = lax.rem(chip - replica * (size // 2) - step + 2 * size, size)
            found.append(lax.rem(ring_place(source, size) - ring_place(chip, size) + size, size))
    return found


def edge_counts(place, own_table, other_table):
    core = place[0]
    slots = own_table.shape[1]
    return [
        jnp.where(core == replica, own_table[1, slot], other_table[1, slot]).astype(F32)
        for replica in range(2)
        for slot in range(slots)
    ]


def flip_kernel(tile, flipped):
    for slot in range(tile.shape[0]):
        flipped[slot] = jnp.swapaxes(tile[slot], 0, 1)


def pick_kernel(size, offsets, place, own_table, other_table, *refs):
    blocks, rows = refs[:-1], refs[-1]
    chosen = distances(place, own_table, other_table, size)
    for slot in range(rows.shape[0]):
        for block, (offset, start) in zip(blocks, offsets, strict=True):

            @pl.when(chosen[slot] == offset)
            def _(slot=slot, block=block, start=start):
                rows[slot, pl.ds(start, block.shape[0]), :] = block[...]


def prepare_kernel(place, types, out_grad, down, mask, grad_hidden, column):
    experts, half, width = mask.shape
    block = types.shape[0]
    row = types[...].astype(F32).reshape(1, block)
    column[...] = jnp.swapaxes(jnp.broadcast_to(row, (8, block)), 0, 1)
    own = column[pl.ds(pl.multiple_of(place[0] * half, half), half), 0:1]
    own = jnp.broadcast_to(own, (half, width))
    total = None
    for expert in range(experts):
        mask[expert] = jnp.where(own == expert, 1.0, 0.0).astype(BF16)
        term = lax.dot_general(
            out_grad[...] * mask[expert], down[expert], NT, preferred_element_type=F32
        )
        total = term if total is None else total + term
    grad_hidden[...] = total


def middle_kernel(
    place,
    own_table,
    other_table,
    own_tile,
    other_tile,
    own_rows,
    other_rows,
    weight,
    mask,
    up,
    grad_hidden,
    hidden,
    packed,
    kept,
    rows,
    wide,
):
    slots = own_tile.shape[0]
    experts, width, inner = up.shape
    half = own_rows.shape[1]
    core = place[0]
    own_start = pl.multiple_of(core * half, half)
    other_start = pl.multiple_of((1 - core) * half, half)
    for slot in range(2 * slots):
        rows[slot, pl.ds(own_start, half), :] = own_rows[slot]
        rows[slot, pl.ds(other_start, half), :] = other_rows[slot]
    total = jnp.zeros((half, width), F32)
    for slot in range(slots):
        for tile, table, which in (
            (own_tile, own_table, core),
            (other_tile, other_table, 1 - core),
        ):
            total += table[1, slot].astype(F32) * jnp.dot(
                tile[slot, pl.ds(own_start, half), :],
                rows[which * slots + slot],
                preferred_element_type=F32,
            )
    high = total.astype(BF16)
    rest = (total - high.astype(F32)).astype(BF16)
    aggregate = jnp.dot(high, weight[...], preferred_element_type=F32)
    aggregate += jnp.dot(rest, weight[...], preferred_element_type=F32)
    edges = jnp.full((1, 1), sum(edge_counts(place, own_table, other_table)), F32)
    aggregate = aggregate / edges
    inv_rms = lax.rsqrt(jnp.mean(aggregate * aggregate, axis=-1, keepdims=True) + 1e-06)
    normed = aggregate * inv_rms
    normed_bf = normed.astype(BF16)
    for expert in range(experts):
        wide[:, expert * width : (expert + 1) * width] = normed_bf * mask[expert]
    up_act = jnp.dot(
        wide[...], up[...].reshape(experts * width, inner), preferred_element_type=F32
    )
    gate = 1.0 / (1.0 + jnp.exp(-up_act))
    hidden[...] = (up_act * gate).astype(BF16)
    grad_act = (grad_hidden[...] * gate * (1.0 + up_act * (1.0 - gate))).astype(BF16)
    grad_pre = jnp.zeros((half, width), F32)
    for expert in range(experts):
        term = lax.dot_general(grad_act, up[expert], NT, preferred_element_type=F32)
        grad_pre += term * mask[expert].astype(F32)
    grad_agg = inv_rms * (
        grad_pre - normed * jnp.mean(grad_pre * normed, axis=-1, keepdims=True)
    )
    grad_scaled = (grad_agg / edges).astype(BF16)
    packed[:half] = grad_scaled
    term = lax.dot_general(high, grad_scaled, TN, preferred_element_type=F32)
    upper, lower = term[: width // 2], term[width // 2 :]
    kept[...] = jnp.where(core == 0, upper, lower)
    packed[half:] = jnp.where(core == 0, lower, upper).astype(BF16)


def product_kernel(
    size,
    place,
    own_table,
    other_table,
    own_flipped,
    other_flipped,
    own_packed,
    other_packed,
    kept,
    products,
    far_first,
    far_second,
    weight_part,
    full_grad,
):
    slots, half = own_flipped.shape[0], products.shape[1]
    core = place[0]
    own_start = pl.multiple_of(core * half, half)
    full_grad[pl.ds(own_start, half), :] = own_packed[:half]
    full_grad[pl.ds(pl.multiple_of((1 - core) * half, half), half), :] = other_packed[:half]
    weight_part[...] = (kept[...] + other_packed[half:].astype(F32)).astype(BF16)
    chosen = distances(place, own_table, other_table, size)
    total = jnp.zeros(products.shape[1:], F32)
    for flipped, table, which in (
        (own_flipped, own_table, core),
        (other_flipped, other_table, 1 - core),
    ):
        for slot in range(slots):
            product = table[1, slot].astype(F32) * jnp.dot(
                flipped[slot, pl.ds(own_start, half), :],
                full_grad[...],
                preferred_element_type=F32,
            )
            products[which * slots + slot] = product
            distance = jnp.where(which == 0, chosen[slot], chosen[slots + slot])
            total += jnp.where(distance == size // 2, product, 0.0)
    cut = far_first.shape[0]
    far_first[...] = total[:cut].astype(BF16)
    far_second[...] = total[cut:].astype(BF16)


def spread_kernel(size, offsets, place, own_table, other_table, products, *terms):
    chosen = distances(place, own_table, other_table, size)
    for term, (offset, start) in zip(terms, offsets, strict=True):
        length = term.shape[0]
        total = jnp.where(chosen[0] == offset, products[0, start : start + length], 0.0)
        for slot in range(1, products.shape[0]):
            total += jnp.where(chosen[slot] == offset, products[slot, start : start + length], 0.0)
        term[...] = total.astype(term.dtype)


def update_kernel(mask, hidden, down, feats_first, feats_second, updated):
    experts, inner, width = down.shape
    total = jnp.concatenate([feats_first[...], feats_second[...]], axis=0).astype(F32)
    for expert in range(experts):
        masked = jnp.concatenate(
            [
                hidden[:, start : start + width] * mask[expert]
                for start in range(0, inner, width)
            ],
            axis=1,
        )
        total += jnp.dot(masked, down[expert], preferred_element_type=F32)
    updated[...] = total.astype(BF16)


def finish_kernel(
    place,
    own,
    up_first,
    up_second,
    down_first,
    down_second,
    weight,
    out_grad,
    own_part,
    own_swapped,
    other_part,
    other_swapped,
    result,
    weight_grad,
):
    cut = up_first.shape[0]
    for start, pair in ((0, (up_first, down_first)), (cut, (up_second, down_second))):
        length = pair[0].shape[0]
        grad_msg = (
            own[start : start + length] + pair[0][...].astype(F32) + pair[1][...].astype(F32)
        ).astype(BF16)
        back = lax.dot_general(grad_msg, weight[...], NT, preferred_element_type=F32)
        result[start : start + length] = (
            out_grad[start : start + length].astype(F32) + back
        ).astype(BF16)
    half = own_part.shape[0]
    upper = own_part[...].astype(F32) + own_swapped[...].astype(F32)
    lower = other_part[...].astype(F32) + other_swapped[...].astype(F32)
    weight_grad[:half] = jnp.where(place[0] == 0, upper, lower)
    weight_grad[half:] = jnp.where(place[0] == 0, lower, upper)


def per_device(
    feats, msg_weight, tiles, tile_step, tile_count, node_type, expert_up, expert_down, out_grad
):
    size = lax.axis_size("grid")
    core = lax.axis_index("rep")
    chip = lax.axis_index("grid")
    order = ring_order(size)
    far = size // 2
    slots = tiles.shape[2]
    block, width = feats.shape
    half = block // 2
    cut = half // 2
    experts, _, inner = expert_up.shape

    first = lax.dynamic_slice_in_dim(feats, core * half, cut, 0)
    second = lax.dynamic_slice_in_dim(feats, core * half + cut, half - cut, 0)

    place = jnp.stack([core, chip]).astype(jnp.int32)
    tile_own, _ = lax.optimization_barrier((tiles[0, 0], first))
    own_table = jnp.stack([tile_step[0, 0], tile_count[0, 0]])
    other_table = other_core(own_table)
    tile_other = other_core(tile_own)
    flip = functools.partial(call, flip_kernel, struct(tile_own.shape, BF16), ())

    arrived = [(0, 0, first), (0, cut, second)]
    up_a = down_a = first
    up_b = down_b = second
    flipped_own = flip((tile_own,))
    for step in range(1, far):
        if step == 2:
            grads_out, _, _ = lax.optimization_barrier((out_grad, up_a, down_b))
            mask, grad_hidden = call(
                prepare_kernel,
                [struct((experts, half, width), BF16), struct((half, inner), F32)],
                (place,),
                (node_type, grads_out, expert_down),
                (pltpu.VMEM((block, 8), F32),),
            )
            up_a, down_b, flipped_own, other_table = lax.optimization_barrier(
                (up_a, down_b, flipped_own, other_table)
            )
        if step == 3:
            up_a, down_b, grad_hidden, mask = lax.optimization_barrier(
                (up_a, down_b, grad_hidden, mask)
            )
        up_a = along_ring(up_a, order, 1)
        down_b = along_ring(down_b, order, -1)
        up_b = along_ring(up_b, order, 1)
        down_a = along_ring(down_a, order, -1)
        arrived += [(size - step, 0, up_a), (size - step, cut, up_b)]
        arrived += [(step, 0, down_a), (step, cut, down_b)]
    tables = (place, own_table, other_table)
    far_first, far_second = along_ring(up_a, order, 1), along_ring(down_b, order, -1)
    arrived += [(far, 0, far_first), (far, cut, far_second)]
    tile_late, _, _ = lax.optimization_barrier((tile_other, up_a, down_b))
    flipped_other = flip((tile_late,))
    source_rows = call(
        functools.partial(pick_kernel, size, [item[:2] for item in arrived]),
        struct((2 * slots, half, width), BF16),
        tables,
        [piece for _, _, piece in arrived],
    )
    other_rows = other_core(source_rows)

    hidden, packed, kept = call(
        middle_kernel,
        [
            struct((half, inner), BF16),
            struct((half + width // 2, width), BF16),
            struct((width // 2, width), F32),
        ],
        tables,
        (
            tile_own,
            tile_other,
            source_rows,
            other_rows,
            msg_weight,
            mask,
            expert_up,
            grad_hidden,
        ),
        (
            pltpu.VMEM((2 * slots, block, width), BF16),
            pltpu.VMEM((half, experts * width), BF16),
        ),
        flops=4 * half * width * (slots * block + experts * inner),
    )
    other_packed = other_core(packed)

    halves = [struct((cut, width), BF16), struct((half - cut, width), BF16)]
    products, up_a, down_b, mine = call(
        functools.partial(product_kernel, size),
        [struct((2 * slots, half, width), F32), *halves, struct((width // 2, width), BF16)],
        tables,
        (flipped_own, flipped_other, packed, other_packed, kept),
        (pltpu.VMEM((block, width), BF16),),
        flops=4 * half * width * slots * block,
    )
    up_a = along_ring(up_a, order, 1)
    down_b = along_ring(down_b, order, -1)
    keys, shapes = [(0, 0)], [struct((half, width), F32)]
    for step in range(far - 1, 0, -1):
        for offset in (step, size - step):
            keys += [(offset, 0), (offset, cut)]
            shapes += halves
    terms = call(functools.partial(spread_kernel, size, keys), shapes, tables, (products,))
    terms = dict(zip(keys, terms, strict=True))

    def joined(received, term):
        return (received.astype(F32) + term.astype(F32)).astype(BF16)

    swap = size // 2
    theirs = swapped(mine, swap)
    up_b, down_a = lax.optimization_barrier(
        (terms[far - 1, cut], terms[size - far + 1, 0], up_a, down_b)
    )[:2]
    for step in range(far - 1, 0, -1):
        up_a = joined(up_a, terms[step, 0])
        down_b = joined(down_b, terms[size - step, cut])
        if step < far - 1:
            up_b = joined(up_b, terms[step, cut])
            down_a = joined(down_a, terms[size - step, 0])
            if swap > 2:
                swap //= 2
                mine = lax.optimization_barrier((joined(mine, theirs), up_a, down_b))[0]
                theirs = swapped(mine, swap)
        if step == 1:
            while swap > 2:
                swap //= 2
                mine = joined(mine, theirs)
                theirs = swapped(mine, swap)
            if swap > 1:
                mine = lax.optimization_barrier((joined(mine, theirs), up_a, down_b))[0]
            weight_parts = (mine, swapped(mine, 1), other_core(mine), swapped(mine, 1, across=True))
        up_a = along_ring(up_a, order, 1)
        down_b = along_ring(down_b, order, -1)
        up_b = along_ring(up_b, order, 1)
        down_a = along_ring(down_a, order, -1)

    updated = call(
        update_kernel,
        struct((half, width), BF16),
        (),
        (mask, hidden, expert_down, first, second),
    )
    feats_grad, msg_weight_grad = call(
        finish_kernel,
        [struct((half, width), BF16), struct((width, width), F32)],
        (place,),
        (
            terms[0, 0],
            up_a,
            up_b,
            down_a,
            down_b,
            msg_weight,
            out_grad,
            *weight_parts,
        ),
    )
    return (updated, feats_grad, msg_weight_grad)


def solution(mesh):
    return jax.shard_map(
        per_device,
        mesh=mesh,
        in_specs=(
            P(("groups", "grid"), None),
            P(),
            P(("groups", "grid"), "rep", None, None, None),
            P(("groups", "grid"), "rep", None),
            P(("groups", "grid"), "rep", None),
            P(("groups", "grid")),
            P(),
            P(),
            P(("groups", "grid", "rep"), None),
        ),
        out_specs=(
            P(("groups", "grid", "rep"), None),
            P(("groups", "grid", "rep"), None),
            P("groups", None),
        ),
        check_vma=False,
    )
```

time: 97.2 us -> 77.6 us (0.80)
  local copies, waits for them, and re-layouts: 19.2 us -> 3.7 us
  waiting for transfers between devices: 22.1 us -> 17.3 us
  other arithmetic: 2.79 us -> 0.42 us
  starting transfers between devices: 35.5 us -> 37.6 us
  Pallas kernels: 14.8 us -> 16.2 us
    dynamic_slice x7 -> x0, local copies, waits for them, and re-layouts: 6.84 us -> none  [the longest x3 4.82 us: rows_of(): return lax.dynamic_slice_in_dim(tile, core * half, half, 1)]
    unnamed x51 -> x18, local copies, waits for them, and re-layouts: 8.12 us -> 2.73 us
    ppermute x3 -> x4, starting transfers between devices: 1.49 us -> 5.1 us  [swapped(): return lax.ppermute(block, axes, route)]
    another operation x2 -> x0, local copies, waits for them, and re-layouts: 3.04 us -> none
    ppermute x28, waiting for transfers between devices: 12.6 us -> 9.78 us  [along_ring(): return lax.ppermute(block, 'grid', route)]
    ppermute x3 -> x4, waiting for transfers between devices: 8.35 us -> 5.67 us  [swapped(): return lax.ppermute(block, axes, route)]
    ppermute x28, starting transfers between devices: 32.8 us -> 31 us  [along_ring(): return lax.ppermute(block, 'grid', route)]
    pallas_call x7 -> x9, Pallas kernels: 14.8 us -> 16.2 us  [call(): pl.pallas_call(kernel, out_shape=out_shape, in_specs=[pl.BlockSpec(memory...]
  transfers between devices with their start and end apart: 37 -> 37, of which waited for: 14 -> 13; matrix products, arithmetic and copies ran while one was open for 14% -> 1% of each run, Pallas kernels for 7% -> 11%
where the time goes in v2:
time: 77.6 us; the launch traced here: 77.4 us
  starting transfers between devices  37.6 us (48%)
  waiting for transfers between devices  17.3 us (22%)
  Pallas kernels  16.2 us (21%)
  local copies, waits for them, and re-layouts  3.7 us (5%)
  between operations  2.22 us (3%)
    ppermute x28, starting transfers between devices, along_ring(): return lax.ppermute(block, 'grid', route)  31 us
    pallas_call x9, Pallas kernels, call(): pl.pallas_call(kernel, out_shape=out_shape, in_specs=[pl.BlockSpec(memory...  16.2 us
    ppermute x28, waiting for transfers between devices, along_ring(): return lax.ppermute(block, 'grid', route)  9.78 us
    ppermute x4, waiting for transfers between devices, swapped(): return lax.ppermute(block, axes, route)  5.67 us
    ppermute x4, starting transfers between devices, swapped(): return lax.ppermute(block, axes, route)  5.1 us
    unnamed x18, local copies, waits for them, and re-layouts  2.73 us
    ppermute x5, waiting for transfers between devices, other_core(): return lax.ppermute(block, 'rep', [(0, 1), (1, 0)])  1.81 us
  transfers between devices with their start and end apart: 37, of which 13 were waited for; matrix products, arithmetic and copies ran while one was open for 1% of the time, Pallas kernels for 11%

profile of v2, /device:TPU:0, one launch (start us, length us, event | category | flops | bytes accessed | tf_op | source)
XLA Modules:
  0.0 77.4 jit_solution(684299904654115697)
XLA Ops:
  0.6 1.0 %constant_dynamic-slice_fusion = (bf16[224,256]{1,0:T(8,128)(2,1)S(1)}, bf16[224,256]{1,0:T(8,128)(2,1)S(1)}) fusion(bf16[896,256]{1,0:T(8,128)(2,1)} %param.9, s32[]{:T(128)S(6)} %select_n.7, s32[]{:T(128)S(6)} %select_n.6), kind=kLoop, calls=%fused_computation.14 | loop fusion | bytes 458760 | tf_op jit(solution)/shard_map/dynamic_slice | solution.py:303
  1.6 0.5 collective-permute-start.5
  2.1 2.6 %collective-permute-start.1 = (bf16[224,256]{1,0:T(8,128)(2,1)S(1)}, bf16[224,256]{1,0:T(8,128)(2,1)S(1)}, u32[]{:S(2)}, u32[]{:S(2)}) collective-permute-start(bf16[224,256]{1,0:T(8,128)(2,1)S(1)} %get-tuple-element.81.refs_1_.feats_second), channel_id=1, source_target_pairs={{0,2},{4,0},{8,4},{12,8},{14,12},{10,14},{6,10},{2,6},{1,3},{5,1},... | collective-permute-start | bytes 344072 | tf_op jit(solution)/shard_map/ppermute | solution.py:26
  4.7 0.1 collective-permute-start
  4.9 1.9 %collective-permute-start.6 = (bf16[224,256]{1,0:T(8,128)(2,1)S(1)}, bf16[224,256]{1,0:T(8,128)(2,1)S(1)}, u32[]{:S(2)}, u32[]{:S(2)}) collective-permute-start(bf16[224,256]{1,0:T(8,128)(2,1)S(1)} %get-tuple-element.81.refs_1_.feats_second), channel_id=1, source_target_pairs={{0,4},{4,8},{8,12},{12,14},{14,10},{10,6},{6,2},{2,0},{1,5},{5,9},... | collective-permute-start | bytes 344072 | tf_op jit(solution)/shard_map/ppermute | solution.py:26
  8.1 0.0 copy-start
  8.1 0.1 collective-permute-start.2
  8.2 1.5 %copy-done.1 = bf16[1,1,1,896,896]{4,3,2,1,0:T(8,128)(2,1)S(1)} copy-done((bf16[1,1,1,896,896]{4,3,2,1,0:T(8,128)(2,1)S(1)}, bf16[1,1,1,896,896]{4,3,2,1,0:T(8,128)(2,1)}, u32[]{:S(2)}) %copy-start.1) | copy-done | bytes 1605656
  9.8 0.5 shard_map.112.own_flipped
  10.2 1.1 %copy-done.3 = bf16[1,896,896]{2,1,0:T(8,128)(2,1)} copy-done((bf16[1,896,896]{2,1,0:T(8,128)(2,1)}, bf16[1,896,896]{2,1,0:T(8,128)(2,1)S(1)}, u32[]{:S(2)}) %copy-start.3) | copy-done | bytes 1605656
  11.4 0.1 collective-permute-start.7
  11.5 1.9 %collective-permute-start.3 = (bf16[224,256]{1,0:T(8,128)(2,1)S(1)}, bf16[224,256]{1,0:T(8,128)(2,1)S(1)}, u32[]{:S(2)}, u32[]{:S(2)}) collective-permute-start(bf16[224,256]{1,0:T(8,128)(2,1)S(1)} %collective-permute-done.refs_2_), channel_id=1, source_target_pairs={{0,4},{4,8},{8,12},{12,14},{14,10},{10,6},{6,2},{2,0},{1,5},{5,9},... | collective-permute-start | bytes 344072 | tf_op jit(solution)/shard_map/ppermute | solution.py:26
  13.4 0.1 collective-permute-start.4
  13.5 0.1 pad_add_fusion.1.place
  13.6 2.1 %shard_map.113 = (bf16[8,448,256]{2,1,0:T(8,128)(2,1)S(1)}, f32[448,512]{1,0:T(8,128)S(1)}) custom-call(s32[2]{0:T(128)S(1)} %pad_add_fusion.1.place, s32[896]{0:T(1024)S(1)} %copy-done.8, bf16[448,256]{1,0:T(8,128)(2,1)S(1)} %copy-done.6, bf16[8,512,256]{2,1,0:T(8,128)(2,1)S(1)} %copy-done), custom_call_target="tpu_custom_call" | custom-call | bytes 5082624 | tf_op jit(solution)/shard_map/pallas_call | solution.py:41
  15.8 2.0 %collective-permute-start.8 = (bf16[224,256]{1,0:T(8,128)(2,1)S(1)}, bf16[224,256]{1,0:T(8,128)(2,1)S(1)}, u32[]{:S(2)}, u32[]{:S(2)}) collective-permute-start(bf16[224,256]{1,0:T(8,128)(2,1)S(1)} %collective-permute-done.6.refs_3_), channel_id=1, source_target_pairs={{0,4},{4,8},{8,12},{12,14},{14,10},{10,6},{6,2},{2,0},{1,5},{5,9},... | collective-permute-start | bytes 344072 | tf_op jit(solution)/shard_map/ppermute | solution.py:26
  17.8 0.1 collective-permute-start.9
  17.8 1.4 %collective-permute-done.4.refs_9_ = bf16[224,256]{1,0:T(8,128)(2,1)S(1)} collective-permute-done((bf16[224,256]{1,0:T(8,128)(2,1)S(1)}, bf16[224,256]{1,0:T(8,128)(2,1)S(1)}, u32[]{:S(2)}, u32[]{:S(2)}) %collective-permute-start.4) | collective-permute-done | bytes 114720 | tf_op jit(solution)/shard_map/ppermute | solution.py:26
  19.3 1.6 %collective-permute-start.10 = (bf16[224,256]{1,0:T(8,128)(2,1)S(1)}, bf16[224,256]{1,0:T(8,128)(2,1)S(1)}, u32[]{:S(2)}, u32[]{:S(2)}) collective-permute-start(bf16[224,256]{1,0:T(8,128)(2,1)S(1)} %collective-permute-done.3.refs_6_), channel_id=1, source_target_pairs={{0,4},{4,8},{8,12},{12,14},{14,10},{10,6},{6,2},{2,0},{1,5},{5,9},... | collective-permute-start | bytes 344072 | tf_op jit(solution)/shard_map/ppermute | solution.py:26
  20.8 0.4 collective-permute-start.13
  21.3 1.6 %collective-permute-start.11 = (bf16[224,256]{1,0:T(8,128)(2,1)S(1)}, bf16[224,256]{1,0:T(8,128)(2,1)S(1)}, u32[]{:S(2)}, u32[]{:S(2)}) collective-permute-start(bf16[224,256]{1,0:T(8,128)(2,1)S(1)} %collective-permute-done.8.refs_7_), channel_id=1, source_target_pairs={{0,4},{4,8},{8,12},{12,14},{14,10},{10,6},{6,2},{2,0},{1,5},{5,9},... | collective-permute-start | bytes 344072 | tf_op jit(solution)/shard_map/ppermute | solution.py:26
  22.9 0.4 collective-permute-start.12
  23.3 1.9 %collective-permute-done.10.refs_10_ = bf16[224,256]{1,0:T(8,128)(2,1)S(1)} collective-permute-done((bf16[224,256]{1,0:T(8,128)(2,1)S(1)}, bf16[224,256]{1,0:T(8,128)(2,1)S(1)}, u32[]{:S(2)}, u32[]{:S(2)}) %collective-permute-start.10) | collective-permute-done | bytes 114720 | tf_op jit(solution)/shard_map/ppermute | solution.py:26
  25.2 1.6 %collective-permute-start.14 = (bf16[224,256]{1,0:T(8,128)(2,1)S(1)}, bf16[224,256]{1,0:T(8,128)(2,1)S(1)}, u32[]{:S(2)}, u32[]{:S(2)}) collective-permute-start(bf16[224,256]{1,0:T(8,128)(2,1)S(1)} %collective-permute-done.10.refs_10_), channel_id=1, source_target_pairs={{0,4},{4,8},{8,12},{12,14},{14,10},{10,6},{6,2},{2,0},{1,5},{5,9},... | collective-permute-start | bytes 344072 | tf_op jit(solution)/shard_map/ppermute | solution.py:26
  26.8 0.4 collective-permute-start.15
  27.3 0.4 collective-permute-done.11.refs_11_
  27.7 1.3 %collective-permute-done.12.refs_12_ = bf16[224,256]{1,0:T(8,128)(2,1)S(1)} collective-permute-done((bf16[224,256]{1,0:T(8,128)(2,1)S(1)}, bf16[224,256]{1,0:T(8,128)(2,1)S(1)}, u32[]{:S(2)}, u32[]{:S(2)}) %collective-permute-start.12) | collective-permute-done | bytes 114720 | tf_op jit(solution)/shard_map/ppermute | solution.py:26
  29.0 1.0 %collective-permute-done.14.refs_14_ = bf16[224,256]{1,0:T(8,128)(2,1)S(1)} collective-permute-done((bf16[224,256]{1,0:T(8,128)(2,1)S(1)}, bf16[224,256]{1,0:T(8,128)(2,1)S(1)}, u32[]{:S(2)}, u32[]{:S(2)}) %collective-permute-start.14) | collective-permute-done | bytes 114720 | tf_op jit(solution)/shard_map/ppermute | solution.py:26
  30.0 1.6 %collective-permute-done.15.refs_15_ = bf16[224,256]{1,0:T(8,128)(2,1)S(1)} collective-permute-done((bf16[224,256]{1,0:T(8,128)(2,1)S(1)}, bf16[224,256]{1,0:T(8,128)(2,1)S(1)}, u32[]{:S(2)}, u32[]{:S(2)}) %collective-permute-start.15) | collective-permute-done | bytes 114720 | tf_op jit(solution)/shard_map/ppermute | solution.py:26
  31.6 0.7 shard_map.114.own_rows
  32.3 0.1 collective-permute-start.16
  32.4 1.8 %collective-permute-done.16.other_rows = bf16[2,448,256]{2,1,0:T(8,128)(2,1)S(1)} collective-permute-done((bf16[2,448,256]{2,1,0:T(8,128)(2,1)S(1)}, bf16[2,448,256]{2,1,0:T(8,128)(2,1)S(1)}, u32[]{:S(2)}, u32[]{:S(2)}) %collective-permute-start.16) | collective-permute-done | bytes 458784 | tf_op jit(solution)/shard_map/ppermute | solution.py:30
  34.2 5.2 %shard_map.115 = (bf16[448,512]{1,0:T(8,128)(2,1)S(1)}, bf16[576,256]{1,0:T(8,128)(2,1)S(1)}, f32[128,256]{1,0:T(8,128)S(1)}) custom-call(s32[2]{0:T(128)S(1)} %pad_add_fusion.1.place, s32[2,1]{1,0:T(2,128)S(1)} %pad_add_fusion.own_table, s32[2,1]{1,0:T(2,128)S(1)} %collective-permute-done.2.other_table, bf16[1,896,896]{2,1,0:T(8,128)(2,1)S(1)} %bitcast.9, ...), custom_call_target="tpu_custom_call" | custom-call | flops 2290089984 | bytes 9994240 | tf_op jit(solution)/shard_map/pallas_call | solution.py:41
  39.4 0.2 collective-permute-start.17
  39.6 2.0 %shard_map.117.other_flipped = bf16[1,896,896]{2,1,0:T(8,128)(2,1)S(1)} custom-call(bf16[1,896,896]{2,1,0:T(8,128)(2,1)} %collective-permute-done.5.other_tile.tile), custom_call_target="tpu_custom_call" | custom-call | bytes 3211264 | tf_op jit(solution)/shard_map/pallas_call | solution.py:41
  41.6 1.3 %shard_map.118 = (f32[2,448,256]{2,1,0:T(8,128)S(1)}, bf16[224,256]{1,0:T(8,128)(2,1)S(1)}, bf16[224,256]{1,0:T(8,128)(2,1)S(1)}, bf16[128,256]{1,0:T(8,128)(2,1)S(1)}) custom-call(s32[2]{0:T(128)S(1)} %pad_add_fusion.1.place, s32[2,1]{1,0:T(2,128)S(1)} %pad_add_fusion.own_table, s32[2,1]{1,0:T(2,128)S(1)} %collective-permute-done.2.other_table, ...), custom_call_target="tpu_custom_call" | custom-call | flops 411041792 | bytes 5144576 | tf_op jit(solution)/shard_map/pallas_call | solution.py:41
  42.9 2.6 %collective-permute-start.32 = (bf16[128,256]{1,0:T(8,128)(2,1)S(1)}, bf16[128,256]{1,0:T(8,128)(2,1)S(1)}, u32[]{:S(2)}, u32[]{:S(2)}) collective-permute-start(bf16[128,256]{1,0:T(8,128)(2,1)S(1)} %get-tuple-element.76), channel_id=1, source_target_pairs={{0,8},{1,9},{2,10},{3,11},{4,12},{5,13},{6,14},{7,15},{8,0},{9,1},... | collective-permute-start | bytes 196616 | tf_op jit(solution)/shard_map/ppermute | solution.py:36
  45.5 0.7 collective-permute-start.18
  46.3 1.3 %collective-permute-start.22 = (bf16[224,256]{1,0:T(8,128)(2,1)S(1)}, bf16[224,256]{1,0:T(8,128)(2,1)S(1)}, u32[]{:S(2)}, u32[]{:S(2)}) collective-permute-start(bf16[224,256]{1,0:T(8,128)(2,1)S(1)} %get-tuple-element.66), channel_id=1, source_target_pairs={{0,2},{4,0},{8,4},{12,8},{14,12},{10,14},{6,10},{2,6},{1,3},{5,1},... | collective-permute-start | bytes 344072 | tf_op jit(solution)/shard_map/ppermute | solution.py:26
  47.6 1.1 %shard_map.119 = (f32[448,256]{1,0:T(8,128)S(1)}, bf16[224,256]{1,0:T(8,128)(2,1)S(1)}, bf16[224,256]{1,0:T(8,128)(2,1)S(1)}, bf16[224,256]{1,0:T(8,128)(2,1)S(1...) custom-call(s32[2]{0:T(128)S(1)} %pad_add_fusion.1.place, ...), custom_call_target="tpu_custom_call" | custom-call | bytes 2752512 | tf_op jit(solution)/shard_map/pallas_call | solution.py:41
  48.7 1.2 %collective-permute-done.32 = bf16[128,256]{1,0:T(8,128)(2,1)S(1)} collective-permute-done((bf16[128,256]{1,0:T(8,128)(2,1)S(1)}, bf16[128,256]{1,0:T(8,128)(2,1)S(1)}, u32[]{:S(2)}, u32[]{:S(2)}) %collective-permute-start.32) | collective-permute-done | bytes 65568 | tf_op jit(solution)/shard_map/ppermute | solution.py:36
  49.9 1.4 %collective-permute-done.22 = bf16[224,256]{1,0:T(8,128)(2,1)S(1)} collective-permute-done((bf16[224,256]{1,0:T(8,128)(2,1)S(1)}, bf16[224,256]{1,0:T(8,128)(2,1)S(1)}, u32[]{:S(2)}, u32[]{:S(2)}) %collective-permute-start.22) | collective-permute-done | bytes 114720 | tf_op jit(solution)/shard_map/ppermute | solution.py:26
  51.4 1.1 %collective-permute-start.29 = (bf16[224,256]{1,0:T(8,128)(2,1)S(1)}, bf16[224,256]{1,0:T(8,128)(2,1)S(1)}, u32[]{:S(2)}, u32[]{:S(2)}) collective-permute-start(bf16[224,256]{1,0:T(8,128)(2,1)S(1)} %add_convert_fusion.2), channel_id=1, source_target_pairs={{0,2},{4,0},{8,4},{12,8},{14,12},{10,14},{6,10},{2,6},{1,3},{5,1},... | collective-permute-start | bytes 344072 | tf_op jit(solution)/shard_map/ppermute | solution.py:26
  52.5 1.1 %collective-permute-start.19 = (bf16[224,256]{1,0:T(8,128)(2,1)S(1)}, bf16[224,256]{1,0:T(8,128)(2,1)S(1)}, u32[]{:S(2)}, u32[]{:S(2)}) collective-permute-start(bf16[224,256]{1,0:T(8,128)(2,1)S(1)} %add_convert_fusion.9), channel_id=1, source_target_pairs={{0,4},{4,8},{8,12},{12,14},{14,10},{10,6},{6,2},{2,0},{1,5},{5,9},... | collective-permute-start | bytes 344072 | tf_op jit(solution)/shard_map/ppermute | solution.py:26
  53.5 1.3 %collective-permute-start.23 = (bf16[224,256]{1,0:T(8,128)(2,1)S(1)}, bf16[224,256]{1,0:T(8,128)(2,1)S(1)}, u32[]{:S(2)}, u32[]{:S(2)}) collective-permute-start(bf16[224,256]{1,0:T(8,128)(2,1)S(1)} %get-tuple-element.67), channel_id=1, source_target_pairs={{0,4},{4,8},{8,12},{12,14},{14,10},{10,6},{6,2},{2,0},{1,5},{5,9},... | collective-permute-start | bytes 344072 | tf_op jit(solution)/shard_map/ppermute | solution.py:26
  54.8 0.7 collective-permute-start.26
  55.6 0.6 collective-permute-done.29
  56.3 1.7 %collective-permute-start.30 = (bf16[224,256]{1,0:T(8,128)(2,1)S(1)}, bf16[224,256]{1,0:T(8,128)(2,1)S(1)}, u32[]{:S(2)}, u32[]{:S(2)}) collective-permute-start(bf16[224,256]{1,0:T(8,128)(2,1)S(1)} %add_convert_fusion.1), channel_id=1, source_target_pairs={{0,2},{4,0},{8,4},{12,8},{14,12},{10,14},{6,10},{2,6},{1,3},{5,1},... | collective-permute-start | bytes 344072 | tf_op jit(solution)/shard_map/ppermute | solution.py:26
  58.0 1.2 %collective-permute-start.20 = (bf16[224,256]{1,0:T(8,128)(2,1)S(1)}, bf16[224,256]{1,0:T(8,128)(2,1)S(1)}, u32[]{:S(2)}, u32[]{:S(2)}) collective-permute-start(bf16[224,256]{1,0:T(8,128)(2,1)S(1)} %add_convert_fusion.8), channel_id=1, source_target_pairs={{0,4},{4,8},{8,12},{12,14},{14,10},{10,6},{6,2},{2,0},{1,5},{5,9},... | collective-permute-start | bytes 344072 | tf_op jit(solution)/shard_map/ppermute | solution.py:26
  59.2 1.5 %collective-permute-start.33 = (bf16[128,256]{1,0:T(8,128)(2,1)S(1)}, bf16[128,256]{1,0:T(8,128)(2,1)S(1)}, u32[]{:S(2)}, u32[]{:S(2)}) collective-permute-start(bf16[128,256]{1,0:T(8,128)(2,1)S(1)} %add_convert_fusion.11), channel_id=1, source_target_pairs={{0,4},{1,5},{2,6},{3,7},{4,0},{5,1},{6,2},{7,3},{8,12},{9,13},{10,... | collective-permute-start | bytes 196616 | tf_op jit(solution)/shard_map/ppermute | solution.py:36
  60.8 0.7 collective-permute-start.24
  61.5 1.4 %collective-permute-start.27 = (bf16[224,256]{1,0:T(8,128)(2,1)S(1)}, bf16[224,256]{1,0:T(8,128)(2,1)S(1)}, u32[]{:S(2)}, u32[]{:S(2)}) collective-permute-start(bf16[224,256]{1,0:T(8,128)(2,1)S(1)} %add_convert_fusion.4), channel_id=1, source_target_pairs={{0,2},{4,0},{8,4},{12,8},{14,12},{10,14},{6,10},{2,6},{1,3},{5,1},... | collective-permute-start | bytes 344072 | tf_op jit(solution)/shard_map/ppermute | solution.py:26
  62.9 1.3 %collective-permute-done.33 = bf16[128,256]{1,0:T(8,128)(2,1)S(1)} collective-permute-done((bf16[128,256]{1,0:T(8,128)(2,1)S(1)}, bf16[128,256]{1,0:T(8,128)(2,1)S(1)}, u32[]{:S(2)}, u32[]{:S(2)}) %collective-permute-start.33) | collective-permute-done | bytes 65568 | tf_op jit(solution)/shard_map/ppermute | solution.py:36
  64.3 1.4 %collective-permute-start.31 = (bf16[224,256]{1,0:T(8,128)(2,1)S(1)}, bf16[224,256]{1,0:T(8,128)(2,1)S(1)}, u32[]{:S(2)}, u32[]{:S(2)}) collective-permute-start(bf16[224,256]{1,0:T(8,128)(2,1)S(1)} %add_convert_fusion), channel_id=1, source_target_pairs={{0,2},{4,0},{8,4},{12,8},{14,12},{10,14},{6,10},{2,6},{1,3},{5,1},... | collective-permute-start | bytes 344072 | tf_op jit(solution)/shard_map/ppermute | solution.py:26
  65.8 0.1 collective-permute-start.36
  65.9 0.6 collective-permute-start.35
  66.4 1.6 %collective-permute-start.21 = (bf16[224,256]{1,0:T(8,128)(2,1)S(1)}, bf16[224,256]{1,0:T(8,128)(2,1)S(1)}, u32[]{:S(2)}, u32[]{:S(2)}) collective-permute-start(bf16[224,256]{1,0:T(8,128)(2,1)S(1)} %add_convert_fusion.7), channel_id=1, source_target_pairs={{0,4},{4,8},{8,12},{12,14},{14,10},{10,6},{6,2},{2,0},{1,5},{5,9},... | collective-permute-start | bytes 344072 | tf_op jit(solution)/shard_map/ppermute | solution.py:26
  68.1 0.6 collective-permute-start.25
  68.8 0.8 collective-permute-done.36.other_swapped
  69.5 1.2 %collective-permute-start.28 = (bf16[224,256]{1,0:T(8,128)(2,1)S(1)}, bf16[224,256]{1,0:T(8,128)(2,1)S(1)}, u32[]{:S(2)}, u32[]{:S(2)}) collective-permute-start(bf16[224,256]{1,0:T(8,128)(2,1)S(1)} %add_convert_fusion.3), channel_id=1, source_target_pairs={{0,2},{4,0},{8,4},{12,8},{14,12},{10,14},{6,10},{2,6},{1,3},{5,1},... | collective-permute-start | bytes 344072 | tf_op jit(solution)/shard_map/ppermute | solution.py:26
  70.7 0.9 %collective-permute-start.34 = (bf16[128,256]{1,0:T(8,128)(2,1)S(1)}, bf16[128,256]{1,0:T(8,128)(2,1)S(1)}, u32[]{:S(2)}, u32[]{:S(2)}) collective-permute-start(bf16[128,256]{1,0:T(8,128)(2,1)S(1)} %add_convert_fusion.10.own_part), channel_id=1, source_target_pairs={{0,2},{1,3},{2,0},{3,1},{4,6},{5,7},{6,4},{7,5},{8,10},{9,11},{10,... | collective-permute-start | bytes 196616 | tf_op jit(solution)/shard_map/ppermute | solution.py:36
  71.6 1.8 %shard_map.116 = bf16[448,256]{1,0:T(8,128)(2,1)} custom-call(bf16[8,448,256]{2,1,0:T(8,128)(2,1)S(1)} %get-tuple-element.48.mask, bf16[448,512]{1,0:T(8,128)(2,1)S(1)} %get-tuple-element.53.hidden, bf16[8,512,256]{2,1,0:T(8,128)(2,1)S(1)} %copy-done, bf16[224,256]{1,0:T(8,128)(2,1)S(1)} %get-tuple-element.82.refs_0_.feats_first, ...), custom_call_target="tpu_custom_call" | custom-call | bytes 4849664 | tf_op jit(solution)/shard_map/pallas_call | solution.py:41
  73.5 2.4 %collective-permute-done.34.own_swapped = bf16[128,256]{1,0:T(8,128)(2,1)S(1)} collective-permute-done((bf16[128,256]{1,0:T(8,128)(2,1)S(1)}, bf16[128,256]{1,0:T(8,128)(2,1)S(1)}, u32[]{:S(2)}, u32[]{:S(2)}) %collective-permute-start.34) | collective-permute-done | bytes 65568 | tf_op jit(solution)/shard_map/ppermute | solution.py:36
  75.9 1.6 %shard_map.120 = (bf16[448,256]{1,0:T(8,128)(2,1)}, f32[256,256]{1,0:T(8,128)}) custom-call(s32[2]{0:T(128)S(1)} %pad_add_fusion.1.place, f32[448,256]{1,0:T(8,128)S(1)} %get-tuple-element.59.own, bf16[224,256]{1,0:T(8,128)(2,1)S(1)} %collective-permute-done.21.up_first, bf16[224,256]{1,0:T(8,128)(2,1)S(1)} %collective-permute-done.25.up_second, ...), custom_call_target="tpu_custom_call" | custom-call | bytes 2031616 | tf_op jit(solution)/shard_map/pallas_call | solution.py:41
  (52 shorter events, 0.4 us)
Async XLA Ops:
  1.6 32.6 %collective-permute-start.5 = (bf16[1,896,896]{2,1,0:T(8,128)(2,1)}, bf16[1,896,896]{2,1,0:T(8,128)(2,1)}, u32[]{:S(2)}, u32[]{:S(2)}) collective-permute-start(bf16[1,896,896]{2,1,0:T(8,128)(2,1)} %bitcast.7), channel_id=1, source_target_pairs={{0,1},{1,0},{2,3},{3,2},{4,5},{5,4},{6,7},{7,6},{8,9},{9,8},{10,11... | collective-permute-start | bytes 4816904 | tf_op jit(solution)/shard_map/ppermute | solution.py:30
  2.1 9.4 %collective-permute-start.1 = (bf16[224,256]{1,0:T(8,128)(2,1)S(1)}, bf16[224,256]{1,0:T(8,128)(2,1)S(1)}, u32[]{:S(2)}, u32[]{:S(2)}) collective-permute-start(bf16[224,256]{1,0:T(8,128)(2,1)S(1)} %get-tuple-element.81.refs_1_.feats_second), channel_id=1, source_target_pairs={{0,2},{4,0},{8,4},{12,8},{14,12},{10,14},{6,10},{2,6},{1,3},{5,1},... | collective-permute-start | bytes 344072 | tf_op jit(solution)/shard_map/ppermute | solution.py:26
  4.7 6.8 %collective-permute-start = (bf16[224,256]{1,0:T(8,128)(2,1)S(1)}, bf16[224,256]{1,0:T(8,128)(2,1)S(1)}, u32[]{:S(2)}, u32[]{:S(2)}) collective-permute-start(bf16[224,256]{1,0:T(8,128)(2,1)S(1)} %get-tuple-element.82.refs_0_.feats_first), channel_id=1, source_target_pairs={{0,4},{4,8},{8,12},{12,14},{14,10},{10,6},{6,2},{2,0},{1,5},{5,9},... | collective-permute-start | bytes 344072 | tf_op jit(solution)/shard_map/ppermute | solution.py:26
  4.9 10.9 %collective-permute-start.6 = (bf16[224,256]{1,0:T(8,128)(2,1)S(1)}, bf16[224,256]{1,0:T(8,128)(2,1)S(1)}, u32[]{:S(2)}, u32[]{:S(2)}) collective-permute-start(bf16[224,256]{1,0:T(8,128)(2,1)S(1)} %get-tuple-element.81.refs_1_.feats_second), channel_id=1, source_target_pairs={{0,4},{4,8},{8,12},{12,14},{14,10},{10,6},{6,2},{2,0},{1,5},{5,9},... | collective-permute-start | bytes 344072 | tf_op jit(solution)/shard_map/ppermute | solution.py:26
  8.1 5.5 %copy-start = (bf16[8,512,256]{2,1,0:T(8,128)(2,1)S(1)}, bf16[8,512,256]{2,1,0:T(8,128)(2,1)}, u32[]{:S(2)}) copy-start(bf16[8,512,256]{2,1,0:T(8,128)(2,1)} %down.3) | copy-start | bytes 6291460
  8.1 3.3 %collective-permute-start.2 = (s32[2,1]{1,0:T(2,128)S(1)}, s32[2,1]{1,0:T(2,128)S(1)}, u32[]{:S(2)}, u32[]{:S(2)}) collective-permute-start(s32[2,1]{1,0:T(2,128)S(1)} %pad_add_fusion.own_table), channel_id=1, source_target_pairs={{0,1},{1,0},{2,3},{3,2},{4,5},{5,4},{6,7},{7,6},{8,9},{9,8},{10,11... | collective-permute-start | bytes 32 | tf_op jit(solution)/shard_map/ppermute | solution.py:30
  8.2 1.6 %copy-start.1 = (bf16[1,1,1,896,896]{4,3,2,1,0:T(8,128)(2,1)S(1)}, bf16[1,1,1,896,896]{4,3,2,1,0:T(8,128)(2,1)}, u32[]{:S(2)}) copy-start(bf16[1,1,1,896,896]{4,3,2,1,0:T(8,128)(2,1)} %param.11) | copy-start | bytes 4816900
  9.8 3.9 %copy-start.6 = (bf16[448,256]{1,0:T(8,128)(2,1)S(1)}, bf16[448,256]{1,0:T(8,128)(2,1)}, u32[]{:S(2)}) copy-start(bf16[448,256]{1,0:T(8,128)(2,1)} %out_grad.2) | copy-start | bytes 688132
  9.8 3.9 %copy-start.8 = (s32[896]{0:T(1024)S(1)}, s32[896]{0:T(1024)}, u32[]{:S(2)}) copy-start(s32[896]{0:T(1024)} %types.1) | copy-start | bytes 10756
  10.2 1.2 %copy-start.3 = (bf16[1,896,896]{2,1,0:T(8,128)(2,1)}, bf16[1,896,896]{2,1,0:T(8,128)(2,1)S(1)}, u32[]{:S(2)}) copy-start(bf16[1,896,896]{2,1,0:T(8,128)(2,1)S(1)} %shard_map.112.own_flipped) | copy-start | bytes 4816900
  11.4 6.4 %collective-permute-start.7 = (bf16[224,256]{1,0:T(8,128)(2,1)S(1)}, bf16[224,256]{1,0:T(8,128)(2,1)S(1)}, u32[]{:S(2)}, u32[]{:S(2)}) collective-permute-start(bf16[224,256]{1,0:T(8,128)(2,1)S(1)} %get-tuple-element.82.refs_0_.feats_first), channel_id=1, source_target_pairs={{0,2},{4,0},{8,4},{12,8},{14,12},{10,14},{6,10},{2,6},{1,3},{5,1},... | collective-permute-start | bytes 344072 | tf_op jit(solution)/shard_map/ppermute | solution.py:26
  11.5 6.3 %collective-permute-start.3 = (bf16[224,256]{1,0:T(8,128)(2,1)S(1)}, bf16[224,256]{1,0:T(8,128)(2,1)S(1)}, u32[]{:S(2)}, u32[]{:S(2)}) collective-permute-start(bf16[224,256]{1,0:T(8,128)(2,1)S(1)} %collective-permute-done.refs_2_), channel_id=1, source_target_pairs={{0,4},{4,8},{8,12},{12,14},{14,10},{10,6},{6,2},{2,0},{1,5},{5,9},... | collective-permute-start | bytes 344072 | tf_op jit(solution)/shard_map/ppermute | solution.py:26
  13.4 5.8 %collective-permute-start.4 = (bf16[224,256]{1,0:T(8,128)(2,1)S(1)}, bf16[224,256]{1,0:T(8,128)(2,1)S(1)}, u32[]{:S(2)}, u32[]{:S(2)}) collective-permute-start(bf16[224,256]{1,0:T(8,128)(2,1)S(1)} %collective-permute-done.1.refs_5_), channel_id=1, source_target_pairs={{0,2},{4,0},{8,4},{12,8},{14,12},{10,14},{6,10},{2,6},{1,3},{5,1},... | collective-permute-start | bytes 344072 | tf_op jit(solution)/shard_map/ppermute | solution.py:26
  13.6 20.6 %copy-start.5 = (bf16[8,256,512]{2,1,0:T(8,128)(2,1)S(1)}, bf16[8,256,512]{2,1,0:T(8,128)(2,1)}, u32[]{:S(2)}) copy-start(bf16[8,256,512]{2,1,0:T(8,128)(2,1)} %up.1) | copy-start | bytes 6291460
  15.7 18.5 %copy-start.2 = (bf16[1,1,1,896,896]{4,3,2,1,0:T(8,128)(2,1)S(1)}, bf16[1,1,1,896,896]{4,3,2,1,0:T(8,128)(2,1)}, u32[]{:S(2)}) copy-start(bf16[1,1,1,896,896]{4,3,2,1,0:T(8,128)(2,1)} %param.11) | copy-start | bytes 4816900
  15.7 18.5 %copy-start.7 = (bf16[256,256]{1,0:T(8,128)(2,1)S(1)}, bf16[256,256]{1,0:T(8,128)(2,1)}, u32[]{:S(2)}) copy-start(bf16[256,256]{1,0:T(8,128)(2,1)} %weight.3) | copy-start | bytes 393220
  15.8 5.5 %collective-permute-start.8 = (bf16[224,256]{1,0:T(8,128)(2,1)S(1)}, bf16[224,256]{1,0:T(8,128)(2,1)S(1)}, u32[]{:S(2)}, u32[]{:S(2)}) collective-permute-start(bf16[224,256]{1,0:T(8,128)(2,1)S(1)} %collective-permute-done.6.refs_3_), channel_id=1, source_target_pairs={{0,4},{4,8},{8,12},{12,14},{14,10},{10,6},{6,2},{2,0},{1,5},{5,9},... | collective-permute-start | bytes 344072 | tf_op jit(solution)/shard_map/ppermute | solution.py:26
  17.8 5.1 %collective-permute-start.9 = (bf16[224,256]{1,0:T(8,128)(2,1)S(1)}, bf16[224,256]{1,0:T(8,128)(2,1)S(1)}, u32[]{:S(2)}, u32[]{:S(2)}) collective-permute-start(bf16[224,256]{1,0:T(8,128)(2,1)S(1)} %collective-permute-done.7.refs_4_), channel_id=1, source_target_pairs={{0,2},{4,0},{8,4},{12,8},{14,12},{10,14},{6,10},{2,6},{1,3},{5,1},... | collective-permute-start | bytes 344072 | tf_op jit(solution)/shard_map/ppermute | solution.py:26
  19.3 6.0 %collective-permute-start.10 = (bf16[224,256]{1,0:T(8,128)(2,1)S(1)}, bf16[224,256]{1,0:T(8,128)(2,1)S(1)}, u32[]{:S(2)}, u32[]{:S(2)}) collective-permute-start(bf16[224,256]{1,0:T(8,128)(2,1)S(1)} %collective-permute-done.3.refs_6_), channel_id=1, source_target_pairs={{0,4},{4,8},{8,12},{12,14},{14,10},{10,6},{6,2},{2,0},{1,5},{5,9},... | collective-permute-start | bytes 344072 | tf_op jit(solution)/shard_map/ppermute | solution.py:26
  20.8 6.0 %collective-permute-start.13 = (bf16[224,256]{1,0:T(8,128)(2,1)S(1)}, bf16[224,256]{1,0:T(8,128)(2,1)S(1)}, u32[]{:S(2)}, u32[]{:S(2)}) collective-permute-start(bf16[224,256]{1,0:T(8,128)(2,1)S(1)} %collective-permute-done.4.refs_9_), channel_id=1, source_target_pairs={{0,2},{4,0},{8,4},{12,8},{14,12},{10,14},{6,10},{2,6},{1,3},{5,1},... | collective-permute-start | bytes 344072 | tf_op jit(solution)/shard_map/ppermute | solution.py:26
  21.3 6.4 %collective-permute-start.11 = (bf16[224,256]{1,0:T(8,128)(2,1)S(1)}, bf16[224,256]{1,0:T(8,128)(2,1)S(1)}, u32[]{:S(2)}, u32[]{:S(2)}) collective-permute-start(bf16[224,256]{1,0:T(8,128)(2,1)S(1)} %collective-permute-done.8.refs_7_), channel_id=1, source_target_pairs={{0,4},{4,8},{8,12},{12,14},{14,10},{10,6},{6,2},{2,0},{1,5},{5,9},... | collective-permute-start | bytes 344072 | tf_op jit(solution)/shard_map/ppermute | solution.py:26
  22.9 6.1 %collective-permute-start.12 = (bf16[224,256]{1,0:T(8,128)(2,1)S(1)}, bf16[224,256]{1,0:T(8,128)(2,1)S(1)}, u32[]{:S(2)}, u32[]{:S(2)}) collective-permute-start(bf16[224,256]{1,0:T(8,128)(2,1)S(1)} %collective-permute-done.9.refs_8_), channel_id=1, source_target_pairs={{0,2},{4,0},{8,4},{12,8},{14,12},{10,14},{6,10},{2,6},{1,3},{5,1},... | collective-permute-start | bytes 344072 | tf_op jit(solution)/shard_map/ppermute | solution.py:26
  25.2 4.8 %collective-permute-start.14 = (bf16[224,256]{1,0:T(8,128)(2,1)S(1)}, bf16[224,256]{1,0:T(8,128)(2,1)S(1)}, u32[]{:S(2)}, u32[]{:S(2)}) collective-permute-start(bf16[224,256]{1,0:T(8,128)(2,1)S(1)} %collective-permute-done.10.refs_10_), channel_id=1, source_target_pairs={{0,4},{4,8},{8,12},{12,14},{14,10},{10,6},{6,2},{2,0},{1,5},{5,9},... | collective-permute-start | bytes 344072 | tf_op jit(solution)/shard_map/ppermute | solution.py:26
  26.8 4.8 %collective-permute-start.15 = (bf16[224,256]{1,0:T(8,128)(2,1)S(1)}, bf16[224,256]{1,0:T(8,128)(2,1)S(1)}, u32[]{:S(2)}, u32[]{:S(2)}) collective-permute-start(bf16[224,256]{1,0:T(8,128)(2,1)S(1)} %collective-permute-done.13.refs_13_), channel_id=1, source_target_pairs={{0,2},{4,0},{8,4},{12,8},{14,12},{10,14},{6,10},{2,6},{1,3},{5,1},... | collective-permute-start | bytes 344072 | tf_op jit(solution)/shard_map/ppermute | solution.py:26
  32.3 1.9 %collective-permute-start.16 = (bf16[2,448,256]{2,1,0:T(8,128)(2,1)S(1)}, bf16[2,448,256]{2,1,0:T(8,128)(2,1)S(1)}, u32[]{:S(2)}, u32[]{:S(2)}) collective-permute-start(bf16[2,448,256]{2,1,0:T(8,128)(2,1)S(1)} %shard_map.114.own_rows), channel_id=1, source_target_pairs={{0,1},{1,0},{2,3},{3,2},{4,5},{5,4},{6,7},{7,6},{8,9},{9,8},{10,11... | collective-permute-start | bytes 1376264 | tf_op jit(solution)/shard_map/ppermute | solution.py:30
  39.4 2.2 %copy-start.4 = (bf16[1,896,896]{2,1,0:T(8,128)(2,1)S(1)}, bf16[1,896,896]{2,1,0:T(8,128)(2,1)}, u32[]{:S(2)}) copy-start(bf16[1,896,896]{2,1,0:T(8,128)(2,1)} %copy-done.3) | copy-start | bytes 4816900
  39.4 2.2 %collective-permute-start.17 = (bf16[576,256]{1,0:T(8,128)(2,1)S(1)}, bf16[576,256]{1,0:T(8,128)(2,1)S(1)}, u32[]{:S(2)}, u32[]{:S(2)}) collective-permute-start(bf16[576,256]{1,0:T(8,128)(2,1)S(1)} %get-tuple-element.56.own_packed), channel_id=1, source_target_pairs={{0,1},{1,0},{2,3},{3,2},{4,5},{5,4},{6,7},{7,6},{8,9},{9,8},{10,11... | collective-permute-start | bytes 884744 | tf_op jit(solution)/shard_map/ppermute | solution.py:30
  42.9 7.0 %collective-permute-start.32 = (bf16[128,256]{1,0:T(8,128)(2,1)S(1)}, bf16[128,256]{1,0:T(8,128)(2,1)S(1)}, u32[]{:S(2)}, u32[]{:S(2)}) collective-permute-start(bf16[128,256]{1,0:T(8,128)(2,1)S(1)} %get-tuple-element.76), channel_id=1, source_target_pairs={{0,8},{1,9},{2,10},{3,11},{4,12},{5,13},{6,14},{7,15},{8,0},{9,1},... | collective-permute-start | bytes 196616 | tf_op jit(solution)/shard_map/ppermute | solution.py:36
  45.5 6.9 %collective-permute-start.18 = (bf16[224,256]{1,0:T(8,128)(2,1)S(1)}, bf16[224,256]{1,0:T(8,128)(2,1)S(1)}, u32[]{:S(2)}, u32[]{:S(2)}) collective-permute-start(bf16[224,256]{1,0:T(8,128)(2,1)S(1)} %get-tuple-element.60), channel_id=1, source_target_pairs={{0,4},{4,8},{8,12},{12,14},{14,10},{10,6},{6,2},{2,0},{1,5},{5,9},... | collective-permute-start | bytes 344072 | tf_op jit(solution)/shard_map/ppermute | solution.py:26
  46.3 5.1 %collective-permute-start.22 = (bf16[224,256]{1,0:T(8,128)(2,1)S(1)}, bf16[224,256]{1,0:T(8,128)(2,1)S(1)}, u32[]{:S(2)}, u32[]{:S(2)}) collective-permute-start(bf16[224,256]{1,0:T(8,128)(2,1)S(1)} %get-tuple-element.66), channel_id=1, source_target_pairs={{0,2},{4,0},{8,4},{12,8},{14,12},{10,14},{6,10},{2,6},{1,3},{5,1},... | collective-permute-start | bytes 344072 | tf_op jit(solution)/shard_map/ppermute | solution.py:26
  51.4 4.8 %collective-permute-start.29 = (bf16[224,256]{1,0:T(8,128)(2,1)S(1)}, bf16[224,256]{1,0:T(8,128)(2,1)S(1)}, u32[]{:S(2)}, u32[]{:S(2)}) collective-permute-start(bf16[224,256]{1,0:T(8,128)(2,1)S(1)} %add_convert_fusion.2), channel_id=1, source_target_pairs={{0,2},{4,0},{8,4},{12,8},{14,12},{10,14},{6,10},{2,6},{1,3},{5,1},... | collective-permute-start | bytes 344072 | tf_op jit(solution)/shard_map/ppermute | solution.py:26
  52.5 5.4 %collective-permute-start.19 = (bf16[224,256]{1,0:T(8,128)(2,1)S(1)}, bf16[224,256]{1,0:T(8,128)(2,1)S(1)}, u32[]{:S(2)}, u32[]{:S(2)}) collective-permute-start(bf16[224,256]{1,0:T(8,128)(2,1)S(1)} %add_convert_fusion.9), channel_id=1, source_target_pairs={{0,4},{4,8},{8,12},{12,14},{14,10},{10,6},{6,2},{2,0},{1,5},{5,9},... | collective-permute-start | bytes 344072 | tf_op jit(solution)/shard_map/ppermute | solution.py:26
  53.5 7.2 %collective-permute-start.23 = (bf16[224,256]{1,0:T(8,128)(2,1)S(1)}, bf16[224,256]{1,0:T(8,128)(2,1)S(1)}, u32[]{:S(2)}, u32[]{:S(2)}) collective-permute-start(bf16[224,256]{1,0:T(8,128)(2,1)S(1)} %get-tuple-element.67), channel_id=1, source_target_pairs={{0,4},{4,8},{8,12},{12,14},{14,10},{10,6},{6,2},{2,0},{1,5},{5,9},... | collective-permute-start | bytes 344072 | tf_op jit(solution)/shard_map/ppermute | solution.py:26
  54.8 6.6 %collective-permute-start.26 = (bf16[224,256]{1,0:T(8,128)(2,1)S(1)}, bf16[224,256]{1,0:T(8,128)(2,1)S(1)}, u32[]{:S(2)}, u32[]{:S(2)}) collective-permute-start(bf16[224,256]{1,0:T(8,128)(2,1)S(1)} %get-tuple-element.70), channel_id=1, source_target_pairs={{0,2},{4,0},{8,4},{12,8},{14,12},{10,14},{6,10},{2,6},{1,3},{5,1},... | collective-permute-start | bytes 344072 | tf_op jit(solution)/shard_map/ppermute | solution.py:26
  56.3 8.0 %collective-permute-start.30 = (bf16[224,256]{1,0:T(8,128)(2,1)S(1)}, bf16[224,256]{1,0:T(8,128)(2,1)S(1)}, u32[]{:S(2)}, u32[]{:S(2)}) collective-permute-start(bf16[224,256]{1,0:T(8,128)(2,1)S(1)} %add_convert_fusion.1), channel_id=1, source_target_pairs={{0,2},{4,0},{8,4},{12,8},{14,12},{10,14},{6,10},{2,6},{1,3},{5,1},... | collective-permute-start | bytes 344072 | tf_op jit(solution)/shard_map/ppermute | solution.py:26
  58.0 7.8 %collective-permute-start.20 = (bf16[224,256]{1,0:T(8,128)(2,1)S(1)}, bf16[224,256]{1,0:T(8,128)(2,1)S(1)}, u32[]{:S(2)}, u32[]{:S(2)}) collective-permute-start(bf16[224,256]{1,0:T(8,128)(2,1)S(1)} %add_convert_fusion.8), channel_id=1, source_target_pairs={{0,4},{4,8},{8,12},{12,14},{14,10},{10,6},{6,2},{2,0},{1,5},{5,9},... | collective-permute-start | bytes 344072 | tf_op jit(solution)/shard_map/ppermute | solution.py:26
  59.2 5.0 %collective-permute-start.33 = (bf16[128,256]{1,0:T(8,128)(2,1)S(1)}, bf16[128,256]{1,0:T(8,128)(2,1)S(1)}, u32[]{:S(2)}, u32[]{:S(2)}) collective-permute-start(bf16[128,256]{1,0:T(8,128)(2,1)S(1)} %add_convert_fusion.11), channel_id=1, source_target_pairs={{0,4},{1,5},{2,6},{3,7},{4,0},{5,1},{6,2},{7,3},{8,12},{9,13},{10,... | collective-permute-start | bytes 196616 | tf_op jit(solution)/shard_map/ppermute | solution.py:36
  60.8 5.7 %collective-permute-start.24 = (bf16[224,256]{1,0:T(8,128)(2,1)S(1)}, bf16[224,256]{1,0:T(8,128)(2,1)S(1)}, u32[]{:S(2)}, u32[]{:S(2)}) collective-permute-start(bf16[224,256]{1,0:T(8,128)(2,1)S(1)} %add_convert_fusion.6), channel_id=1, source_target_pairs={{0,4},{4,8},{8,12},{12,14},{14,10},{10,6},{6,2},{2,0},{1,5},{5,9},... | collective-permute-start | bytes 344072 | tf_op jit(solution)/shard_map/ppermute | solution.py:26
  61.5 6.6 %collective-permute-start.27 = (bf16[224,256]{1,0:T(8,128)(2,1)S(1)}, bf16[224,256]{1,0:T(8,128)(2,1)S(1)}, u32[]{:S(2)}, u32[]{:S(2)}) collective-permute-start(bf16[224,256]{1,0:T(8,128)(2,1)S(1)} %add_convert_fusion.4), channel_id=1, source_target_pairs={{0,2},{4,0},{8,4},{12,8},{14,12},{10,14},{6,10},{2,6},{1,3},{5,1},... | collective-permute-start | bytes 344072 | tf_op jit(solution)/shard_map/ppermute | solution.py:26
  64.3 11.6 %collective-permute-start.31 = (bf16[224,256]{1,0:T(8,128)(2,1)S(1)}, bf16[224,256]{1,0:T(8,128)(2,1)S(1)}, u32[]{:S(2)}, u32[]{:S(2)}) collective-permute-start(bf16[224,256]{1,0:T(8,128)(2,1)S(1)} %add_convert_fusion), channel_id=1, source_target_pairs={{0,2},{4,0},{8,4},{12,8},{14,12},{10,14},{6,10},{2,6},{1,3},{5,1},... | collective-permute-start | bytes 344072 | tf_op jit(solution)/shard_map/ppermute | solution.py:26
  65.8 3.8 %collective-permute-start.36 = (bf16[128,256]{1,0:T(8,128)(2,1)S(1)}, bf16[128,256]{1,0:T(8,128)(2,1)S(1)}, u32[]{:S(2)}, u32[]{:S(2)}) collective-permute-start(bf16[128,256]{1,0:T(8,128)(2,1)S(1)} %add_convert_fusion.10.own_part), channel_id=1, source_target_pairs={{0,3},{1,2},{2,1},{3,0},{4,7},{5,6},{6,5},{7,4},{8,11},{9,10},{10,... | collective-permute-start | bytes 196616 | tf_op jit(solution)/shard_map/ppermute | solution.py:36
  65.9 4.9 %collective-permute-start.35 = (bf16[128,256]{1,0:T(8,128)(2,1)S(1)}, bf16[128,256]{1,0:T(8,128)(2,1)S(1)}, u32[]{:S(2)}, u32[]{:S(2)}) collective-permute-start(bf16[128,256]{1,0:T(8,128)(2,1)S(1)} %add_convert_fusion.10.own_part), channel_id=1, source_target_pairs={{0,1},{1,0},{2,3},{3,2},{4,5},{5,4},{6,7},{7,6},{8,9},{9,8},{10,11... | collective-permute-start | bytes 196616 | tf_op jit(solution)/shard_map/ppermute | solution.py:30
  66.4 9.4 %collective-permute-start.21 = (bf16[224,256]{1,0:T(8,128)(2,1)S(1)}, bf16[224,256]{1,0:T(8,128)(2,1)S(1)}, u32[]{:S(2)}, u32[]{:S(2)}) collective-permute-start(bf16[224,256]{1,0:T(8,128)(2,1)S(1)} %add_convert_fusion.7), channel_id=1, source_target_pairs={{0,4},{4,8},{8,12},{12,14},{14,10},{10,6},{6,2},{2,0},{1,5},{5,9},... | collective-permute-start | bytes 344072 | tf_op jit(solution)/shard_map/ppermute | solution.py:26
  68.1 7.8 %collective-permute-start.25 = (bf16[224,256]{1,0:T(8,128)(2,1)S(1)}, bf16[224,256]{1,0:T(8,128)(2,1)S(1)}, u32[]{:S(2)}, u32[]{:S(2)}) collective-permute-start(bf16[224,256]{1,0:T(8,128)(2,1)S(1)} %add_convert_fusion.5), channel_id=1, source_target_pairs={{0,4},{4,8},{8,12},{12,14},{14,10},{10,6},{6,2},{2,0},{1,5},{5,9},... | collective-permute-start | bytes 344072 | tf_op jit(solution)/shard_map/ppermute | solution.py:26
  69.5 6.3 %collective-permute-start.28 = (bf16[224,256]{1,0:T(8,128)(2,1)S(1)}, bf16[224,256]{1,0:T(8,128)(2,1)S(1)}, u32[]{:S(2)}, u32[]{:S(2)}) collective-permute-start(bf16[224,256]{1,0:T(8,128)(2,1)S(1)} %add_convert_fusion.3), channel_id=1, source_target_pairs={{0,2},{4,0},{8,4},{12,8},{14,12},{10,14},{6,10},{2,6},{1,3},{5,1},... | collective-permute-start | bytes 344072 | tf_op jit(solution)/shard_map/ppermute | solution.py:26
  70.7 5.1 %collective-permute-start.34 = (bf16[128,256]{1,0:T(8,128)(2,1)S(1)}, bf16[128,256]{1,0:T(8,128)(2,1)S(1)}, u32[]{:S(2)}, u32[]{:S(2)}) collective-permute-start(bf16[128,256]{1,0:T(8,128)(2,1)S(1)} %add_convert_fusion.10.own_part), channel_id=1, source_target_pairs={{0,2},{1,3},{2,0},{3,1},{4,6},{5,7},{6,4},{7,5},{8,10},{9,11},{10,... | collective-permute-start | bytes 196616 | tf_op jit(solution)/shard_map/ppermute | solution.py:36

commit v3 on v2

--- a/solution.py
+++ b/solution.py
@@ -1,4 +1,5 @@
 import functools
+import math
 
 import jax
 import jax.numpy as jnp
@@ -11,7 +12,7 @@
 F32 = jnp.float32
 NT = (((1,), (1,)), ((), ()))
 TN = (((0,), (0,)), ((), ()))
-VMEM_LIMIT = 30 * 1024 * 1024
+SPARE_VMEM = 8 * 1024 * 1024
 
 
 def ring_order(size):
@@ -36,16 +37,18 @@
     return lax.ppermute(block, axes, route)
 
 
-def call(kernel, out_shape, smem, vmem, scratch=(), flops=0):
-    moved = sum(item.size * item.dtype.itemsize for item in (*vmem, *jax.tree.leaves(out_shape)))
+def call(kernel, out_shape, smem, vmem, scratch=(), flops=0, space=pltpu.VMEM):
+    held = (*vmem, *jax.tree.leaves(out_shape))
+    moved = sum(math.prod(item.shape) * item.dtype.itemsize for item in held)
+    spare = sum(math.prod(item.shape) * 4 for item in scratch) + SPARE_VMEM
     return pl.pallas_call(
         kernel,
         out_shape=out_shape,
         in_specs=[pl.BlockSpec(memory_space=pltpu.SMEM)] * len(smem)
-        + [pl.BlockSpec(memory_space=pltpu.VMEM)] * len(vmem),
+        + [pl.BlockSpec(memory_space=space)] * len(vmem),
         out_specs=jax.tree.map(lambda _: pl.BlockSpec(memory_space=pltpu.VMEM), out_shape),
         scratch_shapes=list(scratch),
-        compiler_params=pltpu.CompilerParams(vmem_limit_bytes=VMEM_LIMIT),
+        compiler_params=pltpu.CompilerParams(vmem_limit_bytes=moved + spare),
         cost_estimate=pl.CostEstimate(flops=flops, bytes_accessed=moved, transcendentals=0),
     )(*smem, *vmem)
 
@@ -182,11 +185,14 @@
     term = lax.dot_general(high, grad_scaled, TN, preferred_element_type=F32)
     upper, lower = term[: width // 2], term[width // 2 :]
     kept[...] = jnp.where(core == 0, upper, lower)
-    packed[half:] = jnp.where(core == 0, lower, upper).astype(BF16)
+    sent = jnp.where(core == 0, lower, upper)
+    packed[half : half + width // 2] = sent.astype(BF16)
+    packed[half + width // 2 :] = (sent - sent.astype(BF16).astype(F32)).astype(BF16)
 
 
 def product_kernel(
     size,
+    offsets,
     place,
     own_table,
     other_table,
@@ -199,47 +205,51 @@
     far_first,
     far_second,
     weight_part,
-    full_grad,
+    *rest,
 ):
+    terms, full_grad = rest[:-1], rest[-1]
     slots, half = own_flipped.shape[0], products.shape[1]
     core = place[0]
-    own_start = pl.multiple_of(core * half, half)
-    full_grad[pl.ds(own_start, half), :] = own_packed[:half]
+    own = pl.ds(pl.multiple_of(core * half, half), half)
+    full_grad[own, :] = own_packed[:half]
     full_grad[pl.ds(pl.multiple_of((1 - core) * half, half), half), :] = other_packed[:half]
-    weight_part[...] = (kept[...] + other_packed[half:].astype(F32)).astype(BF16)
-    chosen = distances(place, own_table, other_table, size)
-    total = jnp.zeros(products.shape[1:], F32)
+    middle = half + kept.shape[0]
+    weight_part[...] = (
+        kept[...] + other_packed[half:middle].astype(F32) + other_packed[middle:].astype(F32)
+    ).astype(BF16)
     for flipped, table, which in (
         (own_flipped, own_table, core),
         (other_flipped, other_table, 1 - core),
     ):
         for slot in range(slots):
-            product = table[1, slot].astype(F32) * jnp.dot(
-                flipped[slot, pl.ds(own_start, half), :],
-                full_grad[...],
-                preferred_element_type=F32,
+            products[which * slots + slot] = table[1, slot].astype(F32) * jnp.dot(
+                flipped[slot, own, :], full_grad[...], preferred_element_type=F32
             )
-            products[which * slots + slot] = product
-            distance = jnp.where(which == 0, chosen[slot], chosen[slots + slot])
-            total += jnp.where(distance == size // 2, product, 0.0)
+    chosen = distances(place, own_table, other_table, size)
+    total = gathered(chosen, products, size // 2)
     cut = far_first.shape[0]
     far_first[...] = total[:cut].astype(BF16)
     far_second[...] = total[cut:].astype(BF16)
+    for term, offset in zip(terms, offsets, strict=True):
+        term[...] = gathered(chosen, products, offset).astype(BF16)
+
+
+def gathered(chosen, products, offset):
+    total = jnp.where(chosen[0] == offset, products[0], 0.0)
+    for slot in range(1, products.shape[0]):
+        total += jnp.where(chosen[slot] == offset, products[slot], 0.0)
+    return total
 
 
 def spread_kernel(size, offsets, place, own_table, other_table, products, *terms):
     chosen = distances(place, own_table, other_table, size)
-    for term, (offset, start) in zip(terms, offsets, strict=True):
-        length = term.shape[0]
-        total = jnp.where(chosen[0] == offset, products[0, start : start + length], 0.0)
-        for slot in range(1, products.shape[0]):
-            total += jnp.where(chosen[slot] == offset, products[slot, start : start + length], 0.0)
-        term[...] = total.astype(term.dtype)
-
-
-def update_kernel(mask, hidden, down, feats_first, feats_second, updated):
+    for term, offset in zip(terms, offsets, strict=True):
+        term[...] = gathered(chosen, products, offset).astype(term.dtype)
+
+
+def update_kernel(mask, hidden, down, feats, updated):
     experts, inner, width = down.shape
-    total = jnp.concatenate([feats_first[...], feats_second[...]], axis=0).astype(F32)
+    total = feats[...].astype(F32)
     for expert in range(experts):
         masked = jnp.concatenate(
             [
@@ -255,10 +265,8 @@
 def finish_kernel(
     place,
     own,
-    up_first,
-    up_second,
-    down_first,
-    down_second,
+    up,
+    down,
     weight,
     out_grad,
     own_part,
@@ -268,16 +276,9 @@
     result,
     weight_grad,
 ):
-    cut = up_first.shape[0]
-    for start, pair in ((0, (up_first, down_first)), (cut, (up_second, down_second))):
-        length = pair[0].shape[0]
-        grad_msg = (
-            own[start : start + length] + pair[0][...].astype(F32) + pair[1][...].astype(F32)
-        ).astype(BF16)
-        back = lax.dot_general(grad_msg, weight[...], NT, preferred_element_type=F32)
-        result[start : start + length] = (
-            out_grad[start : start + length].astype(F32) + back
-        ).astype(BF16)
+    grad_msg = (own[...] + up[...].astype(F32) + down[...].astype(F32)).astype(BF16)
+    back = lax.dot_general(grad_msg, weight[...], NT, preferred_element_type=F32)
+    result[...] = (out_grad[...].astype(F32) + back).astype(BF16)
     half = own_part.shape[0]
     upper = own_part[...].astype(F32) + own_swapped[...].astype(F32)
     lower = other_part[...].astype(F32) + other_swapped[...].astype(F32)
@@ -299,48 +300,35 @@
     cut = half // 2
     experts, _, inner = expert_up.shape
 
-    first = lax.dynamic_slice_in_dim(feats, core * half, cut, 0)
-    second = lax.dynamic_slice_in_dim(feats, core * half + cut, half - cut, 0)
+    own_feats = lax.dynamic_slice_in_dim(feats, core * half, half, 0)
 
     place = jnp.stack([core, chip]).astype(jnp.int32)
-    tile_own, _ = lax.optimization_barrier((tiles[0, 0], first))
+    tile_own, _ = lax.optimization_barrier((tiles[0, 0], own_feats))
     own_table = jnp.stack([tile_step[0, 0], tile_count[0, 0]])
     other_table = other_core(own_table)
     tile_other = other_core(tile_own)
     flip = functools.partial(call, flip_kernel, struct(tile_own.shape, BF16), ())
 
-    arrived = [(0, 0, first), (0, cut, second)]
-    up_a = down_a = first
-    up_b = down_b = second
-    flipped_own = flip((tile_own,))
+    mask, grad_hidden = call(
+        prepare_kernel,
+        [struct((experts, half, width), BF16), struct((half, inner), F32)],
+        (place,),
+        (node_type, out_grad, expert_down),
+        (pltpu.VMEM((block, 8), F32),),
+        flops=2 * experts * half * width * inner,
+    )
+    arrived = [(0, 0, own_feats)]
+    up = down = own_feats
     for step in range(1, far):
         if step == 2:
-            grads_out, _, _ = lax.optimization_barrier((out_grad, up_a, down_b))
-            mask, grad_hidden = call(
-                prepare_kernel,
-                [struct((experts, half, width), BF16), struct((half, inner), F32)],
-                (place,),
-                (node_type, grads_out, expert_down),
-                (pltpu.VMEM((block, 8), F32),),
-            )
-            up_a, down_b, flipped_own, other_table = lax.optimization_barrier(
-                (up_a, down_b, flipped_own, other_table)
-            )
+            up, down, other_table = lax.optimization_barrier((up, down, other_table))
         if step == 3:
-            up_a, down_b, grad_hidden, mask = lax.optimization_barrier(
-                (up_a, down_b, grad_hidden, mask)
-            )
-        up_a = along_ring(up_a, order, 1)
-        down_b = along_ring(down_b, order, -1)
-        up_b = along_ring(up_b, order, 1)
-        down_a = along_ring(down_a, order, -1)
-        arrived += [(size - step, 0, up_a), (size - step, cut, up_b)]
-        arrived += [(step, 0, down_a), (step, cut, down_b)]
+            up, down, mask, grad_hidden = lax.optimization_barrier((up, down, mask, grad_hidden))
+        up, down = along_ring(up, order, 1), along_ring(down, order, -1)
+        arrived += [(size - step, 0, up), (step, 0, down)]
     tables = (place, own_table, other_table)
-    far_first, far_second = along_ring(up_a, order, 1), along_ring(down_b, order, -1)
-    arrived += [(far, 0, far_first), (far, cut, far_second)]
-    tile_late, _, _ = lax.optimization_barrier((tile_other, up_a, down_b))
-    flipped_other = flip((tile_late,))
+    arrived += [(far, 0, along_ring(up[:cut], order, 1))]
+    arrived += [(far, cut, along_ring(down[cut:], order, -1))]
     source_rows = call(
         functools.partial(pick_kernel, size, [item[:2] for item in arrived]),
         struct((2 * slots, half, width), BF16),
@@ -348,12 +336,14 @@
         [piece for _, _, piece in arrived],
     )
     other_rows = other_core(source_rows)
+    late_own, late_other, _ = lax.optimization_barrier((tile_own, tile_other, source_rows))
+    flipped_own, flipped_other = flip((late_own,)), flip((late_other,))
 
     hidden, packed, kept = call(
         middle_kernel,
         [
             struct((half, inner), BF16),
-            struct((half + width // 2, width), BF16),
+            struct((half + width, width), BF16),
             struct((width // 2, width), F32),
         ],
         tables,
@@ -375,72 +365,71 @@
     )
     other_packed = other_core(packed)
 
-    halves = [struct((cut, width), BF16), struct((half - cut, width), BF16)]
-    products, up_a, down_b, mine = call(
-        functools.partial(product_kernel, size),
-        [struct((2 * slots, half, width), F32), *halves, struct((width // 2, width), BF16)],
+    whole = struct((half, width), BF16)
+    near = [far - 1, size - far + 1]
+    products, up, down, mine, *terms = call(
+        functools.partial(product_kernel, size, near),
+        [
+            struct((2 * slots, half, width), F32),
+            struct((cut, width), BF16),
+            struct((half - cut, width), BF16),
+            struct((width // 2, width), BF16),
+            whole,
+            whole,
+        ],
         tables,
         (flipped_own, flipped_other, packed, other_packed, kept),
         (pltpu.VMEM((block, width), BF16),),
         flops=4 * half * width * slots * block,
     )
-    up_a = along_ring(up_a, order, 1)
-    down_b = along_ring(down_b, order, -1)
-    keys, shapes = [(0, 0)], [struct((half, width), F32)]
-    for step in range(far - 1, 0, -1):
-        for offset in (step, size - step):
-            keys += [(offset, 0), (offset, cut)]
-            shapes += halves
-    terms = call(functools.partial(spread_kernel, size, keys), shapes, tables, (products,))
-    terms = dict(zip(keys, terms, strict=True))
+    up, down = along_ring(up, order, 1), along_ring(down, order, -1)
+    products = lax.optimization_barrier((products, up, down))[0]
+    keys = [0]
+    for step in range(far - 2, 0, -1):
+        keys += [step, size - step]
+    terms += call(
+        functools.partial(spread_kernel, size, keys),
+        [struct((half, width), F32 if key == 0 else BF16) for key in keys],
+        tables,
+        (products,),
+    )
+    terms = dict(zip(near + keys, terms, strict=True))
 
     def joined(received, term):
         return (received.astype(F32) + term.astype(F32)).astype(BF16)
 
     swap = size // 2
-    theirs = swapped(mine, swap)
-    up_b, down_a = lax.optimization_barrier(
-        (terms[far - 1, cut], terms[size - far + 1, 0], up_a, down_b)
-    )[:2]
+    while swap > 4:
+        mine = joined(mine, swapped(mine, swap))
+        swap //= 2
+    four = (swapped(mine, swap), swapped(mine, swap // 2), swapped(mine, swap + swap // 2))
+    up, down = jnp.pad(up, ((0, half - cut), (0, 0))), jnp.pad(down, ((cut, 0), (0, 0)))
     for step in range(far - 1, 0, -1):
-        up_a = joined(up_a, terms[step, 0])
-        down_b = joined(down_b, terms[size - step, cut])
-        if step < far - 1:
-            up_b = joined(up_b, terms[step, cut])
-            down_a = joined(down_a, terms[size - step, 0])
-            if swap > 2:
-                swap //= 2
-                mine = lax.optimization_barrier((joined(mine, theirs), up_a, down_b))[0]
-                theirs = swapped(mine, swap)
+        up, down = joined(up, terms[step]), joined(down, terms[size - step])
         if step == 1:
-            while swap > 2:
-                swap //= 2
-                mine = joined(mine, theirs)
-                theirs = swapped(mine, swap)
-            if swap > 1:
-                mine = lax.optimization_barrier((joined(mine, theirs), up_a, down_b))[0]
+            *four, _, _ = lax.optimization_barrier((*four, up, down))
+            four = [item.astype(F32) for item in (mine, *four)]
+            mine = ((four[0] + four[1]) + (four[2] + four[3])).astype(BF16)
             weight_parts = (mine, swapped(mine, 1), other_core(mine), swapped(mine, 1, across=True))
-        up_a = along_ring(up_a, order, 1)
-        down_b = along_ring(down_b, order, -1)
-        up_b = along_ring(up_b, order, 1)
-        down_a = along_ring(down_a, order, -1)
+        up, down = along_ring(up, order, 1), along_ring(down, order, -1)
+        if step == far - 1:
+            hidden = lax.optimization_barrier((hidden, up))[0]
 
     updated = call(
         update_kernel,
         struct((half, width), BF16),
         (),
-        (mask, hidden, expert_down, first, second),
+        (mask, hidden, expert_down, own_feats),
+        flops=2 * experts * half * width * inner,
     )
     feats_grad, msg_weight_grad = call(
         finish_kernel,
         [struct((half, width), BF16), struct((width, width), F32)],
         (place,),
         (
-            terms[0, 0],
-            up_a,
-            up_b,
-            down_a,
-            down_b,
+            terms[0],
+            up,
+            down,
             msg_weight,
             out_grad,
             *weight_parts,

time: 77.6 us -> 75.7 us (0.976)
  starting transfers between devices: 37.6 us -> 26.6 us
  waiting for transfers between devices: 17.3 us -> 28.1 us
  Pallas kernels: 16.2 us -> 14 us
    ppermute x28 -> x16, waiting for transfers between devices: 9.78 us -> 21.9 us  [along_ring(): return lax.ppermute(block, 'grid', route)]
    ppermute x28 -> x16, starting transfers between devices: 31 us -> 19 us  [along_ring(): return lax.ppermute(block, 'grid', route)]
    ppermute x4 -> x5, waiting for transfers between devices: 5.67 us -> 2.76 us  [swapped(): return lax.ppermute(block, axes, route)]
    pallas_call x9, Pallas kernels: 16.2 us -> 14 us  [call(): pl.pallas_call(kernel, out_shape=out_shape, in_specs=[pl.BlockSpec(memory...]
    ppermute x5, waiting for transfers between devices: 1.81 us -> 3.46 us  [other_core(): return lax.ppermute(block, 'rep', [(0, 1), (1, 0)])]
    unnamed x18, local copies, waits for them, and re-layouts: 2.73 us -> 4.26 us
    ppermute x5, starting transfers between devices: 1.43 us -> 2.77 us  [other_core(): return lax.ppermute(block, 'rep', [(0, 1), (1, 0)])]
    dynamic_slice x1, local copies, waits for them, and re-layouts: 0.98 us -> 0.02 us  [per_device(): own_feats = lax.dynamic_slice_in_dim(feats, core * half, half, 0)]
  transfers between devices with their start and end apart: 37 -> 26, of which waited for: 13 -> 14; matrix products, arithmetic and copies ran while one was open for 1% -> 1% of each run, Pallas kernels for 11% -> 9%
where the time goes in v3:
time: 75.7 us; the launch traced here: 75.5 us
  waiting for transfers between devices  28.1 us (37%)
  starting transfers between devices  26.6 us (35%)
  Pallas kernels  14 us (18%)
  local copies, waits for them, and re-layouts  4.29 us (6%)
  between operations  2.14 us (3%)
    ppermute x16, waiting for transfers between devices, along_ring(): return lax.ppermute(block, 'grid', route)  21.9 us
    ppermute x16, starting transfers between devices, along_ring(): return lax.ppermute(block, 'grid', route)  19 us
    pallas_call x9, Pallas kernels, call(): pl.pallas_call(kernel, out_shape=out_shape, in_specs=[pl.BlockSpec(memory...  14 us
    ppermute x5, starting transfers between devices, swapped(): return lax.ppermute(block, axes, route)  4.74 us
    unnamed x18, local copies, waits for them, and re-layouts  4.26 us
    ppermute x5, waiting for transfers between devices, other_core(): return lax.ppermute(block, 'rep', [(0, 1), (1, 0)])  3.46 us
    ppermute x5, starting transfers between devices, other_core(): return lax.ppermute(block, 'rep', [(0, 1), (1, 0)])  2.77 us
    ppermute x5, waiting for transfers between devices, swapped(): return lax.ppermute(block, axes, route)  2.76 us
  transfers between devices with their start and end apart: 26, of which 14 were waited for; matrix products, arithmetic and copies ran while one was open for 1% of the time, Pallas kernels for 9%

profile of v3, /device:TPU:0, one launch (start us, length us, event | category | flops | bytes accessed | tf_op | source)
XLA Modules:
  0.0 75.5 jit_solution(9374970909384326732)
XLA Ops:
  0.6 0.0 copy-start
  0.6 1.0 %copy-done = bf16[896,256]{1,0:T(8,128)(2,1)S(1)} copy-done((bf16[896,256]{1,0:T(8,128)(2,1)S(1)}, bf16[896,256]{1,0:T(8,128)(2,1)}, u32[]{:S(2)}) %copy-start) | copy-done | bytes 458776
  1.7 0.5 collective-permute-start.5
  2.2 2.6 %collective-permute-start.1 = (bf16[448,256]{1,0:T(8,128)(2,1)S(1)}, bf16[448,256]{1,0:T(8,128)(2,1)S(1)}, u32[]{:S(2)}, u32[]{:S(2)}) collective-permute-start(bf16[448,256]{1,0:T(8,128)(2,1)S(1)} %constant_dynamic-slice_fusion.refs_0_.feats), channel_id=1, source_target_pairs={{0,2},{4,0},{8,4},{12,8},{14,12},{10,14},{6,10},{2,6},{1,3},{5,1},... | collective-permute-start | bytes 688136 | tf_op jit(solution)/shard_map/ppermute | solution.py:27
  4.8 0.1 collective-permute-start
  6.2 0.1 collective-permute-start.2
  6.4 1.1 %collective-permute-done.2.other_table = s32[2,1]{1,0:T(2,128)S(1)} collective-permute-done((s32[2,1]{1,0:T(2,128)S(1)}, s32[2,1]{1,0:T(2,128)S(1)}, u32[]{:S(2)}, u32[]{:S(2)}) %collective-permute-start.2) | collective-permute-done | bytes 40 | tf_op jit(solution)/shard_map/ppermute | solution.py:31
  7.4 3.6 %collective-permute-done.1.refs_2_ = bf16[448,256]{1,0:T(8,128)(2,1)S(1)} collective-permute-done((bf16[448,256]{1,0:T(8,128)(2,1)S(1)}, bf16[448,256]{1,0:T(8,128)(2,1)S(1)}, u32[]{:S(2)}, u32[]{:S(2)}) %collective-permute-start.1) | collective-permute-done | bytes 229408 | tf_op jit(solution)/shard_map/ppermute | solution.py:27
  11.0 1.4 %collective-permute-done.refs_1_ = bf16[448,256]{1,0:T(8,128)(2,1)S(1)} collective-permute-done((bf16[448,256]{1,0:T(8,128)(2,1)S(1)}, bf16[448,256]{1,0:T(8,128)(2,1)S(1)}, u32[]{:S(2)}, u32[]{:S(2)}) %collective-permute-start) | collective-permute-done | bytes 229408 | tf_op jit(solution)/shard_map/ppermute | solution.py:27
  12.4 0.3 collective-permute-start.3
  12.8 1.7 %collective-permute-start.4 = (bf16[448,256]{1,0:T(8,128)(2,1)S(1)}, bf16[448,256]{1,0:T(8,128)(2,1)S(1)}, u32[]{:S(2)}, u32[]{:S(2)}) collective-permute-start(bf16[448,256]{1,0:T(8,128)(2,1)S(1)} %collective-permute-done.1.refs_2_), channel_id=1, source_target_pairs={{0,2},{4,0},{8,4},{12,8},{14,12},{10,14},{6,10},{2,6},{1,3},{5,1},... | collective-permute-start | bytes 688136 | tf_op jit(solution)/shard_map/ppermute | solution.py:27
  14.5 0.1 pad_add_fusion.1.place
  14.6 1.6 %copy-done.3 = bf16[8,512,256]{2,1,0:T(8,128)(2,1)S(1)} copy-done((bf16[8,512,256]{2,1,0:T(8,128)(2,1)S(1)}, bf16[8,512,256]{2,1,0:T(8,128)(2,1)}, u32[]{:S(2)}) %copy-start.3) | copy-done | bytes 2097176
  16.1 0.9 %copy-done.6 = bf16[448,256]{1,0:T(8,128)(2,1)S(1)} copy-done((bf16[448,256]{1,0:T(8,128)(2,1)S(1)}, bf16[448,256]{1,0:T(8,128)(2,1)}, u32[]{:S(2)}) %copy-start.6) | copy-done | bytes 229400
  17.1 0.7 copy-done.8
  17.8 2.1 %shard_map.112 = (bf16[8,448,256]{2,1,0:T(8,128)(2,1)S(1)}, f32[448,512]{1,0:T(8,128)S(1)}) custom-call(s32[2]{0:T(128)S(1)} %pad_add_fusion.1.place, s32[896]{0:T(1024)S(1)} %copy-done.8, bf16[448,256]{1,0:T(8,128)(2,1)S(1)} %copy-done.6, bf16[8,512,256]{2,1,0:T(8,128)(2,1)S(1)} %copy-done.3), custom_call_target="tpu_custom_call" | custom-call | flops 939524096 | bytes 5082624 | tf_op jit(solution)/shard_map/pallas_call | solution.py:44
  19.9 0.0 copy-start.1
  19.9 0.0 copy-start.5
  19.9 0.0 collective-permute-done.4.refs_4_
  19.9 1.3 %collective-permute-start.6 = (bf16[448,256]{1,0:T(8,128)(2,1)S(1)}, bf16[448,256]{1,0:T(8,128)(2,1)S(1)}, u32[]{:S(2)}, u32[]{:S(2)}) collective-permute-start(bf16[448,256]{1,0:T(8,128)(2,1)S(1)} %collective-permute-done.3.refs_3_), channel_id=1, source_target_pairs={{0,4},{4,8},{8,12},{12,14},{14,10},{10,6},{6,2},{2,0},{1,5},{5,9},... | collective-permute-start | bytes 688136 | tf_op jit(solution)/shard_map/ppermute | solution.py:27
  21.2 0.8 collective-permute-start.7
  22.0 4.3 %collective-permute-done.6.refs_5_ = bf16[448,256]{1,0:T(8,128)(2,1)S(1)} collective-permute-done((bf16[448,256]{1,0:T(8,128)(2,1)S(1)}, bf16[448,256]{1,0:T(8,128)(2,1)S(1)}, u32[]{:S(2)}, u32[]{:S(2)}) %collective-permute-start.6) | collective-permute-done | bytes 229408 | tf_op jit(solution)/shard_map/ppermute | solution.py:27
  26.3 1.2 %collective-permute-start.8 = (bf16[224,256]{1,0:T(8,128)(2,1)S(1)}, bf16[224,256]{1,0:T(8,128)(2,1)S(1)}, u32[]{:S(2)}, u32[]{:S(2)}) collective-permute-start(bf16[224,256]{1,0:T(8,128)(2,1)S(1)} %slice.8), channel_id=1, source_target_pairs={{0,4},{4,8},{8,12},{12,14},{14,10},{10,6},{6,2},{2,0},{1,5},{5,9},... | collective-permute-start | bytes 344072 | tf_op jit(solution)/shard_map/ppermute | solution.py:27
  27.5 0.0 collective-permute-done.7.refs_6_
  27.5 0.9 %collective-permute-start.9 = (bf16[224,256]{1,0:T(8,128)(2,1)S(1)}, bf16[224,256]{1,0:T(8,128)(2,1)S(1)}, u32[]{:S(2)}, u32[]{:S(2)}) collective-permute-start(bf16[224,256]{1,0:T(8,128)(2,1)S(1)} %slice.9), channel_id=1, source_target_pairs={{0,2},{4,0},{8,4},{12,8},{14,12},{10,14},{6,10},{2,6},{1,3},{5,1},... | collective-permute-start | bytes 344072 | tf_op jit(solution)/shard_map/ppermute | solution.py:27
  28.4 2.7 %collective-permute-done.8.refs_7_ = bf16[224,256]{1,0:T(8,128)(2,1)S(1)} collective-permute-done((bf16[224,256]{1,0:T(8,128)(2,1)S(1)}, bf16[224,256]{1,0:T(8,128)(2,1)S(1)}, u32[]{:S(2)}, u32[]{:S(2)}) %collective-permute-start.8) | collective-permute-done | bytes 114720 | tf_op jit(solution)/shard_map/ppermute | solution.py:27
  31.1 1.2 %collective-permute-done.9.refs_8_ = bf16[224,256]{1,0:T(8,128)(2,1)S(1)} collective-permute-done((bf16[224,256]{1,0:T(8,128)(2,1)S(1)}, bf16[224,256]{1,0:T(8,128)(2,1)S(1)}, u32[]{:S(2)}, u32[]{:S(2)}) %collective-permute-start.9) | collective-permute-done | bytes 114720 | tf_op jit(solution)/shard_map/ppermute | solution.py:27
  32.3 0.7 shard_map.113.own_rows
  33.0 0.1 collective-permute-start.10
  33.1 1.8 %collective-permute-done.10.other_rows = bf16[2,448,256]{2,1,0:T(8,128)(2,1)S(1)} collective-permute-done((bf16[2,448,256]{2,1,0:T(8,128)(2,1)S(1)}, bf16[2,448,256]{2,1,0:T(8,128)(2,1)S(1)}, u32[]{:S(2)}, u32[]{:S(2)}) %collective-permute-start.10) | collective-permute-done | bytes 458784 | tf_op jit(solution)/shard_map/ppermute | solution.py:31
  34.9 4.3 %shard_map.114 = (bf16[448,512]{1,0:T(8,128)(2,1)S(1)}, bf16[704,256]{1,0:T(8,128)(2,1)S(1)}, f32[128,256]{1,0:T(8,128)S(1)}) custom-call(s32[2]{0:T(128)S(1)} %pad_add_fusion.1.place, s32[2,1]{1,0:T(2,128)S(1)} %pad_add_fusion.own_table, s32[2,1]{1,0:T(2,128)S(1)} %collective-permute-done.2.other_table, bf16[1,896,896]{2,1,0:T(8,128)(2,1)S(1)} %bitcast.8, ...), custom_call_target="tpu_custom_call" | custom-call | flops 2290089984 | bytes 10059776 | tf_op jit(solution)/shard_map/pallas_call | solution.py:44
  39.3 0.2 collective-permute-start.11
  39.5 0.5 shard_map.115.own_flipped
  39.9 0.5 shard_map.116.other_flipped
  40.4 0.6 collective-permute-done.11.other_packed
  41.0 1.5 %shard_map.117 = (f32[2,448,256]{2,1,0:T(8,128)S(1)}, bf16[224,256]{1,0:T(8,128)(2,1)S(1)}, bf16[224,256]{1,0:T(8,128)(2,1)S(1)}, bf16[128,256]{1,0:T(8,128)(2,1...) custom-call(s32[2]{0:T(128)S(1)} %pad_add_fusion.1.place, s32[2,1]{1,0:T(2,128)S(1)} %pad_add_fusion.own_table, ...), custom_call_target="tpu_custom_call" | custom-call | flops 411041792 | bytes 5734400 | tf_op jit(solution)/shard_map/pallas_call | solution.py:44
  42.5 1.6 %collective-permute-start.12 = (bf16[224,256]{1,0:T(8,128)(2,1)S(1)}, bf16[224,256]{1,0:T(8,128)(2,1)S(1)}, u32[]{:S(2)}, u32[]{:S(2)}) collective-permute-start(bf16[224,256]{1,0:T(8,128)(2,1)S(1)} %get-tuple-element.51), channel_id=1, source_target_pairs={{0,4},{4,8},{8,12},{12,14},{14,10},{10,6},{6,2},{2,0},{1,5},{5,9},... | collective-permute-start | bytes 344072 | tf_op jit(solution)/shard_map/ppermute | solution.py:27
  44.1 0.5 collective-permute-start.14
  44.6 3.4 %collective-permute-start.22 = (bf16[128,256]{1,0:T(8,128)(2,1)S(1)}, bf16[128,256]{1,0:T(8,128)(2,1)S(1)}, u32[]{:S(2)}, u32[]{:S(2)}) collective-permute-start(bf16[128,256]{1,0:T(8,128)(2,1)S(1)} %get-tuple-element.63), channel_id=1, source_target_pairs={{0,12},{1,13},{2,14},{3,15},{4,8},{5,9},{6,10},{7,11},{8,4},{9,5},... | collective-permute-start | bytes 196616 | tf_op jit(solution)/shard_map/ppermute | solution.py:37
  48.0 1.0 %collective-permute-start.20 = (bf16[128,256]{1,0:T(8,128)(2,1)S(1)}, bf16[128,256]{1,0:T(8,128)(2,1)S(1)}, u32[]{:S(2)}, u32[]{:S(2)}) collective-permute-start(bf16[128,256]{1,0:T(8,128)(2,1)S(1)} %get-tuple-element.63), channel_id=1, source_target_pairs={{0,8},{1,9},{2,10},{3,11},{4,12},{5,13},{6,14},{7,15},{8,0},{9,1},... | collective-permute-start | bytes 196616 | tf_op jit(solution)/shard_map/ppermute | solution.py:37
  49.0 0.1 collective-permute-done.14
  49.1 3.5 %collective-permute-start.13 = (bf16[448,256]{1,0:T(8,128)(2,1)S(1)}, bf16[448,256]{1,0:T(8,128)(2,1)S(1)}, u32[]{:S(2)}, u32[]{:S(2)}) collective-permute-start(bf16[448,256]{1,0:T(8,128)(2,1)S(1)} %add_convert_fusion.5), channel_id=1, source_target_pairs={{0,4},{4,8},{8,12},{12,14},{14,10},{10,6},{6,2},{2,0},{1,5},{5,9},... | collective-permute-start | bytes 688136 | tf_op jit(solution)/shard_map/ppermute | solution.py:27
  52.6 0.1 collective-permute-start.17
  52.6 1.0 %shard_map.119 = (f32[448,256]{1,0:T(8,128)S(1)}, bf16[448,256]{1,0:T(8,128)(2,1)S(1)}, bf16[448,256]{1,0:T(8,128)(2,1)S(1)}, bf16[448,256]{1,0:T(8,128)(2,1)S(1)}, bf16[448,256]{1,0:T(8,128)(2,1)S(1)}) custom-call(s32[2]{0:T(128)S(1)} %pad_add_fusion.1.place, s32[2,1]{1,0:T(2,128)S(1)} %pad_add_fusion.own_table, ...), custom_call_target="tpu_custom_call" | custom-call | bytes 2293760 | tf_op jit(solution)/shard_map/pallas_call | solution.py:44
  53.6 0.0 copy-start.4
  53.6 3.2 %collective-permute-done.13 = bf16[448,256]{1,0:T(8,128)(2,1)S(1)} collective-permute-done((bf16[448,256]{1,0:T(8,128)(2,1)S(1)}, bf16[448,256]{1,0:T(8,128)(2,1)S(1)}, u32[]{:S(2)}, u32[]{:S(2)}) %collective-permute-start.13) | collective-permute-done | bytes 229408 | tf_op jit(solution)/shard_map/ppermute | solution.py:27
  56.8 0.1 add_convert_fusion.4
  56.9 2.5 %collective-permute-start.15 = (bf16[448,256]{1,0:T(8,128)(2,1)S(1)}, bf16[448,256]{1,0:T(8,128)(2,1)S(1)}, u32[]{:S(2)}, u32[]{:S(2)}) collective-permute-start(bf16[448,256]{1,0:T(8,128)(2,1)S(1)} %add_convert_fusion.4), channel_id=1, source_target_pairs={{0,4},{4,8},{8,12},{12,14},{14,10},{10,6},{6,2},{2,0},{1,5},{5,9},... | collective-permute-start | bytes 688136 | tf_op jit(solution)/shard_map/ppermute | solution.py:27
  59.4 0.1 add_convert_fusion.1
  59.5 0.3 collective-permute-start.18
  59.8 5.0 %collective-permute-done.15 = bf16[448,256]{1,0:T(8,128)(2,1)S(1)} collective-permute-done((bf16[448,256]{1,0:T(8,128)(2,1)S(1)}, bf16[448,256]{1,0:T(8,128)(2,1)S(1)}, u32[]{:S(2)}, u32[]{:S(2)}) %collective-permute-start.15) | collective-permute-done | bytes 229408 | tf_op jit(solution)/shard_map/ppermute | solution.py:27
  64.7 0.1 add_convert_fusion.3
  64.8 1.5 %collective-permute-start.16 = (bf16[448,256]{1,0:T(8,128)(2,1)S(1)}, bf16[448,256]{1,0:T(8,128)(2,1)S(1)}, u32[]{:S(2)}, u32[]{:S(2)}) collective-permute-start(bf16[448,256]{1,0:T(8,128)(2,1)S(1)} %add_convert_fusion.3), channel_id=1, source_target_pairs={{0,4},{4,8},{8,12},{12,14},{14,10},{10,6},{6,2},{2,0},{1,5},{5,9},... | collective-permute-start | bytes 688136 | tf_op jit(solution)/shard_map/ppermute | solution.py:27
  66.3 0.5 collective-permute-done.18
  66.7 0.1 add_convert_fusion
  66.8 0.2 collective-permute-start.19
  67.1 0.0 copy-start.7
  67.1 0.1 collective-permute-start.25
  67.1 1.8 %collective-permute-start.24 = (bf16[128,256]{1,0:T(8,128)(2,1)S(1)}, bf16[128,256]{1,0:T(8,128)(2,1)S(1)}, u32[]{:S(2)}, u32[]{:S(2)}) collective-permute-start(bf16[128,256]{1,0:T(8,128)(2,1)S(1)} %add_convert_fusion.6.own_part), channel_id=1, source_target_pairs={{0,1},{1,0},{2,3},{3,2},{4,5},{5,4},{6,7},{7,6},{8,9},{9,8},{10,11... | collective-permute-start | bytes 196616 | tf_op jit(solution)/shard_map/ppermute | solution.py:31
  69.0 0.3 collective-permute-start.23
  69.3 1.8 %shard_map.118 = bf16[448,256]{1,0:T(8,128)(2,1)} custom-call(bf16[8,448,256]{2,1,0:T(8,128)(2,1)S(1)} %get-tuple-element.40.mask, bf16[448,512]{1,0:T(8,128)(2,1)S(1)} %get-tuple-element.53.hidden, bf16[8,512,256]{2,1,0:T(8,128)(2,1)S(1)} %copy-done.4, bf16[448,256]{1,0:T(8,128)(2,1)S(1)} %constant_dynamic-slice_fusion.refs_0_.feats), custom_call_target="tpu_custom_call" | custom-call | flops 939524096 | bytes 4849664 | tf_op jit(solution)/shard_map/pallas_call | solution.py:44
  71.1 1.8 %collective-permute-done.25.other_swapped = bf16[128,256]{1,0:T(8,128)(2,1)S(1)} collective-permute-done((bf16[128,256]{1,0:T(8,128)(2,1)S(1)}, bf16[128,256]{1,0:T(8,128)(2,1)S(1)}, u32[]{:S(2)}, u32[]{:S(2)}) %collective-permute-start.25) | collective-permute-done | bytes 65568 | tf_op jit(solution)/shard_map/ppermute | solution.py:37
  72.9 1.0 %collective-permute-done.23.own_swapped = bf16[128,256]{1,0:T(8,128)(2,1)S(1)} collective-permute-done((bf16[128,256]{1,0:T(8,128)(2,1)S(1)}, bf16[128,256]{1,0:T(8,128)(2,1)S(1)}, u32[]{:S(2)}, u32[]{:S(2)}) %collective-permute-start.23) | collective-permute-done | bytes 65568 | tf_op jit(solution)/shard_map/ppermute | solution.py:37
  73.9 1.6 %shard_map.120 = (bf16[448,256]{1,0:T(8,128)(2,1)}, f32[256,256]{1,0:T(8,128)}) custom-call(s32[2]{0:T(128)S(1)} %pad_add_fusion.1.place, f32[448,256]{1,0:T(8,128)S(1)} %get-tuple-element.57.own, bf16[448,256]{1,0:T(8,128)(2,1)S(1)} %collective-permute-done.16.up, bf16[448,256]{1,0:T(8,128)(2,1)S(1)} %collective-permute-done.19.down, ...), custom_call_target="tpu_custom_call" | custom-call | bytes 2031616 | tf_op jit(solution)/shard_map/pallas_call | solution.py:44
  (27 shorter events, 0.2 us)
Async XLA Ops:
  0.6 1.0 %copy-start = (bf16[896,256]{1,0:T(8,128)(2,1)S(1)}, bf16[896,256]{1,0:T(8,128)(2,1)}, u32[]{:S(2)}) copy-start(bf16[896,256]{1,0:T(8,128)(2,1)} %param.9) | copy-start | bytes 1376260
  1.7 33.2 %collective-permute-start.5 = (bf16[1,896,896]{2,1,0:T(8,128)(2,1)}, bf16[1,896,896]{2,1,0:T(8,128)(2,1)S(1)}, u32[]{:S(2)}, u32[]{:S(2)}) collective-permute-start(bf16[1,896,896]{2,1,0:T(8,128)(2,1)} %bitcast.7), channel_id=1, source_target_pairs={{0,1},{1,0},{2,3},{3,2},{4,5},{5,4},{6,7},{7,6},{8,9},{9,8},{10,11... | collective-permute-start | bytes 4816904 | tf_op jit(solution)/shard_map/ppermute | solution.py:31
  2.2 8.8 %collective-permute-start.1 = (bf16[448,256]{1,0:T(8,128)(2,1)S(1)}, bf16[448,256]{1,0:T(8,128)(2,1)S(1)}, u32[]{:S(2)}, u32[]{:S(2)}) collective-permute-start(bf16[448,256]{1,0:T(8,128)(2,1)S(1)} %constant_dynamic-slice_fusion.refs_0_.feats), channel_id=1, source_target_pairs={{0,2},{4,0},{8,4},{12,8},{14,12},{10,14},{6,10},{2,6},{1,3},{5,1},... | collective-permute-start | bytes 688136 | tf_op jit(solution)/shard_map/ppermute | solution.py:27
  4.8 7.7 %collective-permute-start = (bf16[448,256]{1,0:T(8,128)(2,1)S(1)}, bf16[448,256]{1,0:T(8,128)(2,1)S(1)}, u32[]{:S(2)}, u32[]{:S(2)}) collective-permute-start(bf16[448,256]{1,0:T(8,128)(2,1)S(1)} %constant_dynamic-slice_fusion.refs_0_.feats), channel_id=1, source_target_pairs={{0,4},{4,8},{8,12},{12,14},{14,10},{10,6},{6,2},{2,0},{1,5},{5,9},... | collective-permute-start | bytes 688136 | tf_op jit(solution)/shard_map/ppermute | solution.py:27
  6.2 1.2 %collective-permute-start.2 = (s32[2,1]{1,0:T(2,128)S(1)}, s32[2,1]{1,0:T(2,128)S(1)}, u32[]{:S(2)}, u32[]{:S(2)}) collective-permute-start(s32[2,1]{1,0:T(2,128)S(1)} %pad_add_fusion.own_table), channel_id=1, source_target_pairs={{0,1},{1,0},{2,3},{3,2},{4,5},{5,4},{6,7},{7,6},{8,9},{9,8},{10,11... | collective-permute-start | bytes 32 | tf_op jit(solution)/shard_map/ppermute | solution.py:31
  12.4 7.5 %collective-permute-start.3 = (bf16[448,256]{1,0:T(8,128)(2,1)S(1)}, bf16[448,256]{1,0:T(8,128)(2,1)S(1)}, u32[]{:S(2)}, u32[]{:S(2)}) collective-permute-start(bf16[448,256]{1,0:T(8,128)(2,1)S(1)} %collective-permute-done.refs_1_), channel_id=1, source_target_pairs={{0,4},{4,8},{8,12},{12,14},{14,10},{10,6},{6,2},{2,0},{1,5},{5,9},... | collective-permute-start | bytes 688136 | tf_op jit(solution)/shard_map/ppermute | solution.py:27
  12.8 7.1 %collective-permute-start.4 = (bf16[448,256]{1,0:T(8,128)(2,1)S(1)}, bf16[448,256]{1,0:T(8,128)(2,1)S(1)}, u32[]{:S(2)}, u32[]{:S(2)}) collective-permute-start(bf16[448,256]{1,0:T(8,128)(2,1)S(1)} %collective-permute-done.1.refs_2_), channel_id=1, source_target_pairs={{0,2},{4,0},{8,4},{12,8},{14,12},{10,14},{6,10},{2,6},{1,3},{5,1},... | collective-permute-start | bytes 688136 | tf_op jit(solution)/shard_map/ppermute | solution.py:27
  14.5 1.6 %copy-start.3 = (bf16[8,512,256]{2,1,0:T(8,128)(2,1)S(1)}, bf16[8,512,256]{2,1,0:T(8,128)(2,1)}, u32[]{:S(2)}) copy-start(bf16[8,512,256]{2,1,0:T(8,128)(2,1)} %down.3) | copy-start | bytes 6291460
  16.1 0.9 %copy-start.6 = (bf16[448,256]{1,0:T(8,128)(2,1)S(1)}, bf16[448,256]{1,0:T(8,128)(2,1)}, u32[]{:S(2)}) copy-start(bf16[448,256]{1,0:T(8,128)(2,1)} %out_grad.3) | copy-start | bytes 688132
  17.1 0.7 copy-start.8
  17.8 17.2 %copy-start.2 = (bf16[8,256,512]{2,1,0:T(8,128)(2,1)S(1)}, bf16[8,256,512]{2,1,0:T(8,128)(2,1)}, u32[]{:S(2)}) copy-start(bf16[8,256,512]{2,1,0:T(8,128)(2,1)} %up.1) | copy-start | bytes 6291460
  19.9 15.1 %copy-start.1 = (bf16[1,1,1,896,896]{4,3,2,1,0:T(8,128)(2,1)S(1)}, bf16[1,1,1,896,896]{4,3,2,1,0:T(8,128)(2,1)}, u32[]{:S(2)}) copy-start(bf16[1,1,1,896,896]{4,3,2,1,0:T(8,128)(2,1)} %param.11) | copy-start | bytes 4816900
  19.9 15.0 %copy-start.5 = (bf16[256,256]{1,0:T(8,128)(2,1)S(1)}, bf16[256,256]{1,0:T(8,128)(2,1)}, u32[]{:S(2)}) copy-start(bf16[256,256]{1,0:T(8,128)(2,1)} %weight.3) | copy-start | bytes 393220
  19.9 6.3 %collective-permute-start.6 = (bf16[448,256]{1,0:T(8,128)(2,1)S(1)}, bf16[448,256]{1,0:T(8,128)(2,1)S(1)}, u32[]{:S(2)}, u32[]{:S(2)}) collective-permute-start(bf16[448,256]{1,0:T(8,128)(2,1)S(1)} %collective-permute-done.3.refs_3_), channel_id=1, source_target_pairs={{0,4},{4,8},{8,12},{12,14},{14,10},{10,6},{6,2},{2,0},{1,5},{5,9},... | collective-permute-start | bytes 688136 | tf_op jit(solution)/shard_map/ppermute | solution.py:27
  21.2 6.2 %collective-permute-start.7 = (bf16[448,256]{1,0:T(8,128)(2,1)S(1)}, bf16[448,256]{1,0:T(8,128)(2,1)S(1)}, u32[]{:S(2)}, u32[]{:S(2)}) collective-permute-start(bf16[448,256]{1,0:T(8,128)(2,1)S(1)} %collective-permute-done.4.refs_4_), channel_id=1, source_target_pairs={{0,2},{4,0},{8,4},{12,8},{14,12},{10,14},{6,10},{2,6},{1,3},{5,1},... | collective-permute-start | bytes 688136 | tf_op jit(solution)/shard_map/ppermute | solution.py:27
  26.3 4.8 %collective-permute-start.8 = (bf16[224,256]{1,0:T(8,128)(2,1)S(1)}, bf16[224,256]{1,0:T(8,128)(2,1)S(1)}, u32[]{:S(2)}, u32[]{:S(2)}) collective-permute-start(bf16[224,256]{1,0:T(8,128)(2,1)S(1)} %slice.8), channel_id=1, source_target_pairs={{0,4},{4,8},{8,12},{12,14},{14,10},{10,6},{6,2},{2,0},{1,5},{5,9},... | collective-permute-start | bytes 344072 | tf_op jit(solution)/shard_map/ppermute | solution.py:27
  27.5 4.8 %collective-permute-start.9 = (bf16[224,256]{1,0:T(8,128)(2,1)S(1)}, bf16[224,256]{1,0:T(8,128)(2,1)S(1)}, u32[]{:S(2)}, u32[]{:S(2)}) collective-permute-start(bf16[224,256]{1,0:T(8,128)(2,1)S(1)} %slice.9), channel_id=1, source_target_pairs={{0,2},{4,0},{8,4},{12,8},{14,12},{10,14},{6,10},{2,6},{1,3},{5,1},... | collective-permute-start | bytes 344072 | tf_op jit(solution)/shard_map/ppermute | solution.py:27
  33.0 1.9 %collective-permute-start.10 = (bf16[2,448,256]{2,1,0:T(8,128)(2,1)S(1)}, bf16[2,448,256]{2,1,0:T(8,128)(2,1)S(1)}, u32[]{:S(2)}, u32[]{:S(2)}) collective-permute-start(bf16[2,448,256]{2,1,0:T(8,128)(2,1)S(1)} %shard_map.113.own_rows), channel_id=1, source_target_pairs={{0,1},{1,0},{2,3},{3,2},{4,5},{5,4},{6,7},{7,6},{8,9},{9,8},{10,11... | collective-permute-start | bytes 1376264 | tf_op jit(solution)/shard_map/ppermute | solution.py:31
  39.3 1.7 %collective-permute-start.11 = (bf16[704,256]{1,0:T(8,128)(2,1)S(1)}, bf16[704,256]{1,0:T(8,128)(2,1)S(1)}, u32[]{:S(2)}, u32[]{:S(2)}) collective-permute-start(bf16[704,256]{1,0:T(8,128)(2,1)S(1)} %get-tuple-element.49.own_packed), channel_id=1, source_target_pairs={{0,1},{1,0},{2,3},{3,2},{4,5},{5,4},{6,7},{7,6},{8,9},{9,8},{10,11... | collective-permute-start | bytes 1081352 | tf_op jit(solution)/shard_map/ppermute | solution.py:31
  42.5 6.5 %collective-permute-start.12 = (bf16[224,256]{1,0:T(8,128)(2,1)S(1)}, bf16[224,256]{1,0:T(8,128)(2,1)S(1)}, u32[]{:S(2)}, u32[]{:S(2)}) collective-permute-start(bf16[224,256]{1,0:T(8,128)(2,1)S(1)} %get-tuple-element.51), channel_id=1, source_target_pairs={{0,4},{4,8},{8,12},{12,14},{14,10},{10,6},{6,2},{2,0},{1,5},{5,9},... | collective-permute-start | bytes 344072 | tf_op jit(solution)/shard_map/ppermute | solution.py:27
  44.1 4.9 %collective-permute-start.14 = (bf16[224,256]{1,0:T(8,128)(2,1)S(1)}, bf16[224,256]{1,0:T(8,128)(2,1)S(1)}, u32[]{:S(2)}, u32[]{:S(2)}) collective-permute-start(bf16[224,256]{1,0:T(8,128)(2,1)S(1)} %get-tuple-element.55), channel_id=1, source_target_pairs={{0,2},{4,0},{8,4},{12,8},{14,12},{10,14},{6,10},{2,6},{1,3},{5,1},... | collective-permute-start | bytes 344072 | tf_op jit(solution)/shard_map/ppermute | solution.py:27
  44.6 22.4 %collective-permute-start.22 = (bf16[128,256]{1,0:T(8,128)(2,1)S(1)}, bf16[128,256]{1,0:T(8,128)(2,1)S(1)}, u32[]{:S(2)}, u32[]{:S(2)}) collective-permute-start(bf16[128,256]{1,0:T(8,128)(2,1)S(1)} %get-tuple-element.63), channel_id=1, source_target_pairs={{0,12},{1,13},{2,14},{3,15},{4,8},{5,9},{6,10},{7,11},{8,4},{9,5},... | collective-permute-start | bytes 196616 | tf_op jit(solution)/shard_map/ppermute | solution.py:37
  48.0 19.0 %collective-permute-start.21 = (bf16[128,256]{1,0:T(8,128)(2,1)S(1)}, bf16[128,256]{1,0:T(8,128)(2,1)S(1)}, u32[]{:S(2)}, u32[]{:S(2)}) collective-permute-start(bf16[128,256]{1,0:T(8,128)(2,1)S(1)} %get-tuple-element.63), channel_id=1, source_target_pairs={{0,4},{1,5},{2,6},{3,7},{4,0},{5,1},{6,2},{7,3},{8,12},{9,13},{10,... | collective-permute-start | bytes 196616 | tf_op jit(solution)/shard_map/ppermute | solution.py:37
  48.0 19.0 %collective-permute-start.20 = (bf16[128,256]{1,0:T(8,128)(2,1)S(1)}, bf16[128,256]{1,0:T(8,128)(2,1)S(1)}, u32[]{:S(2)}, u32[]{:S(2)}) collective-permute-start(bf16[128,256]{1,0:T(8,128)(2,1)S(1)} %get-tuple-element.63), channel_id=1, source_target_pairs={{0,8},{1,9},{2,10},{3,11},{4,12},{5,13},{6,14},{7,15},{8,0},{9,1},... | collective-permute-start | bytes 196616 | tf_op jit(solution)/shard_map/ppermute | solution.py:37
  49.1 7.7 %collective-permute-start.13 = (bf16[448,256]{1,0:T(8,128)(2,1)S(1)}, bf16[448,256]{1,0:T(8,128)(2,1)S(1)}, u32[]{:S(2)}, u32[]{:S(2)}) collective-permute-start(bf16[448,256]{1,0:T(8,128)(2,1)S(1)} %add_convert_fusion.5), channel_id=1, source_target_pairs={{0,4},{4,8},{8,12},{12,14},{14,10},{10,6},{6,2},{2,0},{1,5},{5,9},... | collective-permute-start | bytes 688136 | tf_op jit(solution)/shard_map/ppermute | solution.py:27
  52.6 6.9 %collective-permute-start.17 = (bf16[448,256]{1,0:T(8,128)(2,1)S(1)}, bf16[448,256]{1,0:T(8,128)(2,1)S(1)}, u32[]{:S(2)}, u32[]{:S(2)}) collective-permute-start(bf16[448,256]{1,0:T(8,128)(2,1)S(1)} %add_convert_fusion.2), channel_id=1, source_target_pairs={{0,2},{4,0},{8,4},{12,8},{14,12},{10,14},{6,10},{2,6},{1,3},{5,1},... | collective-permute-start | bytes 688136 | tf_op jit(solution)/shard_map/ppermute | solution.py:27
  53.6 15.7 %copy-start.4 = (bf16[8,512,256]{2,1,0:T(8,128)(2,1)S(1)}, bf16[8,512,256]{2,1,0:T(8,128)(2,1)}, u32[]{:S(2)}) copy-start(bf16[8,512,256]{2,1,0:T(8,128)(2,1)} %down.3) | copy-start | bytes 6291460
  56.9 7.9 %collective-permute-start.15 = (bf16[448,256]{1,0:T(8,128)(2,1)S(1)}, bf16[448,256]{1,0:T(8,128)(2,1)S(1)}, u32[]{:S(2)}, u32[]{:S(2)}) collective-permute-start(bf16[448,256]{1,0:T(8,128)(2,1)S(1)} %add_convert_fusion.4), channel_id=1, source_target_pairs={{0,4},{4,8},{8,12},{12,14},{14,10},{10,6},{6,2},{2,0},{1,5},{5,9},... | collective-permute-start | bytes 688136 | tf_op jit(solution)/shard_map/ppermute | solution.py:27
  59.5 7.2 %collective-permute-start.18 = (bf16[448,256]{1,0:T(8,128)(2,1)S(1)}, bf16[448,256]{1,0:T(8,128)(2,1)S(1)}, u32[]{:S(2)}, u32[]{:S(2)}) collective-permute-start(bf16[448,256]{1,0:T(8,128)(2,1)S(1)} %add_convert_fusion.1), channel_id=1, source_target_pairs={{0,2},{4,0},{8,4},{12,8},{14,12},{10,14},{6,10},{2,6},{1,3},{5,1},... | collective-permute-start | bytes 688136 | tf_op jit(solution)/shard_map/ppermute | solution.py:27
  64.8 9.1 %collective-permute-start.16 = (bf16[448,256]{1,0:T(8,128)(2,1)S(1)}, bf16[448,256]{1,0:T(8,128)(2,1)S(1)}, u32[]{:S(2)}, u32[]{:S(2)}) collective-permute-start(bf16[448,256]{1,0:T(8,128)(2,1)S(1)} %add_convert_fusion.3), channel_id=1, source_target_pairs={{0,4},{4,8},{8,12},{12,14},{14,10},{10,6},{6,2},{2,0},{1,5},{5,9},... | collective-permute-start | bytes 688136 | tf_op jit(solution)/shard_map/ppermute | solution.py:27
  66.8 7.1 %collective-permute-start.19 = (bf16[448,256]{1,0:T(8,128)(2,1)S(1)}, bf16[448,256]{1,0:T(8,128)(2,1)S(1)}, u32[]{:S(2)}, u32[]{:S(2)}) collective-permute-start(bf16[448,256]{1,0:T(8,128)(2,1)S(1)} %add_convert_fusion), channel_id=1, source_target_pairs={{0,2},{4,0},{8,4},{12,8},{14,12},{10,14},{6,10},{2,6},{1,3},{5,1},... | collective-permute-start | bytes 688136 | tf_op jit(solution)/shard_map/ppermute | solution.py:27
  67.1 6.8 %copy-start.7 = (bf16[448,256]{1,0:T(8,128)(2,1)S(1)}, bf16[448,256]{1,0:T(8,128)(2,1)}, u32[]{:S(2)}) copy-start(bf16[448,256]{1,0:T(8,128)(2,1)} %out_grad.3) | copy-start | bytes 688132
  67.1 5.8 %collective-permute-start.25 = (bf16[128,256]{1,0:T(8,128)(2,1)S(1)}, bf16[128,256]{1,0:T(8,128)(2,1)S(1)}, u32[]{:S(2)}, u32[]{:S(2)}) collective-permute-start(bf16[128,256]{1,0:T(8,128)(2,1)S(1)} %add_convert_fusion.6.own_part), channel_id=1, source_target_pairs={{0,3},{1,2},{2,1},{3,0},{4,7},{5,6},{6,5},{7,4},{8,11},{9,10},{10,... | collective-permute-start | bytes 196616 | tf_op jit(solution)/shard_map/ppermute | solution.py:37
  67.1 5.8 %collective-permute-start.24 = (bf16[128,256]{1,0:T(8,128)(2,1)S(1)}, bf16[128,256]{1,0:T(8,128)(2,1)S(1)}, u32[]{:S(2)}, u32[]{:S(2)}) collective-permute-start(bf16[128,256]{1,0:T(8,128)(2,1)S(1)} %add_convert_fusion.6.own_part), channel_id=1, source_target_pairs={{0,1},{1,0},{2,3},{3,2},{4,5},{5,4},{6,7},{7,6},{8,9},{9,8},{10,11... | collective-permute-start | bytes 196616 | tf_op jit(solution)/shard_map/ppermute | solution.py:31
  69.0 4.9 %collective-permute-start.23 = (bf16[128,256]{1,0:T(8,128)(2,1)S(1)}, bf16[128,256]{1,0:T(8,128)(2,1)S(1)}, u32[]{:S(2)}, u32[]{:S(2)}) collective-permute-start(bf16[128,256]{1,0:T(8,128)(2,1)S(1)} %add_convert_fusion.6.own_part), channel_id=1, source_target_pairs={{0,2},{1,3},{2,0},{3,1},{4,6},{5,7},{6,4},{7,5},{8,10},{9,11},{10,... | collective-permute-start | bytes 196616 | tf_op jit(solution)/shard_map/ppermute | solution.py:37

commit v4 on v3

--- a/solution.py
+++ b/solution.py
@@ -31,10 +31,8 @@
     return lax.ppermute(block, "rep", [(0, 1), (1, 0)])
 
 
-def swapped(block, distance, across=False):
-    axes, flip = ("grid", "rep"), 2 * distance + int(across)
-    route = [(device, device ^ flip) for device in range(2 * lax.axis_size("grid"))]
-    return lax.ppermute(block, axes, route)
+def swapped(block, distance):
+    return lax.ppermute(block, "grid", [(i, i ^ distance) for i in range(lax.axis_size("grid"))])
 
 
 def call(kernel, out_shape, smem, vmem, scratch=(), flops=0, space=pltpu.VMEM):
@@ -85,9 +83,15 @@
     ]
 
 
-def flip_kernel(tile, flipped):
+def split_kernel(place, tile, sent_rows, own_flipped, sent_flipped, flipped):
+    half = sent_rows.shape[1]
+    own = pl.ds(pl.multiple_of(place[0] * half, half), half)
+    other = pl.ds(pl.multiple_of((1 - place[0]) * half, half), half)
     for slot in range(tile.shape[0]):
-        flipped[slot] = jnp.swapaxes(tile[slot], 0, 1)
+        sent_rows[slot] = tile[slot, other, :]
+        flipped[...] = jnp.swapaxes(tile[slot], 0, 1)
+        own_flipped[slot] = flipped[own, :]
+        sent_flipped[slot] = flipped[other, :]
 
 
 def pick_kernel(size, offsets, place, own_table, other_table, *refs):
@@ -147,12 +151,12 @@
         rows[slot, pl.ds(other_start, half), :] = other_rows[slot]
     total = jnp.zeros((half, width), F32)
     for slot in range(slots):
-        for tile, table, which in (
-            (own_tile, own_table, core),
-            (other_tile, other_table, 1 - core),
+        for tile_rows, table, which in (
+            (own_tile[slot, pl.ds(own_start, half), :], own_table, core),
+            (other_tile[slot], other_table, 1 - core),
         ):
             total += table[1, slot].astype(F32) * jnp.dot(
-                tile[slot, pl.ds(own_start, half), :],
+                tile_rows,
                 rows[which * slots + slot],
                 preferred_element_type=F32,
             )
@@ -208,10 +212,9 @@
     *rest,
 ):
     terms, full_grad = rest[:-1], rest[-1]
-    slots, half = own_flipped.shape[0], products.shape[1]
+    slots, half, _ = own_flipped.shape
     core = place[0]
-    own = pl.ds(pl.multiple_of(core * half, half), half)
-    full_grad[own, :] = own_packed[:half]
+    full_grad[pl.ds(pl.multiple_of(core * half, half), half), :] = own_packed[:half]
     full_grad[pl.ds(pl.multiple_of((1 - core) * half, half), half), :] = other_packed[:half]
     middle = half + kept.shape[0]
     weight_part[...] = (
@@ -223,7 +226,7 @@
     ):
         for slot in range(slots):
             products[which * slots + slot] = table[1, slot].astype(F32) * jnp.dot(
-                flipped[slot, own, :], full_grad[...], preferred_element_type=F32
+                flipped[slot], full_grad[...], preferred_element_type=F32
             )
     chosen = distances(place, own_table, other_table, size)
     total = gathered(chosen, products, size // 2)
@@ -269,19 +272,16 @@
     down,
     weight,
     out_grad,
-    own_part,
-    own_swapped,
-    other_part,
-    other_swapped,
+    own_total,
+    other_total,
     result,
     weight_grad,
 ):
     grad_msg = (own[...] + up[...].astype(F32) + down[...].astype(F32)).astype(BF16)
     back = lax.dot_general(grad_msg, weight[...], NT, preferred_element_type=F32)
     result[...] = (out_grad[...].astype(F32) + back).astype(BF16)
-    half = own_part.shape[0]
-    upper = own_part[...].astype(F32) + own_swapped[...].astype(F32)
-    lower = other_part[...].astype(F32) + other_swapped[...].astype(F32)
+    half = own_total.shape[0]
+    upper, lower = own_total[...], other_total[...]
     weight_grad[:half] = jnp.where(place[0] == 0, upper, lower)
     weight_grad[half:] = jnp.where(place[0] == 0, lower, upper)
 
@@ -303,11 +303,9 @@
     own_feats = lax.dynamic_slice_in_dim(feats, core * half, half, 0)
 
     place = jnp.stack([core, chip]).astype(jnp.int32)
-    tile_own, _ = lax.optimization_barrier((tiles[0, 0], own_feats))
+    tile_own = tiles[0, 0]
     own_table = jnp.stack([tile_step[0, 0], tile_count[0, 0]])
     other_table = other_core(own_table)
-    tile_other = other_core(tile_own)
-    flip = functools.partial(call, flip_kernel, struct(tile_own.shape, BF16), ())
 
     mask, grad_hidden = call(
         prepare_kernel,
@@ -324,11 +322,24 @@
             up, down, other_table = lax.optimization_barrier((up, down, other_table))
         if step == 3:
             up, down, mask, grad_hidden = lax.optimization_barrier((up, down, mask, grad_hidden))
-        up, down = along_ring(up, order, 1), along_ring(down, order, -1)
+        if step == min(3, far - 1):
+            tile_late = lax.optimization_barrier((tile_own, up, down))[0]
+            sent_rows, flipped_own, sent_flipped = call(
+                split_kernel,
+                [struct((slots, half, block), BF16)] * 3,
+                (place,),
+                (tile_late,),
+                (pltpu.VMEM((block, block), BF16),),
+            )
+            tile_other = other_core(sent_rows)
+        if step % 2:
+            up, down = along_ring(up, order, 1), along_ring(down, order, -1)
+        else:
+            down, up = along_ring(down, order, -1), along_ring(up, order, 1)
         arrived += [(size - step, 0, up), (step, 0, down)]
     tables = (place, own_table, other_table)
+    arrived += [(far, cut, along_ring(down[cut:], order, -1))]
     arrived += [(far, 0, along_ring(up[:cut], order, 1))]
-    arrived += [(far, cut, along_ring(down[cut:], order, -1))]
     source_rows = call(
         functools.partial(pick_kernel, size, [item[:2] for item in arrived]),
         struct((2 * slots, half, width), BF16),
@@ -336,8 +347,7 @@
         [piece for _, _, piece in arrived],
     )
     other_rows = other_core(source_rows)
-    late_own, late_other, _ = lax.optimization_barrier((tile_own, tile_other, source_rows))
-    flipped_own, flipped_other = flip((late_own,)), flip((late_other,))
+    flipped_other = other_core(lax.optimization_barrier((sent_flipped, other_rows))[0])
 
     hidden, packed, kept = call(
         middle_kernel,
@@ -395,23 +405,33 @@
     )
     terms = dict(zip(near + keys, terms, strict=True))
 
+    def added(mine, theirs):
+        values = [mine.astype(F32)] + [item.astype(F32) for item in theirs]
+        while len(values) > 1:
+            values = [values[i] + values[i + 1] for i in range(0, len(values), 2)]
+        return values[0]
+
     def joined(received, term):
         return (received.astype(F32) + term.astype(F32)).astype(BF16)
 
-    swap = size // 2
-    while swap > 4:
-        mine = joined(mine, swapped(mine, swap))
-        swap //= 2
-    four = (swapped(mine, swap), swapped(mine, swap // 2), swapped(mine, swap + swap // 2))
+    swaps = [(1, 2, 3)] + [(1 << bit,) for bit in range(2, size.bit_length() - 1)]
+    theirs = [swapped(mine, distance) for distance in swaps.pop(0)]
+    total = None
     up, down = jnp.pad(up, ((0, half - cut), (0, 0))), jnp.pad(down, ((cut, 0), (0, 0)))
     for step in range(far - 1, 0, -1):
         up, down = joined(up, terms[step]), joined(down, terms[size - step])
-        if step == 1:
-            *four, _, _ = lax.optimization_barrier((*four, up, down))
-            four = [item.astype(F32) for item in (mine, *four)]
-            mine = ((four[0] + four[1]) + (four[2] + four[3])).astype(BF16)
-            weight_parts = (mine, swapped(mine, 1), other_core(mine), swapped(mine, 1, across=True))
-        up, down = along_ring(up, order, 1), along_ring(down, order, -1)
+        if step < far - 1 and total is None:
+            *theirs, _, _ = lax.optimization_barrier((*theirs, up, down))
+            total = added(mine, theirs)
+            if swaps:
+                mine, total = total.astype(BF16), None
+                theirs = [swapped(mine, distance) for distance in swaps.pop(0)]
+            else:
+                other_total = other_core(total)
+        if step % 2:
+            down, up = along_ring(down, order, -1), along_ring(up, order, 1)
+        else:
+            up, down = along_ring(up, order, 1), along_ring(down, order, -1)
         if step == far - 1:
             hidden = lax.optimization_barrier((hidden, up))[0]
 
@@ -432,7 +452,8 @@
             down,
             msg_weight,
             out_grad,
-            *weight_parts,
+            total,
+            other_total,
         ),
     )
     return (updated, feats_grad, msg_weight_grad)

time: 75.7 us -> 73.2 us (0.967)
  waiting for transfers between devices: 28.1 us -> 26.6 us
  starting transfers between devices: 26.6 us -> 25.4 us
    ppermute x16, waiting for transfers between devices: 21.9 us -> 19.1 us  [along_ring(): return lax.ppermute(block, 'grid', route)]
    ppermute x5 -> x6, starting transfers between devices: 2.77 us -> 0.86 us  [other_core(): return lax.ppermute(block, 'rep', [(0, 1), (1, 0)])]
    ppermute x5 -> x4, starting transfers between devices: 4.74 us -> 5.92 us  [swapped(): lax.ppermute(block, 'grid', [(i, i ^ distance) for i in range(lax.axis_si...]
    ppermute x5 -> x6, waiting for transfers between devices: 3.46 us -> 4.24 us  [other_core(): return lax.ppermute(block, 'rep', [(0, 1), (1, 0)])]
    ppermute x5 -> x4, waiting for transfers between devices: 2.76 us -> 3.23 us  [swapped(): lax.ppermute(block, 'grid', [(i, i ^ distance) for i in range(lax.axis_si...]
    pallas_call x9 -> x8, Pallas kernels: 14 us -> 14.1 us  [call(): pl.pallas_call(kernel, out_shape=out_shape, in_specs=[pl.BlockSpec(memory...]
  transfers between devices with their start and end apart: 26 -> 26, of which waited for: 14 -> 13; matrix products, arithmetic and copies ran while one was open for 1% -> 1% of each run, Pallas kernels for 9% -> 15%
where the time goes in v4:
time: 73.2 us; the launch traced here: 72.9 us
  waiting for transfers between devices  26.6 us (36%)
  starting transfers between devices  25.4 us (35%)
  Pallas kernels  14.1 us (19%)
  local copies, waits for them, and re-layouts  4.28 us (6%)
  between operations  2.15 us (3%)
    ppermute x16, waiting for transfers between devices, along_ring(): return lax.ppermute(block, 'grid', route)  19.1 us
    ppermute x16, starting transfers between devices, along_ring(): return lax.ppermute(block, 'grid', route)  18.6 us
    pallas_call x8, Pallas kernels, call(): pl.pallas_call(kernel, out_shape=out_shape, in_specs=[pl.BlockSpec(memory...  14.1 us
    ppermute x4, starting transfers between devices, swapped(): lax.ppermute(block, 'grid', [(i, i ^ distance) for i in range(lax.axis_si...  5.92 us
    unnamed x18, local copies, waits for them, and re-layouts  4.25 us
    ppermute x6, waiting for transfers between devices, other_core(): return lax.ppermute(block, 'rep', [(0, 1), (1, 0)])  4.24 us
    ppermute x4, waiting for transfers between devices, swapped(): lax.ppermute(block, 'grid', [(i, i ^ distance) for i in range(lax.axis_si...  3.23 us
  transfers between devices with their start and end apart: 26, of which 13 were waited for; matrix products, arithmetic and copies ran while one was open for 1% of the time, Pallas kernels for 15%

profile of v4, /device:TPU:0, one launch (start us, length us, event | category | flops | bytes accessed | tf_op | source)
XLA Modules:
  0.0 72.9 jit_solution(13011325202914795488)
XLA Ops:
  0.6 0.0 copy-start
  0.6 1.0 %copy-done = bf16[896,256]{1,0:T(8,128)(2,1)S(1)} copy-done((bf16[896,256]{1,0:T(8,128)(2,1)S(1)}, bf16[896,256]{1,0:T(8,128)(2,1)}, u32[]{:S(2)}) %copy-start) | copy-done | bytes 458776
  1.7 3.0 %collective-permute-start.1 = (bf16[448,256]{1,0:T(8,128)(2,1)S(1)}, bf16[448,256]{1,0:T(8,128)(2,1)S(1)}, u32[]{:S(2)}, u32[]{:S(2)}) collective-permute-start(bf16[448,256]{1,0:T(8,128)(2,1)S(1)} %constant_dynamic-slice_fusion.refs_0_.feats), channel_id=1, source_target_pairs={{0,2},{4,0},{8,4},{12,8},{14,12},{10,14},{6,10},{2,6},{1,3},{5,1},... | collective-permute-start | bytes 688136 | tf_op jit(solution)/shard_map/ppermute | solution.py:27
  4.7 0.1 collective-permute-start
  6.1 0.1 collective-permute-start.2
  6.2 1.1 %collective-permute-done.2.other_table = s32[2,1]{1,0:T(2,128)S(1)} collective-permute-done((s32[2,1]{1,0:T(2,128)S(1)}, s32[2,1]{1,0:T(2,128)S(1)}, u32[]{:S(2)}, u32[]{:S(2)}) %collective-permute-start.2) | collective-permute-done | bytes 40 | tf_op jit(solution)/shard_map/ppermute | solution.py:31
  7.3 3.0 %collective-permute-done.1.refs_2_ = bf16[448,256]{1,0:T(8,128)(2,1)S(1)} collective-permute-done((bf16[448,256]{1,0:T(8,128)(2,1)S(1)}, bf16[448,256]{1,0:T(8,128)(2,1)S(1)}, u32[]{:S(2)}, u32[]{:S(2)}) %collective-permute-start.1) | collective-permute-done | bytes 229408 | tf_op jit(solution)/shard_map/ppermute | solution.py:27
  10.4 1.4 %collective-permute-done.refs_1_ = bf16[448,256]{1,0:T(8,128)(2,1)S(1)} collective-permute-done((bf16[448,256]{1,0:T(8,128)(2,1)S(1)}, bf16[448,256]{1,0:T(8,128)(2,1)S(1)}, u32[]{:S(2)}, u32[]{:S(2)}) %collective-permute-start) | collective-permute-done | bytes 229408 | tf_op jit(solution)/shard_map/ppermute | solution.py:27
  11.8 0.4 collective-permute-start.3
  12.2 1.6 %collective-permute-start.4 = (bf16[448,256]{1,0:T(8,128)(2,1)S(1)}, bf16[448,256]{1,0:T(8,128)(2,1)S(1)}, u32[]{:S(2)}, u32[]{:S(2)}) collective-permute-start(bf16[448,256]{1,0:T(8,128)(2,1)S(1)} %collective-permute-done.1.refs_2_), channel_id=1, source_target_pairs={{0,2},{4,0},{8,4},{12,8},{14,12},{10,14},{6,10},{2,6},{1,3},{5,1},... | collective-permute-start | bytes 688136 | tf_op jit(solution)/shard_map/ppermute | solution.py:27
  13.8 0.1 pad_add_fusion.1.place
  13.9 1.6 %copy-done.1 = bf16[8,512,256]{2,1,0:T(8,128)(2,1)S(1)} copy-done((bf16[8,512,256]{2,1,0:T(8,128)(2,1)S(1)}, bf16[8,512,256]{2,1,0:T(8,128)(2,1)}, u32[]{:S(2)}) %copy-start.1) | copy-done | bytes 2097176
  15.5 0.9 %copy-done.4 = bf16[448,256]{1,0:T(8,128)(2,1)S(1)} copy-done((bf16[448,256]{1,0:T(8,128)(2,1)S(1)}, bf16[448,256]{1,0:T(8,128)(2,1)}, u32[]{:S(2)}) %copy-start.4) | copy-done | bytes 229400
  16.4 0.7 copy-done.8
  17.1 2.1 %shard_map.112 = (bf16[8,448,256]{2,1,0:T(8,128)(2,1)S(1)}, f32[448,512]{1,0:T(8,128)S(1)}) custom-call(s32[2]{0:T(128)S(1)} %pad_add_fusion.1.place, s32[896]{0:T(1024)S(1)} %copy-done.8, bf16[448,256]{1,0:T(8,128)(2,1)S(1)} %copy-done.4, bf16[8,512,256]{2,1,0:T(8,128)(2,1)S(1)} %copy-done.1), custom_call_target="tpu_custom_call" | custom-call | flops 939524096 | bytes 5082624 | tf_op jit(solution)/shard_map/pallas_call | solution.py:42
  19.2 0.0 collective-permute-done.4.refs_4_
  19.2 0.7 collective-permute-start.6
  19.9 1.4 %collective-permute-start.7 = (bf16[448,256]{1,0:T(8,128)(2,1)S(1)}, bf16[448,256]{1,0:T(8,128)(2,1)S(1)}, u32[]{:S(2)}, u32[]{:S(2)}) collective-permute-start(bf16[448,256]{1,0:T(8,128)(2,1)S(1)} %collective-permute-done.4.refs_4_), channel_id=1, source_target_pairs={{0,2},{4,0},{8,4},{12,8},{14,12},{10,14},{6,10},{2,6},{1,3},{5,1},... | collective-permute-start | bytes 688136 | tf_op jit(solution)/shard_map/ppermute | solution.py:27
  21.3 1.2 %shard_map.113 = (bf16[1,448,896]{2,1,0:T(8,128)(2,1)S(1)}, bf16[1,448,896]{2,1,0:T(8,128)(2,1)S(1)}, bf16[1,448,896]{2,1,0:T(8,128)(2,1)S(1)}) custom-call(s32[2]{0:T(128)S(1)} %pad_add_fusion.1.place, bf16[1,896,896]{2,1,0:T(8,128)(2,1)S(1)} %bitcast.7), custom_call_target="tpu_custom_call" | custom-call | bytes 4014080 | tf_op jit(solution)/shard_map/pallas_call | solution.py:42
  22.5 0.1 collective-permute-start.5
  22.6 2.7 %collective-permute-done.6.refs_5_ = bf16[448,256]{1,0:T(8,128)(2,1)S(1)} collective-permute-done((bf16[448,256]{1,0:T(8,128)(2,1)S(1)}, bf16[448,256]{1,0:T(8,128)(2,1)S(1)}, u32[]{:S(2)}, u32[]{:S(2)}) %collective-permute-start.6) | collective-permute-done | bytes 229408 | tf_op jit(solution)/shard_map/ppermute | solution.py:27
  25.3 0.7 collective-permute-start.9
  26.0 1.5 %collective-permute-start.8 = (bf16[224,256]{1,0:T(8,128)(2,1)S(1)}, bf16[224,256]{1,0:T(8,128)(2,1)S(1)}, u32[]{:S(2)}, u32[]{:S(2)}) collective-permute-start(bf16[224,256]{1,0:T(8,128)(2,1)S(1)} %slice.8), channel_id=1, source_target_pairs={{0,2},{4,0},{8,4},{12,8},{14,12},{10,14},{6,10},{2,6},{1,3},{5,1},... | collective-permute-start | bytes 344072 | tf_op jit(solution)/shard_map/ppermute | solution.py:27
  27.4 2.7 %collective-permute-done.9.refs_8_ = bf16[224,256]{1,0:T(8,128)(2,1)S(1)} collective-permute-done((bf16[224,256]{1,0:T(8,128)(2,1)S(1)}, bf16[224,256]{1,0:T(8,128)(2,1)S(1)}, u32[]{:S(2)}, u32[]{:S(2)}) %collective-permute-start.9) | collective-permute-done | bytes 114720 | tf_op jit(solution)/shard_map/ppermute | solution.py:27
  30.1 0.7 collective-permute-done.8.refs_7_
  30.8 0.7 shard_map.114.own_rows
  31.5 0.1 collective-permute-start.10
  31.6 1.8 %collective-permute-done.10.other_rows = bf16[2,448,256]{2,1,0:T(8,128)(2,1)S(1)} collective-permute-done((bf16[2,448,256]{2,1,0:T(8,128)(2,1)S(1)}, bf16[2,448,256]{2,1,0:T(8,128)(2,1)S(1)}, u32[]{:S(2)}, u32[]{:S(2)}) %collective-permute-start.10) | collective-permute-done | bytes 458784 | tf_op jit(solution)/shard_map/ppermute | solution.py:31
  33.4 0.1 collective-permute-start.11
  33.5 0.0 collective-permute-done.5.other_tile
  33.5 4.3 %shard_map.115 = (bf16[448,512]{1,0:T(8,128)(2,1)S(1)}, bf16[704,256]{1,0:T(8,128)(2,1)S(1)}, f32[128,256]{1,0:T(8,128)S(1)}) custom-call(s32[2]{0:T(128)S(1)} %pad_add_fusion.1.place, s32[2,1]{1,0:T(2,128)S(1)} %pad_add_fusion.own_table, s32[2,1]{1,0:T(2,128)S(1)} %collective-permute-done.2.other_table, bf16[1,896,896]{2,1,0:T(8,128)(2,1)S(1)} %bitcast.8, ...), custom_call_target="tpu_custom_call" | custom-call | flops 2290089984 | bytes 9256960 | tf_op jit(solution)/shard_map/pallas_call | solution.py:42
  37.9 0.4 collective-permute-start.12
  38.3 1.3 %collective-permute-done.12.other_packed = bf16[704,256]{1,0:T(8,128)(2,1)S(1)} collective-permute-done((bf16[704,256]{1,0:T(8,128)(2,1)S(1)}, bf16[704,256]{1,0:T(8,128)(2,1)S(1)}, u32[]{:S(2)}, u32[]{:S(2)}) %collective-permute-start.12) | collective-permute-done | bytes 360480 | tf_op jit(solution)/shard_map/ppermute | solution.py:31
  39.6 1.5 %shard_map.116 = (f32[2,448,256]{2,1,0:T(8,128)S(1)}, bf16[224,256]{1,0:T(8,128)(2,1)S(1)}, bf16[224,256]{1,0:T(8,128)(2,1)S(1)}, bf16[128,256]{1,0:T(8,128)(2,1...) custom-call(s32[2]{0:T(128)S(1)} %pad_add_fusion.1.place, s32[2,1]{1,0:T(2,128)S(1)} %pad_add_fusion.own_table, ...), custom_call_target="tpu_custom_call" | custom-call | flops 411041792 | bytes 4128768 | tf_op jit(solution)/shard_map/pallas_call | solution.py:42
  41.1 1.6 %collective-permute-start.13 = (bf16[224,256]{1,0:T(8,128)(2,1)S(1)}, bf16[224,256]{1,0:T(8,128)(2,1)S(1)}, u32[]{:S(2)}, u32[]{:S(2)}) collective-permute-start(bf16[224,256]{1,0:T(8,128)(2,1)S(1)} %get-tuple-element.56), channel_id=1, source_target_pairs={{0,4},{4,8},{8,12},{12,14},{14,10},{10,6},{6,2},{2,0},{1,5},{5,9},... | collective-permute-start | bytes 344072 | tf_op jit(solution)/shard_map/ppermute | solution.py:27
  42.8 0.4 collective-permute-start.15
  43.2 2.4 %collective-permute-start.23 = (bf16[128,256]{1,0:T(8,128)(2,1)S(1)}, bf16[128,256]{1,0:T(8,128)(2,1)S(1)}, u32[]{:S(2)}, u32[]{:S(2)}) collective-permute-start(bf16[128,256]{1,0:T(8,128)(2,1)S(1)} %get-tuple-element.68), channel_id=1, source_target_pairs={{0,6},{2,4},{4,2},{6,0},{8,14},{10,12},{12,10},{14,8},{1,7},{3,5},... | collective-permute-start | bytes 196616 | tf_op jit(solution)/shard_map/ppermute | solution.py:35
  45.6 0.5 collective-permute-start.22
  46.1 0.6 collective-permute-start.21
  46.7 2.1 %collective-permute-done.15 = bf16[224,256]{1,0:T(8,128)(2,1)S(1)} collective-permute-done((bf16[224,256]{1,0:T(8,128)(2,1)S(1)}, bf16[224,256]{1,0:T(8,128)(2,1)S(1)}, u32[]{:S(2)}, u32[]{:S(2)}) %collective-permute-start.15) | collective-permute-done | bytes 114720 | tf_op jit(solution)/shard_map/ppermute | solution.py:27
  48.8 0.7 %collective-permute-start.14 = (bf16[448,256]{1,0:T(8,128)(2,1)S(1)}, bf16[448,256]{1,0:T(8,128)(2,1)S(1)}, u32[]{:S(2)}, u32[]{:S(2)}) collective-permute-start(bf16[448,256]{1,0:T(8,128)(2,1)S(1)} %add_convert_fusion.5), channel_id=1, source_target_pairs={{0,4},{4,8},{8,12},{12,14},{14,10},{10,6},{6,2},{2,0},{1,5},{5,9},... | collective-permute-start | bytes 688136 | tf_op jit(solution)/shard_map/ppermute | solution.py:27
  49.6 0.0 copy-start.2
  49.6 1.4 %collective-permute-start.18 = (bf16[448,256]{1,0:T(8,128)(2,1)S(1)}, bf16[448,256]{1,0:T(8,128)(2,1)S(1)}, u32[]{:S(2)}, u32[]{:S(2)}) collective-permute-start(bf16[448,256]{1,0:T(8,128)(2,1)S(1)} %add_convert_fusion.2), channel_id=1, source_target_pairs={{0,2},{4,0},{8,4},{12,8},{14,12},{10,14},{6,10},{2,6},{1,3},{5,1},... | collective-permute-start | bytes 688136 | tf_op jit(solution)/shard_map/ppermute | solution.py:27
  51.0 1.0 %shard_map.118 = (f32[448,256]{1,0:T(8,128)S(1)}, bf16[448,256]{1,0:T(8,128)(2,1)S(1)}, bf16[448,256]{1,0:T(8,128)(2,1)S(1)}, bf16[448,256]{1,0:T(8,128)(2,1)S(1)}, bf16[448,256]{1,0:T(8,128)(2,1)S(1)}) custom-call(s32[2]{0:T(128)S(1)} %pad_add_fusion.1.place, s32[2,1]{1,0:T(2,128)S(1)} %pad_add_fusion.own_table, ...), custom_call_target="tpu_custom_call" | custom-call | bytes 2293760 | tf_op jit(solution)/shard_map/pallas_call | solution.py:42
  52.0 3.3 %collective-permute-done.14 = bf16[448,256]{1,0:T(8,128)(2,1)S(1)} collective-permute-done((bf16[448,256]{1,0:T(8,128)(2,1)S(1)}, bf16[448,256]{1,0:T(8,128)(2,1)S(1)}, u32[]{:S(2)}, u32[]{:S(2)}) %collective-permute-start.14) | collective-permute-done | bytes 229408 | tf_op jit(solution)/shard_map/ppermute | solution.py:27
  55.3 0.1 add_convert_fusion.4
  55.3 1.1 %collective-permute-start.16 = (bf16[448,256]{1,0:T(8,128)(2,1)S(1)}, bf16[448,256]{1,0:T(8,128)(2,1)S(1)}, u32[]{:S(2)}, u32[]{:S(2)}) collective-permute-start(bf16[448,256]{1,0:T(8,128)(2,1)S(1)} %add_convert_fusion.4), channel_id=1, source_target_pairs={{0,4},{4,8},{8,12},{12,14},{14,10},{10,6},{6,2},{2,0},{1,5},{5,9},... | collective-permute-start | bytes 688136 | tf_op jit(solution)/shard_map/ppermute | solution.py:27
  56.4 0.0 collective-permute-done.18
  56.4 0.1 add_convert_fusion.1
  56.5 1.1 %collective-permute-start.19 = (bf16[448,256]{1,0:T(8,128)(2,1)S(1)}, bf16[448,256]{1,0:T(8,128)(2,1)S(1)}, u32[]{:S(2)}, u32[]{:S(2)}) collective-permute-start(bf16[448,256]{1,0:T(8,128)(2,1)S(1)} %add_convert_fusion.1), channel_id=1, source_target_pairs={{0,2},{4,0},{8,4},{12,8},{14,12},{10,14},{6,10},{2,6},{1,3},{5,1},... | collective-permute-start | bytes 688136 | tf_op jit(solution)/shard_map/ppermute | solution.py:27
  57.5 0.0 collective-permute-done.23
  57.5 0.0 collective-permute-done.22
  57.6 2.4 %collective-permute-start.24 = (bf16[128,256]{1,0:T(8,128)(2,1)S(1)}, bf16[128,256]{1,0:T(8,128)(2,1)S(1)}, u32[]{:S(2)}, u32[]{:S(2)}) collective-permute-start(bf16[128,256]{1,0:T(8,128)(2,1)S(1)} %add_convert_fusion.6), channel_id=1, source_target_pairs={{0,8},{2,10},{4,12},{6,14},{8,0},{10,2},{12,4},{14,6},{1,9},{3,11}... | collective-permute-start | bytes 196616 | tf_op jit(solution)/shard_map/ppermute | solution.py:35
  60.0 1.8 %collective-permute-done.16 = bf16[448,256]{1,0:T(8,128)(2,1)S(1)} collective-permute-done((bf16[448,256]{1,0:T(8,128)(2,1)S(1)}, bf16[448,256]{1,0:T(8,128)(2,1)S(1)}, u32[]{:S(2)}, u32[]{:S(2)}) %collective-permute-start.16) | collective-permute-done | bytes 229408 | tf_op jit(solution)/shard_map/ppermute | solution.py:27
  61.8 0.1 add_convert_fusion.3
  61.9 2.8 %collective-permute-start.17 = (bf16[448,256]{1,0:T(8,128)(2,1)S(1)}, bf16[448,256]{1,0:T(8,128)(2,1)S(1)}, u32[]{:S(2)}, u32[]{:S(2)}) collective-permute-start(bf16[448,256]{1,0:T(8,128)(2,1)S(1)} %add_convert_fusion.3), channel_id=1, source_target_pairs={{0,4},{4,8},{8,12},{12,14},{14,10},{10,6},{6,2},{2,0},{1,5},{5,9},... | collective-permute-start | bytes 688136 | tf_op jit(solution)/shard_map/ppermute | solution.py:27
  64.6 0.1 add_convert_fusion
  64.7 0.1 collective-permute-start.20
  64.8 3.2 %collective-permute-done.24 = bf16[128,256]{1,0:T(8,128)(2,1)S(1)} collective-permute-done((bf16[128,256]{1,0:T(8,128)(2,1)S(1)}, bf16[128,256]{1,0:T(8,128)(2,1)S(1)}, u32[]{:S(2)}, u32[]{:S(2)}) %collective-permute-start.24) | collective-permute-done | bytes 65568 | tf_op jit(solution)/shard_map/ppermute | solution.py:35
  68.0 0.1 collective-permute-start.25
  68.1 0.0 copy-start.5
  68.1 1.8 %shard_map.117 = bf16[448,256]{1,0:T(8,128)(2,1)} custom-call(bf16[8,448,256]{2,1,0:T(8,128)(2,1)S(1)} %get-tuple-element.43.mask, bf16[448,512]{1,0:T(8,128)(2,1)S(1)} %get-tuple-element.58.hidden, bf16[8,512,256]{2,1,0:T(8,128)(2,1)S(1)} %copy-done.2, bf16[448,256]{1,0:T(8,128)(2,1)S(1)} %constant_dynamic-slice_fusion.refs_0_.feats), custom_call_target="tpu_custom_call" | custom-call | flops 939524096 | bytes 4849664 | tf_op jit(solution)/shard_map/pallas_call | solution.py:42
  70.0 1.4 %collective-permute-done.20.down = bf16[448,256]{1,0:T(8,128)(2,1)S(1)} collective-permute-done((bf16[448,256]{1,0:T(8,128)(2,1)S(1)}, bf16[448,256]{1,0:T(8,128)(2,1)S(1)}, u32[]{:S(2)}, u32[]{:S(2)}) %collective-permute-start.20) | collective-permute-done | bytes 229408 | tf_op jit(solution)/shard_map/ppermute | solution.py:27
  71.4 1.5 %shard_map.119 = (bf16[448,256]{1,0:T(8,128)(2,1)}, f32[256,256]{1,0:T(8,128)}) custom-call(s32[2]{0:T(128)S(1)} %pad_add_fusion.1.place, f32[448,256]{1,0:T(8,128)S(1)} %get-tuple-element.62.own, bf16[448,256]{1,0:T(8,128)(2,1)S(1)} %collective-permute-done.17.up, bf16[448,256]{1,0:T(8,128)(2,1)S(1)} %collective-permute-done.20.down, ...), custom_call_target="tpu_custom_call" | custom-call | bytes 2031616 | tf_op jit(solution)/shard_map/pallas_call | solution.py:42
  (27 shorter events, 0.2 us)
Async XLA Ops:
  0.6 1.0 %copy-start = (bf16[896,256]{1,0:T(8,128)(2,1)S(1)}, bf16[896,256]{1,0:T(8,128)(2,1)}, u32[]{:S(2)}) copy-start(bf16[896,256]{1,0:T(8,128)(2,1)} %param.9) | copy-start | bytes 1376260
  1.7 8.7 %collective-permute-start.1 = (bf16[448,256]{1,0:T(8,128)(2,1)S(1)}, bf16[448,256]{1,0:T(8,128)(2,1)S(1)}, u32[]{:S(2)}, u32[]{:S(2)}) collective-permute-start(bf16[448,256]{1,0:T(8,128)(2,1)S(1)} %constant_dynamic-slice_fusion.refs_0_.feats), channel_id=1, source_target_pairs={{0,2},{4,0},{8,4},{12,8},{14,12},{10,14},{6,10},{2,6},{1,3},{5,1},... | collective-permute-start | bytes 688136 | tf_op jit(solution)/shard_map/ppermute | solution.py:27
  4.7 7.1 %collective-permute-start = (bf16[448,256]{1,0:T(8,128)(2,1)S(1)}, bf16[448,256]{1,0:T(8,128)(2,1)S(1)}, u32[]{:S(2)}, u32[]{:S(2)}) collective-permute-start(bf16[448,256]{1,0:T(8,128)(2,1)S(1)} %constant_dynamic-slice_fusion.refs_0_.feats), channel_id=1, source_target_pairs={{0,4},{4,8},{8,12},{12,14},{14,10},{10,6},{6,2},{2,0},{1,5},{5,9},... | collective-permute-start | bytes 688136 | tf_op jit(solution)/shard_map/ppermute | solution.py:27
  6.1 1.2 %collective-permute-start.2 = (s32[2,1]{1,0:T(2,128)S(1)}, s32[2,1]{1,0:T(2,128)S(1)}, u32[]{:S(2)}, u32[]{:S(2)}) collective-permute-start(s32[2,1]{1,0:T(2,128)S(1)} %pad_add_fusion.own_table), channel_id=1, source_target_pairs={{0,1},{1,0},{2,3},{3,2},{4,5},{5,4},{6,7},{7,6},{8,9},{9,8},{10,11... | collective-permute-start | bytes 32 | tf_op jit(solution)/shard_map/ppermute | solution.py:31
  11.8 7.4 %collective-permute-start.3 = (bf16[448,256]{1,0:T(8,128)(2,1)S(1)}, bf16[448,256]{1,0:T(8,128)(2,1)S(1)}, u32[]{:S(2)}, u32[]{:S(2)}) collective-permute-start(bf16[448,256]{1,0:T(8,128)(2,1)S(1)} %collective-permute-done.refs_1_), channel_id=1, source_target_pairs={{0,4},{4,8},{8,12},{12,14},{14,10},{10,6},{6,2},{2,0},{1,5},{5,9},... | collective-permute-start | bytes 688136 | tf_op jit(solution)/shard_map/ppermute | solution.py:27
  12.2 7.0 %collective-permute-start.4 = (bf16[448,256]{1,0:T(8,128)(2,1)S(1)}, bf16[448,256]{1,0:T(8,128)(2,1)S(1)}, u32[]{:S(2)}, u32[]{:S(2)}) collective-permute-start(bf16[448,256]{1,0:T(8,128)(2,1)S(1)} %collective-permute-done.1.refs_2_), channel_id=1, source_target_pairs={{0,2},{4,0},{8,4},{12,8},{14,12},{10,14},{6,10},{2,6},{1,3},{5,1},... | collective-permute-start | bytes 688136 | tf_op jit(solution)/shard_map/ppermute | solution.py:27
  13.9 1.6 %copy-start.1 = (bf16[8,512,256]{2,1,0:T(8,128)(2,1)S(1)}, bf16[8,512,256]{2,1,0:T(8,128)(2,1)}, u32[]{:S(2)}) copy-start(bf16[8,512,256]{2,1,0:T(8,128)(2,1)} %down.3) | copy-start | bytes 6291460
  15.5 0.9 %copy-start.4 = (bf16[448,256]{1,0:T(8,128)(2,1)S(1)}, bf16[448,256]{1,0:T(8,128)(2,1)}, u32[]{:S(2)}) copy-start(bf16[448,256]{1,0:T(8,128)(2,1)} %out_grad.3) | copy-start | bytes 688132
  16.4 0.7 copy-start.8
  17.1 4.2 %copy-start.3 = (bf16[1,1,1,896,896]{4,3,2,1,0:T(8,128)(2,1)S(1)}, bf16[1,1,1,896,896]{4,3,2,1,0:T(8,128)(2,1)}, u32[]{:S(2)}) copy-start(bf16[1,1,1,896,896]{4,3,2,1,0:T(8,128)(2,1)} %param.11) | copy-start | bytes 4816900
  19.2 6.1 %collective-permute-start.6 = (bf16[448,256]{1,0:T(8,128)(2,1)S(1)}, bf16[448,256]{1,0:T(8,128)(2,1)S(1)}, u32[]{:S(2)}, u32[]{:S(2)}) collective-permute-start(bf16[448,256]{1,0:T(8,128)(2,1)S(1)} %collective-permute-done.3.refs_3_), channel_id=1, source_target_pairs={{0,4},{4,8},{8,12},{12,14},{14,10},{10,6},{6,2},{2,0},{1,5},{5,9},... | collective-permute-start | bytes 688136 | tf_op jit(solution)/shard_map/ppermute | solution.py:27
  19.9 6.1 %collective-permute-start.7 = (bf16[448,256]{1,0:T(8,128)(2,1)S(1)}, bf16[448,256]{1,0:T(8,128)(2,1)S(1)}, u32[]{:S(2)}, u32[]{:S(2)}) collective-permute-start(bf16[448,256]{1,0:T(8,128)(2,1)S(1)} %collective-permute-done.4.refs_4_), channel_id=1, source_target_pairs={{0,2},{4,0},{8,4},{12,8},{14,12},{10,14},{6,10},{2,6},{1,3},{5,1},... | collective-permute-start | bytes 688136 | tf_op jit(solution)/shard_map/ppermute | solution.py:27
  21.3 12.2 %copy-start.6 = (bf16[256,256]{1,0:T(8,128)(2,1)S(1)}, bf16[256,256]{1,0:T(8,128)(2,1)}, u32[]{:S(2)}) copy-start(bf16[256,256]{1,0:T(8,128)(2,1)} %weight.3) | copy-start | bytes 393220
  21.3 12.3 %copy-start.7 = (bf16[8,256,512]{2,1,0:T(8,128)(2,1)S(1)}, bf16[8,256,512]{2,1,0:T(8,128)(2,1)}, u32[]{:S(2)}) copy-start(bf16[8,256,512]{2,1,0:T(8,128)(2,1)} %up.1) | copy-start | bytes 6291460
  22.5 11.0 %collective-permute-start.5 = (bf16[1,448,896]{2,1,0:T(8,128)(2,1)S(1)}, bf16[1,448,896]{2,1,0:T(8,128)(2,1)S(1)}, u32[]{:S(2)}, u32[]{:S(2)}) collective-permute-start(bf16[1,448,896]{2,1,0:T(8,128)(2,1)S(1)} %get-tuple-element.48), channel_id=1, source_target_pairs={{0,1},{1,0},{2,3},{3,2},{4,5},{5,4},{6,7},{7,6},{8,9},{9,8},{10,11... | collective-permute-start | bytes 2408456 | tf_op jit(solution)/shard_map/ppermute | solution.py:31
  25.3 4.8 %collective-permute-start.9 = (bf16[224,256]{1,0:T(8,128)(2,1)S(1)}, bf16[224,256]{1,0:T(8,128)(2,1)S(1)}, u32[]{:S(2)}, u32[]{:S(2)}) collective-permute-start(bf16[224,256]{1,0:T(8,128)(2,1)S(1)} %slice.9), channel_id=1, source_target_pairs={{0,4},{4,8},{8,12},{12,14},{14,10},{10,6},{6,2},{2,0},{1,5},{5,9},... | collective-permute-start | bytes 344072 | tf_op jit(solution)/shard_map/ppermute | solution.py:27
  26.0 4.8 %collective-permute-start.8 = (bf16[224,256]{1,0:T(8,128)(2,1)S(1)}, bf16[224,256]{1,0:T(8,128)(2,1)S(1)}, u32[]{:S(2)}, u32[]{:S(2)}) collective-permute-start(bf16[224,256]{1,0:T(8,128)(2,1)S(1)} %slice.8), channel_id=1, source_target_pairs={{0,2},{4,0},{8,4},{12,8},{14,12},{10,14},{6,10},{2,6},{1,3},{5,1},... | collective-permute-start | bytes 344072 | tf_op jit(solution)/shard_map/ppermute | solution.py:27
  31.5 1.9 %collective-permute-start.10 = (bf16[2,448,256]{2,1,0:T(8,128)(2,1)S(1)}, bf16[2,448,256]{2,1,0:T(8,128)(2,1)S(1)}, u32[]{:S(2)}, u32[]{:S(2)}) collective-permute-start(bf16[2,448,256]{2,1,0:T(8,128)(2,1)S(1)} %shard_map.114.own_rows), channel_id=1, source_target_pairs={{0,1},{1,0},{2,3},{3,2},{4,5},{5,4},{6,7},{7,6},{8,9},{9,8},{10,11... | collective-permute-start | bytes 1376264 | tf_op jit(solution)/shard_map/ppermute | solution.py:31
  33.4 6.2 %collective-permute-start.11 = (bf16[1,448,896]{2,1,0:T(8,128)(2,1)S(1)}, bf16[1,448,896]{2,1,0:T(8,128)(2,1)S(1)}, u32[]{:S(2)}, u32[]{:S(2)}) collective-permute-start(bf16[1,448,896]{2,1,0:T(8,128)(2,1)S(1)} %get-tuple-element.53), channel_id=1, source_target_pairs={{0,1},{1,0},{2,3},{3,2},{4,5},{5,4},{6,7},{7,6},{8,9},{9,8},{10,11... | collective-permute-start | bytes 2408456 | tf_op jit(solution)/shard_map/ppermute | solution.py:31
  37.9 1.7 %collective-permute-start.12 = (bf16[704,256]{1,0:T(8,128)(2,1)S(1)}, bf16[704,256]{1,0:T(8,128)(2,1)S(1)}, u32[]{:S(2)}, u32[]{:S(2)}) collective-permute-start(bf16[704,256]{1,0:T(8,128)(2,1)S(1)} %get-tuple-element.54.own_packed), channel_id=1, source_target_pairs={{0,1},{1,0},{2,3},{3,2},{4,5},{5,4},{6,7},{7,6},{8,9},{9,8},{10,11... | collective-permute-start | bytes 1081352 | tf_op jit(solution)/shard_map/ppermute | solution.py:31
  41.1 5.6 %collective-permute-start.13 = (bf16[224,256]{1,0:T(8,128)(2,1)S(1)}, bf16[224,256]{1,0:T(8,128)(2,1)S(1)}, u32[]{:S(2)}, u32[]{:S(2)}) collective-permute-start(bf16[224,256]{1,0:T(8,128)(2,1)S(1)} %get-tuple-element.56), channel_id=1, source_target_pairs={{0,4},{4,8},{8,12},{12,14},{14,10},{10,6},{6,2},{2,0},{1,5},{5,9},... | collective-permute-start | bytes 344072 | tf_op jit(solution)/shard_map/ppermute | solution.py:27
  42.8 6.0 %collective-permute-start.15 = (bf16[224,256]{1,0:T(8,128)(2,1)S(1)}, bf16[224,256]{1,0:T(8,128)(2,1)S(1)}, u32[]{:S(2)}, u32[]{:S(2)}) collective-permute-start(bf16[224,256]{1,0:T(8,128)(2,1)S(1)} %get-tuple-element.60), channel_id=1, source_target_pairs={{0,2},{4,0},{8,4},{12,8},{14,12},{10,14},{6,10},{2,6},{1,3},{5,1},... | collective-permute-start | bytes 344072 | tf_op jit(solution)/shard_map/ppermute | solution.py:27
  43.2 14.3 %collective-permute-start.23 = (bf16[128,256]{1,0:T(8,128)(2,1)S(1)}, bf16[128,256]{1,0:T(8,128)(2,1)S(1)}, u32[]{:S(2)}, u32[]{:S(2)}) collective-permute-start(bf16[128,256]{1,0:T(8,128)(2,1)S(1)} %get-tuple-element.68), channel_id=1, source_target_pairs={{0,6},{2,4},{4,2},{6,0},{8,14},{10,12},{12,10},{14,8},{1,7},{3,5},... | collective-permute-start | bytes 196616 | tf_op jit(solution)/shard_map/ppermute | solution.py:35
  45.6 11.9 %collective-permute-start.22 = (bf16[128,256]{1,0:T(8,128)(2,1)S(1)}, bf16[128,256]{1,0:T(8,128)(2,1)S(1)}, u32[]{:S(2)}, u32[]{:S(2)}) collective-permute-start(bf16[128,256]{1,0:T(8,128)(2,1)S(1)} %get-tuple-element.68), channel_id=1, source_target_pairs={{0,4},{2,6},{4,0},{6,2},{8,12},{10,14},{12,8},{14,10},{1,5},{3,7},... | collective-permute-start | bytes 196616 | tf_op jit(solution)/shard_map/ppermute | solution.py:35
  46.1 11.4 %collective-permute-start.21 = (bf16[128,256]{1,0:T(8,128)(2,1)S(1)}, bf16[128,256]{1,0:T(8,128)(2,1)S(1)}, u32[]{:S(2)}, u32[]{:S(2)}) collective-permute-start(bf16[128,256]{1,0:T(8,128)(2,1)S(1)} %get-tuple-element.68), channel_id=1, source_target_pairs={{0,2},{2,0},{4,6},{6,4},{8,10},{10,8},{12,14},{14,12},{1,3},{3,1},... | collective-permute-start | bytes 196616 | tf_op jit(solution)/shard_map/ppermute | solution.py:35
  48.8 6.5 %collective-permute-start.14 = (bf16[448,256]{1,0:T(8,128)(2,1)S(1)}, bf16[448,256]{1,0:T(8,128)(2,1)S(1)}, u32[]{:S(2)}, u32[]{:S(2)}) collective-permute-start(bf16[448,256]{1,0:T(8,128)(2,1)S(1)} %add_convert_fusion.5), channel_id=1, source_target_pairs={{0,4},{4,8},{8,12},{12,14},{14,10},{10,6},{6,2},{2,0},{1,5},{5,9},... | collective-permute-start | bytes 688136 | tf_op jit(solution)/shard_map/ppermute | solution.py:27
  49.6 18.5 %copy-start.2 = (bf16[8,512,256]{2,1,0:T(8,128)(2,1)S(1)}, bf16[8,512,256]{2,1,0:T(8,128)(2,1)}, u32[]{:S(2)}) copy-start(bf16[8,512,256]{2,1,0:T(8,128)(2,1)} %down.3) | copy-start | bytes 6291460
  49.6 6.8 %collective-permute-start.18 = (bf16[448,256]{1,0:T(8,128)(2,1)S(1)}, bf16[448,256]{1,0:T(8,128)(2,1)S(1)}, u32[]{:S(2)}, u32[]{:S(2)}) collective-permute-start(bf16[448,256]{1,0:T(8,128)(2,1)S(1)} %add_convert_fusion.2), channel_id=1, source_target_pairs={{0,2},{4,0},{8,4},{12,8},{14,12},{10,14},{6,10},{2,6},{1,3},{5,1},... | collective-permute-start | bytes 688136 | tf_op jit(solution)/shard_map/ppermute | solution.py:27
  55.3 6.5 %collective-permute-start.16 = (bf16[448,256]{1,0:T(8,128)(2,1)S(1)}, bf16[448,256]{1,0:T(8,128)(2,1)S(1)}, u32[]{:S(2)}, u32[]{:S(2)}) collective-permute-start(bf16[448,256]{1,0:T(8,128)(2,1)S(1)} %add_convert_fusion.4), channel_id=1, source_target_pairs={{0,4},{4,8},{8,12},{12,14},{14,10},{10,6},{6,2},{2,0},{1,5},{5,9},... | collective-permute-start | bytes 688136 | tf_op jit(solution)/shard_map/ppermute | solution.py:27
  56.5 8.2 %collective-permute-start.19 = (bf16[448,256]{1,0:T(8,128)(2,1)S(1)}, bf16[448,256]{1,0:T(8,128)(2,1)S(1)}, u32[]{:S(2)}, u32[]{:S(2)}) collective-permute-start(bf16[448,256]{1,0:T(8,128)(2,1)S(1)} %add_convert_fusion.1), channel_id=1, source_target_pairs={{0,2},{4,0},{8,4},{12,8},{14,12},{10,14},{6,10},{2,6},{1,3},{5,1},... | collective-permute-start | bytes 688136 | tf_op jit(solution)/shard_map/ppermute | solution.py:27
  57.6 10.4 %collective-permute-start.24 = (bf16[128,256]{1,0:T(8,128)(2,1)S(1)}, bf16[128,256]{1,0:T(8,128)(2,1)S(1)}, u32[]{:S(2)}, u32[]{:S(2)}) collective-permute-start(bf16[128,256]{1,0:T(8,128)(2,1)S(1)} %add_convert_fusion.6), channel_id=1, source_target_pairs={{0,8},{2,10},{4,12},{6,14},{8,0},{10,2},{12,4},{14,6},{1,9},{3,11}... | collective-permute-start | bytes 196616 | tf_op jit(solution)/shard_map/ppermute | solution.py:35
  61.9 8.1 %collective-permute-start.17 = (bf16[448,256]{1,0:T(8,128)(2,1)S(1)}, bf16[448,256]{1,0:T(8,128)(2,1)S(1)}, u32[]{:S(2)}, u32[]{:S(2)}) collective-permute-start(bf16[448,256]{1,0:T(8,128)(2,1)S(1)} %add_convert_fusion.3), channel_id=1, source_target_pairs={{0,4},{4,8},{8,12},{12,14},{14,10},{10,6},{6,2},{2,0},{1,5},{5,9},... | collective-permute-start | bytes 688136 | tf_op jit(solution)/shard_map/ppermute | solution.py:27
  64.7 6.7 %collective-permute-start.20 = (bf16[448,256]{1,0:T(8,128)(2,1)S(1)}, bf16[448,256]{1,0:T(8,128)(2,1)S(1)}, u32[]{:S(2)}, u32[]{:S(2)}) collective-permute-start(bf16[448,256]{1,0:T(8,128)(2,1)S(1)} %add_convert_fusion), channel_id=1, source_target_pairs={{0,2},{4,0},{8,4},{12,8},{14,12},{10,14},{6,10},{2,6},{1,3},{5,1},... | collective-permute-start | bytes 688136 | tf_op jit(solution)/shard_map/ppermute | solution.py:27
  68.0 1.9 %collective-permute-start.25 = (f32[128,256]{1,0:T(8,128)S(1)}, f32[128,256]{1,0:T(8,128)S(1)}, u32[]{:S(2)}, u32[]{:S(2)}) collective-permute-start(f32[128,256]{1,0:T(8,128)S(1)} %convert_add_fusion.own_total), channel_id=1, source_target_pairs={{0,1},{1,0},{2,3},{3,2},{4,5},{5,4},{6,7},{7,6},{8,9},{9,8},{10,11... | collective-permute-start | bytes 393224 | tf_op jit(solution)/shard_map/ppermute | solution.py:31
  68.1 3.3 %copy-start.5 = (bf16[448,256]{1,0:T(8,128)(2,1)S(1)}, bf16[448,256]{1,0:T(8,128)(2,1)}, u32[]{:S(2)}) copy-start(bf16[448,256]{1,0:T(8,128)(2,1)} %out_grad.3) | copy-start | bytes 688132

commit v5 on v4

--- a/solution.py
+++ b/solution.py
@@ -265,21 +265,13 @@
     updated[...] = total.astype(BF16)
 
 
-def finish_kernel(
-    place,
-    own,
-    up,
-    down,
-    weight,
-    out_grad,
-    own_total,
-    other_total,
-    result,
-    weight_grad,
-):
+def finish_kernel(own, up, down, weight, out_grad, result):
     grad_msg = (own[...] + up[...].astype(F32) + down[...].astype(F32)).astype(BF16)
     back = lax.dot_general(grad_msg, weight[...], NT, preferred_element_type=F32)
     result[...] = (out_grad[...].astype(F32) + back).astype(BF16)
+
+
+def weight_kernel(place, own_total, other_total, weight_grad):
     half = own_total.shape[0]
     upper, lower = own_total[...], other_total[...]
     weight_grad[:half] = jnp.where(place[0] == 0, upper, lower)
@@ -421,7 +413,8 @@
     for step in range(far - 1, 0, -1):
         up, down = joined(up, terms[step]), joined(down, terms[size - step])
         if step < far - 1 and total is None:
-            *theirs, _, _ = lax.optimization_barrier((*theirs, up, down))
+            behind = (up, down) if step < far - 2 else (terms[step], terms[size - step])
+            *theirs, _, _ = lax.optimization_barrier((*theirs, *behind))
             total = added(mine, theirs)
             if swaps:
                 mine, total = total.astype(BF16), None
@@ -442,19 +435,15 @@
         (mask, hidden, expert_down, own_feats),
         flops=2 * experts * half * width * inner,
     )
-    feats_grad, msg_weight_grad = call(
+    msg_weight_grad = call(
+        weight_kernel, struct((width, width), F32), (place,), (total, other_total)
+    )
+    feats_grad = call(
         finish_kernel,
-        [struct((half, width), BF16), struct((width, width), F32)],
-        (place,),
-        (
-            terms[0],
-            up,
-            down,
-            msg_weight,
-            out_grad,
-            total,
-            other_total,
-        ),
+        struct((half, width), BF16),
+        (),
+        (terms[0], up, down, msg_weight, out_grad),
+        flops=2 * half * width * width,
     )
     return (updated, feats_grad, msg_weight_grad)
 

time: 73.2 us -> 71 us (0.970)
  waiting for transfers between devices: 26.6 us -> 24.2 us
    ppermute x4, waiting for transfers between devices: 3.23 us -> 0.01 us  [swapped(): lax.ppermute(block, 'grid', [(i, i ^ distance) for i in range(lax.axis_si...]
    ppermute x16, waiting for transfers between devices: 19.1 us -> 19.9 us  [along_ring(): return lax.ppermute(block, 'grid', route)]
    pallas_call x8 -> x9, Pallas kernels: 14.1 us -> 14.8 us  [call(): pl.pallas_call(kernel, out_shape=out_shape, in_specs=[pl.BlockSpec(memory...]
  transfers between devices with their start and end apart: 26 -> 26, of which waited for: 13 -> 13; matrix products, arithmetic and copies ran while one was open for 1% -> 1% of each run, Pallas kernels for 15% -> 18%
where the time goes in v5:
time: 71 us; the launch traced here: 70.7 us
  starting transfers between devices  24.8 us (35%)
  waiting for transfers between devices  24.2 us (34%)
  Pallas kernels  14.8 us (21%)
  local copies, waits for them, and re-layouts  4.28 us (6%)
  between operations  2.17 us (3%)
    ppermute x16, waiting for transfers between devices, along_ring(): return lax.ppermute(block, 'grid', route)  19.9 us
    ppermute x16, starting transfers between devices, along_ring(): return lax.ppermute(block, 'grid', route)  17.8 us
    pallas_call x9, Pallas kernels, call(): pl.pallas_call(kernel, out_shape=out_shape, in_specs=[pl.BlockSpec(memory...  14.8 us
    ppermute x4, starting transfers between devices, swapped(): lax.ppermute(block, 'grid', [(i, i ^ distance) for i in range(lax.axis_si...  6.08 us
    unnamed x18, local copies, waits for them, and re-layouts  4.25 us
    ppermute x6, waiting for transfers between devices, other_core(): return lax.ppermute(block, 'rep', [(0, 1), (1, 0)])  4.24 us
  transfers between devices with their start and end apart: 26, of which 13 were waited for; matrix products, arithmetic and copies ran while one was open for 1% of the time, Pallas kernels for 18%

profile of v5, /device:TPU:0, one launch (start us, length us, event | category | flops | bytes accessed | tf_op | source)
XLA Modules:
  0.0 70.7 jit_solution(10117813423791519530)
XLA Ops:
  0.6 0.0 copy-start
  0.6 1.0 %copy-done = bf16[896,256]{1,0:T(8,128)(2,1)S(1)} copy-done((bf16[896,256]{1,0:T(8,128)(2,1)S(1)}, bf16[896,256]{1,0:T(8,128)(2,1)}, u32[]{:S(2)}) %copy-start) | copy-done | bytes 458776
  1.7 3.0 %collective-permute-start.1 = (bf16[448,256]{1,0:T(8,128)(2,1)S(1)}, bf16[448,256]{1,0:T(8,128)(2,1)S(1)}, u32[]{:S(2)}, u32[]{:S(2)}) collective-permute-start(bf16[448,256]{1,0:T(8,128)(2,1)S(1)} %constant_dynamic-slice_fusion.refs_0_.feats), channel_id=1, source_target_pairs={{0,2},{4,0},{8,4},{12,8},{14,12},{10,14},{6,10},{2,6},{1,3},{5,1},... | collective-permute-start | bytes 688136 | tf_op jit(solution)/shard_map/ppermute | solution.py:27
  4.7 0.1 collective-permute-start
  6.1 0.1 collective-permute-start.2
  6.2 1.1 %collective-permute-done.2.other_table = s32[2,1]{1,0:T(2,128)S(1)} collective-permute-done((s32[2,1]{1,0:T(2,128)S(1)}, s32[2,1]{1,0:T(2,128)S(1)}, u32[]{:S(2)}, u32[]{:S(2)}) %collective-permute-start.2) | collective-permute-done | bytes 40 | tf_op jit(solution)/shard_map/ppermute | solution.py:31
  7.3 3.0 %collective-permute-done.1.refs_2_ = bf16[448,256]{1,0:T(8,128)(2,1)S(1)} collective-permute-done((bf16[448,256]{1,0:T(8,128)(2,1)S(1)}, bf16[448,256]{1,0:T(8,128)(2,1)S(1)}, u32[]{:S(2)}, u32[]{:S(2)}) %collective-permute-start.1) | collective-permute-done | bytes 229408 | tf_op jit(solution)/shard_map/ppermute | solution.py:27
  10.4 1.4 %collective-permute-done.refs_1_ = bf16[448,256]{1,0:T(8,128)(2,1)S(1)} collective-permute-done((bf16[448,256]{1,0:T(8,128)(2,1)S(1)}, bf16[448,256]{1,0:T(8,128)(2,1)S(1)}, u32[]{:S(2)}, u32[]{:S(2)}) %collective-permute-start) | collective-permute-done | bytes 229408 | tf_op jit(solution)/shard_map/ppermute | solution.py:27
  11.8 0.4 collective-permute-start.3
  12.2 1.6 %collective-permute-start.4 = (bf16[448,256]{1,0:T(8,128)(2,1)S(1)}, bf16[448,256]{1,0:T(8,128)(2,1)S(1)}, u32[]{:S(2)}, u32[]{:S(2)}) collective-permute-start(bf16[448,256]{1,0:T(8,128)(2,1)S(1)} %collective-permute-done.1.refs_2_), channel_id=1, source_target_pairs={{0,2},{4,0},{8,4},{12,8},{14,12},{10,14},{6,10},{2,6},{1,3},{5,1},... | collective-permute-start | bytes 688136 | tf_op jit(solution)/shard_map/ppermute | solution.py:27
  13.8 0.1 pad_add_fusion.1.place
  13.9 1.6 %copy-done.1 = bf16[8,512,256]{2,1,0:T(8,128)(2,1)S(1)} copy-done((bf16[8,512,256]{2,1,0:T(8,128)(2,1)S(1)}, bf16[8,512,256]{2,1,0:T(8,128)(2,1)}, u32[]{:S(2)}) %copy-start.1) | copy-done | bytes 2097176
  15.5 0.9 %copy-done.4 = bf16[448,256]{1,0:T(8,128)(2,1)S(1)} copy-done((bf16[448,256]{1,0:T(8,128)(2,1)S(1)}, bf16[448,256]{1,0:T(8,128)(2,1)}, u32[]{:S(2)}) %copy-start.4) | copy-done | bytes 229400
  16.4 0.7 copy-done.8
  17.1 2.1 %shard_map.112 = (bf16[8,448,256]{2,1,0:T(8,128)(2,1)S(1)}, f32[448,512]{1,0:T(8,128)S(1)}) custom-call(s32[2]{0:T(128)S(1)} %pad_add_fusion.1.place, s32[896]{0:T(1024)S(1)} %copy-done.8, bf16[448,256]{1,0:T(8,128)(2,1)S(1)} %copy-done.4, bf16[8,512,256]{2,1,0:T(8,128)(2,1)S(1)} %copy-done.1), custom_call_target="tpu_custom_call" | custom-call | flops 939524096 | bytes 5082624 | tf_op jit(solution)/shard_map/pallas_call | solution.py:42
  19.2 0.0 collective-permute-done.4.refs_4_
  19.2 0.7 collective-permute-start.6
  19.9 1.4 %collective-permute-start.7 = (bf16[448,256]{1,0:T(8,128)(2,1)S(1)}, bf16[448,256]{1,0:T(8,128)(2,1)S(1)}, u32[]{:S(2)}, u32[]{:S(2)}) collective-permute-start(bf16[448,256]{1,0:T(8,128)(2,1)S(1)} %collective-permute-done.4.refs_4_), channel_id=1, source_target_pairs={{0,2},{4,0},{8,4},{12,8},{14,12},{10,14},{6,10},{2,6},{1,3},{5,1},... | collective-permute-start | bytes 688136 | tf_op jit(solution)/shard_map/ppermute | solution.py:27
  21.3 1.2 %shard_map.113 = (bf16[1,448,896]{2,1,0:T(8,128)(2,1)S(1)}, bf16[1,448,896]{2,1,0:T(8,128)(2,1)S(1)}, bf16[1,448,896]{2,1,0:T(8,128)(2,1)S(1)}) custom-call(s32[2]{0:T(128)S(1)} %pad_add_fusion.1.place, bf16[1,896,896]{2,1,0:T(8,128)(2,1)S(1)} %bitcast.7), custom_call_target="tpu_custom_call" | custom-call | bytes 4014080 | tf_op jit(solution)/shard_map/pallas_call | solution.py:42
  22.5 0.1 collective-permute-start.5
  22.6 2.7 %collective-permute-done.6.refs_5_ = bf16[448,256]{1,0:T(8,128)(2,1)S(1)} collective-permute-done((bf16[448,256]{1,0:T(8,128)(2,1)S(1)}, bf16[448,256]{1,0:T(8,128)(2,1)S(1)}, u32[]{:S(2)}, u32[]{:S(2)}) %collective-permute-start.6) | collective-permute-done | bytes 229408 | tf_op jit(solution)/shard_map/ppermute | solution.py:27
  25.3 0.7 collective-permute-start.9
  26.0 1.5 %collective-permute-start.8 = (bf16[224,256]{1,0:T(8,128)(2,1)S(1)}, bf16[224,256]{1,0:T(8,128)(2,1)S(1)}, u32[]{:S(2)}, u32[]{:S(2)}) collective-permute-start(bf16[224,256]{1,0:T(8,128)(2,1)S(1)} %slice.8), channel_id=1, source_target_pairs={{0,2},{4,0},{8,4},{12,8},{14,12},{10,14},{6,10},{2,6},{1,3},{5,1},... | collective-permute-start | bytes 344072 | tf_op jit(solution)/shard_map/ppermute | solution.py:27
  27.4 2.7 %collective-permute-done.9.refs_8_ = bf16[224,256]{1,0:T(8,128)(2,1)S(1)} collective-permute-done((bf16[224,256]{1,0:T(8,128)(2,1)S(1)}, bf16[224,256]{1,0:T(8,128)(2,1)S(1)}, u32[]{:S(2)}, u32[]{:S(2)}) %collective-permute-start.9) | collective-permute-done | bytes 114720 | tf_op jit(solution)/shard_map/ppermute | solution.py:27
  30.1 0.7 collective-permute-done.8.refs_7_
  30.8 0.7 shard_map.114.own_rows
  31.5 0.1 collective-permute-start.10
  31.6 1.8 %collective-permute-done.10.other_rows = bf16[2,448,256]{2,1,0:T(8,128)(2,1)S(1)} collective-permute-done((bf16[2,448,256]{2,1,0:T(8,128)(2,1)S(1)}, bf16[2,448,256]{2,1,0:T(8,128)(2,1)S(1)}, u32[]{:S(2)}, u32[]{:S(2)}) %collective-permute-start.10) | collective-permute-done | bytes 458784 | tf_op jit(solution)/shard_map/ppermute | solution.py:31
  33.4 0.1 collective-permute-start.11
  33.5 0.0 collective-permute-done.5.other_tile
  33.5 4.3 %shard_map.115 = (bf16[448,512]{1,0:T(8,128)(2,1)S(1)}, bf16[704,256]{1,0:T(8,128)(2,1)S(1)}, f32[128,256]{1,0:T(8,128)S(1)}) custom-call(s32[2]{0:T(128)S(1)} %pad_add_fusion.1.place, s32[2,1]{1,0:T(2,128)S(1)} %pad_add_fusion.own_table, s32[2,1]{1,0:T(2,128)S(1)} %collective-permute-done.2.other_table, bf16[1,896,896]{2,1,0:T(8,128)(2,1)S(1)} %bitcast.8, ...), custom_call_target="tpu_custom_call" | custom-call | flops 2290089984 | bytes 9256960 | tf_op jit(solution)/shard_map/pallas_call | solution.py:42
  37.9 0.4 collective-permute-start.12
  38.3 1.3 %collective-permute-done.12.other_packed = bf16[704,256]{1,0:T(8,128)(2,1)S(1)} collective-permute-done((bf16[704,256]{1,0:T(8,128)(2,1)S(1)}, bf16[704,256]{1,0:T(8,128)(2,1)S(1)}, u32[]{:S(2)}, u32[]{:S(2)}) %collective-permute-start.12) | collective-permute-done | bytes 360480 | tf_op jit(solution)/shard_map/ppermute | solution.py:31
  39.6 1.5 %shard_map.116 = (f32[2,448,256]{2,1,0:T(8,128)S(1)}, bf16[224,256]{1,0:T(8,128)(2,1)S(1)}, bf16[224,256]{1,0:T(8,128)(2,1)S(1)}, bf16[128,256]{1,0:T(8,128)(2,1...) custom-call(s32[2]{0:T(128)S(1)} %pad_add_fusion.1.place, s32[2,1]{1,0:T(2,128)S(1)} %pad_add_fusion.own_table, ...), custom_call_target="tpu_custom_call" | custom-call | flops 411041792 | bytes 4128768 | tf_op jit(solution)/shard_map/pallas_call | solution.py:42
  41.1 1.6 %collective-permute-start.13 = (bf16[224,256]{1,0:T(8,128)(2,1)S(1)}, bf16[224,256]{1,0:T(8,128)(2,1)S(1)}, u32[]{:S(2)}, u32[]{:S(2)}) collective-permute-start(bf16[224,256]{1,0:T(8,128)(2,1)S(1)} %get-tuple-element.54), channel_id=1, source_target_pairs={{0,4},{4,8},{8,12},{12,14},{14,10},{10,6},{6,2},{2,0},{1,5},{5,9},... | collective-permute-start | bytes 344072 | tf_op jit(solution)/shard_map/ppermute | solution.py:27
  42.8 0.4 collective-permute-start.15
  43.2 2.4 %collective-permute-start.23 = (bf16[128,256]{1,0:T(8,128)(2,1)S(1)}, bf16[128,256]{1,0:T(8,128)(2,1)S(1)}, u32[]{:S(2)}, u32[]{:S(2)}) collective-permute-start(bf16[128,256]{1,0:T(8,128)(2,1)S(1)} %get-tuple-element.66), channel_id=1, source_target_pairs={{0,6},{2,4},{4,2},{6,0},{8,14},{10,12},{12,10},{14,8},{1,7},{3,5},... | collective-permute-start | bytes 196616 | tf_op jit(solution)/shard_map/ppermute | solution.py:35
  45.6 0.5 collective-permute-start.22
  46.1 0.6 collective-permute-start.21
  46.7 2.1 %collective-permute-done.15 = bf16[224,256]{1,0:T(8,128)(2,1)S(1)} collective-permute-done((bf16[224,256]{1,0:T(8,128)(2,1)S(1)}, bf16[224,256]{1,0:T(8,128)(2,1)S(1)}, u32[]{:S(2)}, u32[]{:S(2)}) %collective-permute-start.15) | collective-permute-done | bytes 114720 | tf_op jit(solution)/shard_map/ppermute | solution.py:27
  48.8 0.1 collective-permute-start.18
  48.9 0.0 copy-start.2
  48.9 2.1 %collective-permute-start.14 = (bf16[448,256]{1,0:T(8,128)(2,1)S(1)}, bf16[448,256]{1,0:T(8,128)(2,1)S(1)}, u32[]{:S(2)}, u32[]{:S(2)}) collective-permute-start(bf16[448,256]{1,0:T(8,128)(2,1)S(1)} %add_convert_fusion.5), channel_id=1, source_target_pairs={{0,4},{4,8},{8,12},{12,14},{14,10},{10,6},{6,2},{2,0},{1,5},{5,9},... | collective-permute-start | bytes 688136 | tf_op jit(solution)/shard_map/ppermute | solution.py:27
  51.0 1.0 %shard_map.118 = (f32[448,256]{1,0:T(8,128)S(1)}, bf16[448,256]{1,0:T(8,128)(2,1)S(1)}, bf16[448,256]{1,0:T(8,128)(2,1)S(1)}, bf16[448,256]{1,0:T(8,128)(2,1)S(1)}, bf16[448,256]{1,0:T(8,128)(2,1)S(1)}) custom-call(s32[2]{0:T(128)S(1)} %pad_add_fusion.1.place, s32[2,1]{1,0:T(2,128)S(1)} %pad_add_fusion.own_table, ...), custom_call_target="tpu_custom_call" | custom-call | bytes 2293760 | tf_op jit(solution)/shard_map/pallas_call | solution.py:42
  52.0 0.0 collective-permute-done.23
  52.0 2.6 %collective-permute-start.24 = (bf16[128,256]{1,0:T(8,128)(2,1)S(1)}, bf16[128,256]{1,0:T(8,128)(2,1)S(1)}, u32[]{:S(2)}, u32[]{:S(2)}) collective-permute-start(bf16[128,256]{1,0:T(8,128)(2,1)S(1)} %add_convert_fusion.6), channel_id=1, source_target_pairs={{0,8},{2,10},{4,12},{6,14},{8,0},{10,2},{12,4},{14,6},{1,9},{3,11}... | collective-permute-start | bytes 196616 | tf_op jit(solution)/shard_map/ppermute | solution.py:35
  54.6 1.7 %collective-permute-done.18 = bf16[448,256]{1,0:T(8,128)(2,1)S(1)} collective-permute-done((bf16[448,256]{1,0:T(8,128)(2,1)S(1)}, bf16[448,256]{1,0:T(8,128)(2,1)S(1)}, u32[]{:S(2)}, u32[]{:S(2)}) %collective-permute-start.18) | collective-permute-done | bytes 229408 | tf_op jit(solution)/shard_map/ppermute | solution.py:27
  56.3 0.1 add_convert_fusion.1
  56.4 0.3 collective-permute-start.19
  56.7 0.0 collective-permute-done.14
  56.7 0.1 add_convert_fusion.4
  56.7 1.8 %collective-permute-start.16 = (bf16[448,256]{1,0:T(8,128)(2,1)S(1)}, bf16[448,256]{1,0:T(8,128)(2,1)S(1)}, u32[]{:S(2)}, u32[]{:S(2)}) collective-permute-start(bf16[448,256]{1,0:T(8,128)(2,1)S(1)} %add_convert_fusion.4), channel_id=1, source_target_pairs={{0,4},{4,8},{8,12},{12,14},{14,10},{10,6},{6,2},{2,0},{1,5},{5,9},... | collective-permute-start | bytes 688136 | tf_op jit(solution)/shard_map/ppermute | solution.py:27
  58.6 4.0 %collective-permute-done.19 = bf16[448,256]{1,0:T(8,128)(2,1)S(1)} collective-permute-done((bf16[448,256]{1,0:T(8,128)(2,1)S(1)}, bf16[448,256]{1,0:T(8,128)(2,1)S(1)}, u32[]{:S(2)}, u32[]{:S(2)}) %collective-permute-start.19) | collective-permute-done | bytes 229408 | tf_op jit(solution)/shard_map/ppermute | solution.py:27
  62.5 0.1 add_convert_fusion
  62.6 1.0 %collective-permute-start.20 = (bf16[448,256]{1,0:T(8,128)(2,1)S(1)}, bf16[448,256]{1,0:T(8,128)(2,1)S(1)}, u32[]{:S(2)}, u32[]{:S(2)}) collective-permute-start(bf16[448,256]{1,0:T(8,128)(2,1)S(1)} %add_convert_fusion), channel_id=1, source_target_pairs={{0,2},{4,0},{8,4},{12,8},{14,12},{10,14},{6,10},{2,6},{1,3},{5,1},... | collective-permute-start | bytes 688136 | tf_op jit(solution)/shard_map/ppermute | solution.py:27
  63.6 0.1 add_convert_fusion.3
  63.6 1.2 %collective-permute-start.17 = (bf16[448,256]{1,0:T(8,128)(2,1)S(1)}, bf16[448,256]{1,0:T(8,128)(2,1)S(1)}, u32[]{:S(2)}, u32[]{:S(2)}) collective-permute-start(bf16[448,256]{1,0:T(8,128)(2,1)S(1)} %add_convert_fusion.3), channel_id=1, source_target_pairs={{0,4},{4,8},{8,12},{12,14},{14,10},{10,6},{6,2},{2,0},{1,5},{5,9},... | collective-permute-start | bytes 688136 | tf_op jit(solution)/shard_map/ppermute | solution.py:27
  64.8 0.1 collective-permute-start.25
  64.9 0.0 copy-start.5
  64.9 1.8 %shard_map.117 = bf16[448,256]{1,0:T(8,128)(2,1)} custom-call(bf16[8,448,256]{2,1,0:T(8,128)(2,1)S(1)} %get-tuple-element.41.mask, bf16[448,512]{1,0:T(8,128)(2,1)S(1)} %get-tuple-element.56.hidden, bf16[8,512,256]{2,1,0:T(8,128)(2,1)S(1)} %copy-done.2, bf16[448,256]{1,0:T(8,128)(2,1)S(1)} %constant_dynamic-slice_fusion.refs_0_.feats), custom_call_target="tpu_custom_call" | custom-call | flops 939524096 | bytes 4849664 | tf_op jit(solution)/shard_map/pallas_call | solution.py:42
  66.8 1.3 %shard_map.120 = f32[256,256]{1,0:T(8,128)} custom-call(s32[2]{0:T(128)S(1)} %pad_add_fusion.1.place, f32[128,256]{1,0:T(8,128)S(1)} %convert_add_fusion.own_total, f32[128,256]{1,0:T(8,128)S(1)} %collective-permute-done.25.other_total), custom_call_target="tpu_custom_call" | custom-call | bytes 524288 | tf_op jit(solution)/shard_map/pallas_call | solution.py:42
  68.1 0.6 collective-permute-done.20.down
  68.7 1.0 %collective-permute-done.17.up = bf16[448,256]{1,0:T(8,128)(2,1)S(1)} collective-permute-done((bf16[448,256]{1,0:T(8,128)(2,1)S(1)}, bf16[448,256]{1,0:T(8,128)(2,1)S(1)}, u32[]{:S(2)}, u32[]{:S(2)}) %collective-permute-start.17) | collective-permute-done | bytes 229408 | tf_op jit(solution)/shard_map/ppermute | solution.py:27
  69.7 1.0 %shard_map.119 = bf16[448,256]{1,0:T(8,128)(2,1)} custom-call(f32[448,256]{1,0:T(8,128)S(1)} %get-tuple-element.60.own, bf16[448,256]{1,0:T(8,128)(2,1)S(1)} %collective-permute-done.17.up, bf16[448,256]{1,0:T(8,128)(2,1)S(1)} %collective-permute-done.20.down, bf16[256,256]{1,0:T(8,128)(2,1)S(1)} %copy-done.6, bf16[448,256]{1,0:T(8,128)(2,1)S(1)} %copy-done.5), custom_call_target="tpu_custom_call" | custom-call | flops 58720256 | bytes 1507328 | tf_op jit(solution)/shard_map/pallas_call | solution.py:42
  (28 shorter events, 0.2 us)
Async XLA Ops:
  0.6 1.0 %copy-start = (bf16[896,256]{1,0:T(8,128)(2,1)S(1)}, bf16[896,256]{1,0:T(8,128)(2,1)}, u32[]{:S(2)}) copy-start(bf16[896,256]{1,0:T(8,128)(2,1)} %param.9) | copy-start | bytes 1376260
  1.7 8.7 %collective-permute-start.1 = (bf16[448,256]{1,0:T(8,128)(2,1)S(1)}, bf16[448,256]{1,0:T(8,128)(2,1)S(1)}, u32[]{:S(2)}, u32[]{:S(2)}) collective-permute-start(bf16[448,256]{1,0:T(8,128)(2,1)S(1)} %constant_dynamic-slice_fusion.refs_0_.feats), channel_id=1, source_target_pairs={{0,2},{4,0},{8,4},{12,8},{14,12},{10,14},{6,10},{2,6},{1,3},{5,1},... | collective-permute-start | bytes 688136 | tf_op jit(solution)/shard_map/ppermute | solution.py:27
  4.7 7.1 %collective-permute-start = (bf16[448,256]{1,0:T(8,128)(2,1)S(1)}, bf16[448,256]{1,0:T(8,128)(2,1)S(1)}, u32[]{:S(2)}, u32[]{:S(2)}) collective-permute-start(bf16[448,256]{1,0:T(8,128)(2,1)S(1)} %constant_dynamic-slice_fusion.refs_0_.feats), channel_id=1, source_target_pairs={{0,4},{4,8},{8,12},{12,14},{14,10},{10,6},{6,2},{2,0},{1,5},{5,9},... | collective-permute-start | bytes 688136 | tf_op jit(solution)/shard_map/ppermute | solution.py:27
  6.1 1.2 %collective-permute-start.2 = (s32[2,1]{1,0:T(2,128)S(1)}, s32[2,1]{1,0:T(2,128)S(1)}, u32[]{:S(2)}, u32[]{:S(2)}) collective-permute-start(s32[2,1]{1,0:T(2,128)S(1)} %pad_add_fusion.own_table), channel_id=1, source_target_pairs={{0,1},{1,0},{2,3},{3,2},{4,5},{5,4},{6,7},{7,6},{8,9},{9,8},{10,11... | collective-permute-start | bytes 32 | tf_op jit(solution)/shard_map/ppermute | solution.py:31
  11.8 7.4 %collective-permute-start.3 = (bf16[448,256]{1,0:T(8,128)(2,1)S(1)}, bf16[448,256]{1,0:T(8,128)(2,1)S(1)}, u32[]{:S(2)}, u32[]{:S(2)}) collective-permute-start(bf16[448,256]{1,0:T(8,128)(2,1)S(1)} %collective-permute-done.refs_1_), channel_id=1, source_target_pairs={{0,4},{4,8},{8,12},{12,14},{14,10},{10,6},{6,2},{2,0},{1,5},{5,9},... | collective-permute-start | bytes 688136 | tf_op jit(solution)/shard_map/ppermute | solution.py:27
  12.2 7.0 %collective-permute-start.4 = (bf16[448,256]{1,0:T(8,128)(2,1)S(1)}, bf16[448,256]{1,0:T(8,128)(2,1)S(1)}, u32[]{:S(2)}, u32[]{:S(2)}) collective-permute-start(bf16[448,256]{1,0:T(8,128)(2,1)S(1)} %collective-permute-done.1.refs_2_), channel_id=1, source_target_pairs={{0,2},{4,0},{8,4},{12,8},{14,12},{10,14},{6,10},{2,6},{1,3},{5,1},... | collective-permute-start | bytes 688136 | tf_op jit(solution)/shard_map/ppermute | solution.py:27
  13.9 1.6 %copy-start.1 = (bf16[8,512,256]{2,1,0:T(8,128)(2,1)S(1)}, bf16[8,512,256]{2,1,0:T(8,128)(2,1)}, u32[]{:S(2)}) copy-start(bf16[8,512,256]{2,1,0:T(8,128)(2,1)} %down.3) | copy-start | bytes 6291460
  15.5 0.9 %copy-start.4 = (bf16[448,256]{1,0:T(8,128)(2,1)S(1)}, bf16[448,256]{1,0:T(8,128)(2,1)}, u32[]{:S(2)}) copy-start(bf16[448,256]{1,0:T(8,128)(2,1)} %out_grad.3) | copy-start | bytes 688132
  16.4 0.7 copy-start.8
  17.1 4.2 %copy-start.3 = (bf16[1,1,1,896,896]{4,3,2,1,0:T(8,128)(2,1)S(1)}, bf16[1,1,1,896,896]{4,3,2,1,0:T(8,128)(2,1)}, u32[]{:S(2)}) copy-start(bf16[1,1,1,896,896]{4,3,2,1,0:T(8,128)(2,1)} %param.11) | copy-start | bytes 4816900
  19.2 6.1 %collective-permute-start.6 = (bf16[448,256]{1,0:T(8,128)(2,1)S(1)}, bf16[448,256]{1,0:T(8,128)(2,1)S(1)}, u32[]{:S(2)}, u32[]{:S(2)}) collective-permute-start(bf16[448,256]{1,0:T(8,128)(2,1)S(1)} %collective-permute-done.3.refs_3_), channel_id=1, source_target_pairs={{0,4},{4,8},{8,12},{12,14},{14,10},{10,6},{6,2},{2,0},{1,5},{5,9},... | collective-permute-start | bytes 688136 | tf_op jit(solution)/shard_map/ppermute | solution.py:27
  19.9 6.1 %collective-permute-start.7 = (bf16[448,256]{1,0:T(8,128)(2,1)S(1)}, bf16[448,256]{1,0:T(8,128)(2,1)S(1)}, u32[]{:S(2)}, u32[]{:S(2)}) collective-permute-start(bf16[448,256]{1,0:T(8,128)(2,1)S(1)} %collective-permute-done.4.refs_4_), channel_id=1, source_target_pairs={{0,2},{4,0},{8,4},{12,8},{14,12},{10,14},{6,10},{2,6},{1,3},{5,1},... | collective-permute-start | bytes 688136 | tf_op jit(solution)/shard_map/ppermute | solution.py:27
  21.3 12.2 %copy-start.6 = (bf16[256,256]{1,0:T(8,128)(2,1)S(1)}, bf16[256,256]{1,0:T(8,128)(2,1)}, u32[]{:S(2)}) copy-start(bf16[256,256]{1,0:T(8,128)(2,1)} %weight.3) | copy-start | bytes 393220
  21.3 12.3 %copy-start.7 = (bf16[8,256,512]{2,1,0:T(8,128)(2,1)S(1)}, bf16[8,256,512]{2,1,0:T(8,128)(2,1)}, u32[]{:S(2)}) copy-start(bf16[8,256,512]{2,1,0:T(8,128)(2,1)} %up.1) | copy-start | bytes 6291460
  22.5 11.0 %collective-permute-start.5 = (bf16[1,448,896]{2,1,0:T(8,128)(2,1)S(1)}, bf16[1,448,896]{2,1,0:T(8,128)(2,1)S(1)}, u32[]{:S(2)}, u32[]{:S(2)}) collective-permute-start(bf16[1,448,896]{2,1,0:T(8,128)(2,1)S(1)} %get-tuple-element.46), channel_id=1, source_target_pairs={{0,1},{1,0},{2,3},{3,2},{4,5},{5,4},{6,7},{7,6},{8,9},{9,8},{10,11... | collective-permute-start | bytes 2408456 | tf_op jit(solution)/shard_map/ppermute | solution.py:31
  25.3 4.8 %collective-permute-start.9 = (bf16[224,256]{1,0:T(8,128)(2,1)S(1)}, bf16[224,256]{1,0:T(8,128)(2,1)S(1)}, u32[]{:S(2)}, u32[]{:S(2)}) collective-permute-start(bf16[224,256]{1,0:T(8,128)(2,1)S(1)} %slice.9), channel_id=1, source_target_pairs={{0,4},{4,8},{8,12},{12,14},{14,10},{10,6},{6,2},{2,0},{1,5},{5,9},... | collective-permute-start | bytes 344072 | tf_op jit(solution)/shard_map/ppermute | solution.py:27
  26.0 4.8 %collective-permute-start.8 = (bf16[224,256]{1,0:T(8,128)(2,1)S(1)}, bf16[224,256]{1,0:T(8,128)(2,1)S(1)}, u32[]{:S(2)}, u32[]{:S(2)}) collective-permute-start(bf16[224,256]{1,0:T(8,128)(2,1)S(1)} %slice.8), channel_id=1, source_target_pairs={{0,2},{4,0},{8,4},{12,8},{14,12},{10,14},{6,10},{2,6},{1,3},{5,1},... | collective-permute-start | bytes 344072 | tf_op jit(solution)/shard_map/ppermute | solution.py:27
  31.5 1.9 %collective-permute-start.10 = (bf16[2,448,256]{2,1,0:T(8,128)(2,1)S(1)}, bf16[2,448,256]{2,1,0:T(8,128)(2,1)S(1)}, u32[]{:S(2)}, u32[]{:S(2)}) collective-permute-start(bf16[2,448,256]{2,1,0:T(8,128)(2,1)S(1)} %shard_map.114.own_rows), channel_id=1, source_target_pairs={{0,1},{1,0},{2,3},{3,2},{4,5},{5,4},{6,7},{7,6},{8,9},{9,8},{10,11... | collective-permute-start | bytes 1376264 | tf_op jit(solution)/shard_map/ppermute | solution.py:31
  33.4 6.2 %collective-permute-start.11 = (bf16[1,448,896]{2,1,0:T(8,128)(2,1)S(1)}, bf16[1,448,896]{2,1,0:T(8,128)(2,1)S(1)}, u32[]{:S(2)}, u32[]{:S(2)}) collective-permute-start(bf16[1,448,896]{2,1,0:T(8,128)(2,1)S(1)} %get-tuple-element.51), channel_id=1, source_target_pairs={{0,1},{1,0},{2,3},{3,2},{4,5},{5,4},{6,7},{7,6},{8,9},{9,8},{10,11... | collective-permute-start | bytes 2408456 | tf_op jit(solution)/shard_map/ppermute | solution.py:31
  37.9 1.7 %collective-permute-start.12 = (bf16[704,256]{1,0:T(8,128)(2,1)S(1)}, bf16[704,256]{1,0:T(8,128)(2,1)S(1)}, u32[]{:S(2)}, u32[]{:S(2)}) collective-permute-start(bf16[704,256]{1,0:T(8,128)(2,1)S(1)} %get-tuple-element.52.own_packed), channel_id=1, source_target_pairs={{0,1},{1,0},{2,3},{3,2},{4,5},{5,4},{6,7},{7,6},{8,9},{9,8},{10,11... | collective-permute-start | bytes 1081352 | tf_op jit(solution)/shard_map/ppermute | solution.py:31
  41.1 5.6 %collective-permute-start.13 = (bf16[224,256]{1,0:T(8,128)(2,1)S(1)}, bf16[224,256]{1,0:T(8,128)(2,1)S(1)}, u32[]{:S(2)}, u32[]{:S(2)}) collective-permute-start(bf16[224,256]{1,0:T(8,128)(2,1)S(1)} %get-tuple-element.54), channel_id=1, source_target_pairs={{0,4},{4,8},{8,12},{12,14},{14,10},{10,6},{6,2},{2,0},{1,5},{5,9},... | collective-permute-start | bytes 344072 | tf_op jit(solution)/shard_map/ppermute | solution.py:27
  42.8 6.0 %collective-permute-start.15 = (bf16[224,256]{1,0:T(8,128)(2,1)S(1)}, bf16[224,256]{1,0:T(8,128)(2,1)S(1)}, u32[]{:S(2)}, u32[]{:S(2)}) collective-permute-start(bf16[224,256]{1,0:T(8,128)(2,1)S(1)} %get-tuple-element.58), channel_id=1, source_target_pairs={{0,2},{4,0},{8,4},{12,8},{14,12},{10,14},{6,10},{2,6},{1,3},{5,1},... | collective-permute-start | bytes 344072 | tf_op jit(solution)/shard_map/ppermute | solution.py:27
  43.2 8.7 %collective-permute-start.23 = (bf16[128,256]{1,0:T(8,128)(2,1)S(1)}, bf16[128,256]{1,0:T(8,128)(2,1)S(1)}, u32[]{:S(2)}, u32[]{:S(2)}) collective-permute-start(bf16[128,256]{1,0:T(8,128)(2,1)S(1)} %get-tuple-element.66), channel_id=1, source_target_pairs={{0,6},{2,4},{4,2},{6,0},{8,14},{10,12},{12,10},{14,8},{1,7},{3,5},... | collective-permute-start | bytes 196616 | tf_op jit(solution)/shard_map/ppermute | solution.py:35
  45.6 6.3 %collective-permute-start.22 = (bf16[128,256]{1,0:T(8,128)(2,1)S(1)}, bf16[128,256]{1,0:T(8,128)(2,1)S(1)}, u32[]{:S(2)}, u32[]{:S(2)}) collective-permute-start(bf16[128,256]{1,0:T(8,128)(2,1)S(1)} %get-tuple-element.66), channel_id=1, source_target_pairs={{0,4},{2,6},{4,0},{6,2},{8,12},{10,14},{12,8},{14,10},{1,5},{3,7},... | collective-permute-start | bytes 196616 | tf_op jit(solution)/shard_map/ppermute | solution.py:35
  46.1 5.9 %collective-permute-start.21 = (bf16[128,256]{1,0:T(8,128)(2,1)S(1)}, bf16[128,256]{1,0:T(8,128)(2,1)S(1)}, u32[]{:S(2)}, u32[]{:S(2)}) collective-permute-start(bf16[128,256]{1,0:T(8,128)(2,1)S(1)} %get-tuple-element.66), channel_id=1, source_target_pairs={{0,2},{2,0},{4,6},{6,4},{8,10},{10,8},{12,14},{14,12},{1,3},{3,1},... | collective-permute-start | bytes 196616 | tf_op jit(solution)/shard_map/ppermute | solution.py:35
  48.8 7.5 %collective-permute-start.18 = (bf16[448,256]{1,0:T(8,128)(2,1)S(1)}, bf16[448,256]{1,0:T(8,128)(2,1)S(1)}, u32[]{:S(2)}, u32[]{:S(2)}) collective-permute-start(bf16[448,256]{1,0:T(8,128)(2,1)S(1)} %add_convert_fusion.2), channel_id=1, source_target_pairs={{0,2},{4,0},{8,4},{12,8},{14,12},{10,14},{6,10},{2,6},{1,3},{5,1},... | collective-permute-start | bytes 688136 | tf_op jit(solution)/shard_map/ppermute | solution.py:27
  48.9 16.0 %copy-start.2 = (bf16[8,512,256]{2,1,0:T(8,128)(2,1)S(1)}, bf16[8,512,256]{2,1,0:T(8,128)(2,1)}, u32[]{:S(2)}) copy-start(bf16[8,512,256]{2,1,0:T(8,128)(2,1)} %down.3) | copy-start | bytes 6291460
  48.9 7.8 %collective-permute-start.14 = (bf16[448,256]{1,0:T(8,128)(2,1)S(1)}, bf16[448,256]{1,0:T(8,128)(2,1)S(1)}, u32[]{:S(2)}, u32[]{:S(2)}) collective-permute-start(bf16[448,256]{1,0:T(8,128)(2,1)S(1)} %add_convert_fusion.5), channel_id=1, source_target_pairs={{0,4},{4,8},{8,12},{12,14},{14,10},{10,6},{6,2},{2,0},{1,5},{5,9},... | collective-permute-start | bytes 688136 | tf_op jit(solution)/shard_map/ppermute | solution.py:27
  52.0 12.8 %collective-permute-start.24 = (bf16[128,256]{1,0:T(8,128)(2,1)S(1)}, bf16[128,256]{1,0:T(8,128)(2,1)S(1)}, u32[]{:S(2)}, u32[]{:S(2)}) collective-permute-start(bf16[128,256]{1,0:T(8,128)(2,1)S(1)} %add_convert_fusion.6), channel_id=1, source_target_pairs={{0,8},{2,10},{4,12},{6,14},{8,0},{10,2},{12,4},{14,6},{1,9},{3,11}... | collective-permute-start | bytes 196616 | tf_op jit(solution)/shard_map/ppermute | solution.py:35
  56.4 6.2 %collective-permute-start.19 = (bf16[448,256]{1,0:T(8,128)(2,1)S(1)}, bf16[448,256]{1,0:T(8,128)(2,1)S(1)}, u32[]{:S(2)}, u32[]{:S(2)}) collective-permute-start(bf16[448,256]{1,0:T(8,128)(2,1)S(1)} %add_convert_fusion.1), channel_id=1, source_target_pairs={{0,2},{4,0},{8,4},{12,8},{14,12},{10,14},{6,10},{2,6},{1,3},{5,1},... | collective-permute-start | bytes 688136 | tf_op jit(solution)/shard_map/ppermute | solution.py:27
  56.7 6.8 %collective-permute-start.16 = (bf16[448,256]{1,0:T(8,128)(2,1)S(1)}, bf16[448,256]{1,0:T(8,128)(2,1)S(1)}, u32[]{:S(2)}, u32[]{:S(2)}) collective-permute-start(bf16[448,256]{1,0:T(8,128)(2,1)S(1)} %add_convert_fusion.4), channel_id=1, source_target_pairs={{0,4},{4,8},{8,12},{12,14},{14,10},{10,6},{6,2},{2,0},{1,5},{5,9},... | collective-permute-start | bytes 688136 | tf_op jit(solution)/shard_map/ppermute | solution.py:27
  62.6 6.1 %collective-permute-start.20 = (bf16[448,256]{1,0:T(8,128)(2,1)S(1)}, bf16[448,256]{1,0:T(8,128)(2,1)S(1)}, u32[]{:S(2)}, u32[]{:S(2)}) collective-permute-start(bf16[448,256]{1,0:T(8,128)(2,1)S(1)} %add_convert_fusion), channel_id=1, source_target_pairs={{0,2},{4,0},{8,4},{12,8},{14,12},{10,14},{6,10},{2,6},{1,3},{5,1},... | collective-permute-start | bytes 688136 | tf_op jit(solution)/shard_map/ppermute | solution.py:27
  63.6 6.1 %collective-permute-start.17 = (bf16[448,256]{1,0:T(8,128)(2,1)S(1)}, bf16[448,256]{1,0:T(8,128)(2,1)S(1)}, u32[]{:S(2)}, u32[]{:S(2)}) collective-permute-start(bf16[448,256]{1,0:T(8,128)(2,1)S(1)} %add_convert_fusion.3), channel_id=1, source_target_pairs={{0,4},{4,8},{8,12},{12,14},{14,10},{10,6},{6,2},{2,0},{1,5},{5,9},... | collective-permute-start | bytes 688136 | tf_op jit(solution)/shard_map/ppermute | solution.py:27
  64.8 2.0 %collective-permute-start.25 = (f32[128,256]{1,0:T(8,128)S(1)}, f32[128,256]{1,0:T(8,128)S(1)}, u32[]{:S(2)}, u32[]{:S(2)}) collective-permute-start(f32[128,256]{1,0:T(8,128)S(1)} %convert_add_fusion.own_total), channel_id=1, source_target_pairs={{0,1},{1,0},{2,3},{3,2},{4,5},{5,4},{6,7},{7,6},{8,9},{9,8},{10,11... | collective-permute-start | bytes 393224 | tf_op jit(solution)/shard_map/ppermute | solution.py:31
  64.9 4.8 %copy-start.5 = (bf16[448,256]{1,0:T(8,128)(2,1)S(1)}, bf16[448,256]{1,0:T(8,128)(2,1)}, u32[]{:S(2)}) copy-start(bf16[448,256]{1,0:T(8,128)(2,1)} %out_grad.3) | copy-start | bytes 688132

commit v6 on v5

--- a/solution.py
+++ b/solution.py
@@ -17,7 +17,7 @@
 
 def ring_order(size):
     if size <= 8:
-        return list(range(0, size, 2)) + list(range(1, size, 2))[::-1]
+        return list(range(1, size, 2)) + list(range(0, size, 2))[::-1]
     return list(range(size))
 
 
@@ -57,7 +57,7 @@
 
 def ring_place(chip, size):
     if size <= 8:
-        return jnp.where(lax.rem(chip, 2) == 0, lax.div(chip, 2), size - 1 - lax.div(chip, 2))
+        return jnp.where(lax.rem(chip, 2) == 1, lax.div(chip, 2), size - 1 - lax.div(chip, 2))
     return chip
 
 

time: 71 us -> 70.8 us (level)
  transfers between devices with their start and end apart: 26 -> 26, of which waited for: 13 -> 14; matrix products, arithmetic and copies ran while one was open for 1% -> 1% of each run, Pallas kernels for 18% -> 18%
where the time goes in v6:
time: 70.8 us; the launch traced here: 70.5 us
  starting transfers between devices  24.5 us (35%)
  waiting for transfers between devices  24.3 us (34%)
  Pallas kernels  14.8 us (21%)
  local copies, waits for them, and re-layouts  4.28 us (6%)
  between operations  2.15 us (3%)
    ppermute x16, waiting for transfers between devices, along_ring(): return lax.ppermute(block, 'grid', route)  19.7 us
    ppermute x16, starting transfers between devices, along_ring(): return lax.ppermute(block, 'grid', route)  18.2 us
    pallas_call x9, Pallas kernels, call(): pl.pallas_call(kernel, out_shape=out_shape, in_specs=[pl.BlockSpec(memory...  14.8 us
    ppermute x4, starting transfers between devices, swapped(): lax.ppermute(block, 'grid', [(i, i ^ distance) for i in range(lax.axis_si...  5.39 us
    unnamed x18, local copies, waits for them, and re-layouts  4.25 us
    ppermute x6, waiting for transfers between devices, other_core(): return lax.ppermute(block, 'rep', [(0, 1), (1, 0)])  4.24 us
  transfers between devices with their start and end apart: 26, of which 14 were waited for; matrix products, arithmetic and copies ran while one was open for 1% of the time, Pallas kernels for 18%

profile of v6, /device:TPU:0, one launch (start us, length us, event | category | flops | bytes accessed | tf_op | source)
XLA Modules:
  0.0 70.5 jit_solution(18352298789681086299)
XLA Ops:
  0.6 0.0 copy-start
  0.6 1.0 %copy-done = bf16[896,256]{1,0:T(8,128)(2,1)S(1)} copy-done((bf16[896,256]{1,0:T(8,128)(2,1)S(1)}, bf16[896,256]{1,0:T(8,128)(2,1)}, u32[]{:S(2)}) %copy-start) | copy-done | bytes 458776
  1.7 3.1 %collective-permute-start.1 = (bf16[448,256]{1,0:T(8,128)(2,1)S(1)}, bf16[448,256]{1,0:T(8,128)(2,1)S(1)}, u32[]{:S(2)}, u32[]{:S(2)}) collective-permute-start(bf16[448,256]{1,0:T(8,128)(2,1)S(1)} %constant_dynamic-slice_fusion.refs_0_.feats), channel_id=1, source_target_pairs={{2,0},{6,2},{10,6},{14,10},{12,14},{8,12},{4,8},{0,4},{3,1},{7,3},... | collective-permute-start | bytes 688136 | tf_op jit(solution)/shard_map/ppermute | solution.py:27
  4.7 0.0 collective-permute-start
  6.1 0.1 collective-permute-start.2
  6.2 1.1 %collective-permute-done.2.other_table = s32[2,1]{1,0:T(2,128)S(1)} collective-permute-done((s32[2,1]{1,0:T(2,128)S(1)}, s32[2,1]{1,0:T(2,128)S(1)}, u32[]{:S(2)}, u32[]{:S(2)}) %collective-permute-start.2) | collective-permute-done | bytes 40 | tf_op jit(solution)/shard_map/ppermute | solution.py:31
  7.3 3.0 %collective-permute-done.1.refs_2_ = bf16[448,256]{1,0:T(8,128)(2,1)S(1)} collective-permute-done((bf16[448,256]{1,0:T(8,128)(2,1)S(1)}, bf16[448,256]{1,0:T(8,128)(2,1)S(1)}, u32[]{:S(2)}, u32[]{:S(2)}) %collective-permute-start.1) | collective-permute-done | bytes 229408 | tf_op jit(solution)/shard_map/ppermute | solution.py:27
  10.3 1.5 %collective-permute-done.refs_1_ = bf16[448,256]{1,0:T(8,128)(2,1)S(1)} collective-permute-done((bf16[448,256]{1,0:T(8,128)(2,1)S(1)}, bf16[448,256]{1,0:T(8,128)(2,1)S(1)}, u32[]{:S(2)}, u32[]{:S(2)}) %collective-permute-start) | collective-permute-done | bytes 229408 | tf_op jit(solution)/shard_map/ppermute | solution.py:27
  11.8 0.3 collective-permute-start.3
  12.1 1.7 %collective-permute-start.4 = (bf16[448,256]{1,0:T(8,128)(2,1)S(1)}, bf16[448,256]{1,0:T(8,128)(2,1)S(1)}, u32[]{:S(2)}, u32[]{:S(2)}) collective-permute-start(bf16[448,256]{1,0:T(8,128)(2,1)S(1)} %collective-permute-done.1.refs_2_), channel_id=1, source_target_pairs={{2,0},{6,2},{10,6},{14,10},{12,14},{8,12},{4,8},{0,4},{3,1},{7,3},... | collective-permute-start | bytes 688136 | tf_op jit(solution)/shard_map/ppermute | solution.py:27
  13.8 0.1 pad_add_fusion.1.place
  13.9 1.6 %copy-done.1 = bf16[8,512,256]{2,1,0:T(8,128)(2,1)S(1)} copy-done((bf16[8,512,256]{2,1,0:T(8,128)(2,1)S(1)}, bf16[8,512,256]{2,1,0:T(8,128)(2,1)}, u32[]{:S(2)}) %copy-start.1) | copy-done | bytes 2097176
  15.5 0.9 %copy-done.4 = bf16[448,256]{1,0:T(8,128)(2,1)S(1)} copy-done((bf16[448,256]{1,0:T(8,128)(2,1)S(1)}, bf16[448,256]{1,0:T(8,128)(2,1)}, u32[]{:S(2)}) %copy-start.4) | copy-done | bytes 229400
  16.4 0.7 copy-done.8
  17.1 2.1 %shard_map.112 = (bf16[8,448,256]{2,1,0:T(8,128)(2,1)S(1)}, f32[448,512]{1,0:T(8,128)S(1)}) custom-call(s32[2]{0:T(128)S(1)} %pad_add_fusion.1.place, s32[896]{0:T(1024)S(1)} %copy-done.8, bf16[448,256]{1,0:T(8,128)(2,1)S(1)} %copy-done.4, bf16[8,512,256]{2,1,0:T(8,128)(2,1)S(1)} %copy-done.1), custom_call_target="tpu_custom_call" | custom-call | flops 939524096 | bytes 5082624 | tf_op jit(solution)/shard_map/pallas_call | solution.py:42
  19.2 0.0 collective-permute-done.3.refs_3_
  19.3 0.6 collective-permute-start.6
  19.8 1.5 %collective-permute-start.7 = (bf16[448,256]{1,0:T(8,128)(2,1)S(1)}, bf16[448,256]{1,0:T(8,128)(2,1)S(1)}, u32[]{:S(2)}, u32[]{:S(2)}) collective-permute-start(bf16[448,256]{1,0:T(8,128)(2,1)S(1)} %collective-permute-done.4.refs_4_), channel_id=1, source_target_pairs={{2,0},{6,2},{10,6},{14,10},{12,14},{8,12},{4,8},{0,4},{3,1},{7,3},... | collective-permute-start | bytes 688136 | tf_op jit(solution)/shard_map/ppermute | solution.py:27
  21.3 1.2 %shard_map.113 = (bf16[1,448,896]{2,1,0:T(8,128)(2,1)S(1)}, bf16[1,448,896]{2,1,0:T(8,128)(2,1)S(1)}, bf16[1,448,896]{2,1,0:T(8,128)(2,1)S(1)}) custom-call(s32[2]{0:T(128)S(1)} %pad_add_fusion.1.place, bf16[1,896,896]{2,1,0:T(8,128)(2,1)S(1)} %bitcast.7), custom_call_target="tpu_custom_call" | custom-call | bytes 4014080 | tf_op jit(solution)/shard_map/pallas_call | solution.py:42
  22.5 0.1 collective-permute-start.5
  22.6 2.7 %collective-permute-done.6.refs_5_ = bf16[448,256]{1,0:T(8,128)(2,1)S(1)} collective-permute-done((bf16[448,256]{1,0:T(8,128)(2,1)S(1)}, bf16[448,256]{1,0:T(8,128)(2,1)S(1)}, u32[]{:S(2)}, u32[]{:S(2)}) %collective-permute-start.6) | collective-permute-done | bytes 229408 | tf_op jit(solution)/shard_map/ppermute | solution.py:27
  25.3 0.6 collective-permute-start.9
  25.9 0.0 collective-permute-done.7.refs_6_
  25.9 1.6 %collective-permute-start.8 = (bf16[224,256]{1,0:T(8,128)(2,1)S(1)}, bf16[224,256]{1,0:T(8,128)(2,1)S(1)}, u32[]{:S(2)}, u32[]{:S(2)}) collective-permute-start(bf16[224,256]{1,0:T(8,128)(2,1)S(1)} %slice.8), channel_id=1, source_target_pairs={{2,0},{6,2},{10,6},{14,10},{12,14},{8,12},{4,8},{0,4},{3,1},{7,3},... | collective-permute-start | bytes 344072 | tf_op jit(solution)/shard_map/ppermute | solution.py:27
  27.5 2.7 %collective-permute-done.9.refs_8_ = bf16[224,256]{1,0:T(8,128)(2,1)S(1)} collective-permute-done((bf16[224,256]{1,0:T(8,128)(2,1)S(1)}, bf16[224,256]{1,0:T(8,128)(2,1)S(1)}, u32[]{:S(2)}, u32[]{:S(2)}) %collective-permute-start.9) | collective-permute-done | bytes 114720 | tf_op jit(solution)/shard_map/ppermute | solution.py:27
  30.2 0.6 collective-permute-done.8.refs_7_
  30.8 0.7 shard_map.114.own_rows
  31.5 0.1 collective-permute-start.10
  31.5 1.8 %collective-permute-done.10.other_rows = bf16[2,448,256]{2,1,0:T(8,128)(2,1)S(1)} collective-permute-done((bf16[2,448,256]{2,1,0:T(8,128)(2,1)S(1)}, bf16[2,448,256]{2,1,0:T(8,128)(2,1)S(1)}, u32[]{:S(2)}, u32[]{:S(2)}) %collective-permute-start.10) | collective-permute-done | bytes 458784 | tf_op jit(solution)/shard_map/ppermute | solution.py:31
  33.3 0.1 collective-permute-start.11
  33.5 4.3 %shard_map.115 = (bf16[448,512]{1,0:T(8,128)(2,1)S(1)}, bf16[704,256]{1,0:T(8,128)(2,1)S(1)}, f32[128,256]{1,0:T(8,128)S(1)}) custom-call(s32[2]{0:T(128)S(1)} %pad_add_fusion.1.place, s32[2,1]{1,0:T(2,128)S(1)} %pad_add_fusion.own_table, s32[2,1]{1,0:T(2,128)S(1)} %collective-permute-done.2.other_table, bf16[1,896,896]{2,1,0:T(8,128)(2,1)S(1)} %bitcast.8, ...), custom_call_target="tpu_custom_call" | custom-call | flops 2290089984 | bytes 9256960 | tf_op jit(solution)/shard_map/pallas_call | solution.py:42
  37.8 0.4 collective-permute-start.12
  38.2 1.3 %collective-permute-done.12.other_packed = bf16[704,256]{1,0:T(8,128)(2,1)S(1)} collective-permute-done((bf16[704,256]{1,0:T(8,128)(2,1)S(1)}, bf16[704,256]{1,0:T(8,128)(2,1)S(1)}, u32[]{:S(2)}, u32[]{:S(2)}) %collective-permute-start.12) | collective-permute-done | bytes 360480 | tf_op jit(solution)/shard_map/ppermute | solution.py:31
  39.5 1.5 %shard_map.116 = (f32[2,448,256]{2,1,0:T(8,128)S(1)}, bf16[224,256]{1,0:T(8,128)(2,1)S(1)}, bf16[224,256]{1,0:T(8,128)(2,1)S(1)}, bf16[128,256]{1,0:T(8,128)(2,1...) custom-call(s32[2]{0:T(128)S(1)} %pad_add_fusion.1.place, s32[2,1]{1,0:T(2,128)S(1)} %pad_add_fusion.own_table, ...), custom_call_target="tpu_custom_call" | custom-call | flops 411041792 | bytes 4128768 | tf_op jit(solution)/shard_map/pallas_call | solution.py:42
  41.1 1.6 %collective-permute-start.13 = (bf16[224,256]{1,0:T(8,128)(2,1)S(1)}, bf16[224,256]{1,0:T(8,128)(2,1)S(1)}, u32[]{:S(2)}, u32[]{:S(2)}) collective-permute-start(bf16[224,256]{1,0:T(8,128)(2,1)S(1)} %get-tuple-element.54), channel_id=1, source_target_pairs={{2,6},{6,10},{10,14},{14,12},{12,8},{8,4},{4,0},{0,2},{3,7},{7,11}... | collective-permute-start | bytes 344072 | tf_op jit(solution)/shard_map/ppermute | solution.py:27
  42.7 0.4 collective-permute-start.15
  43.2 2.6 %collective-permute-start.23 = (bf16[128,256]{1,0:T(8,128)(2,1)S(1)}, bf16[128,256]{1,0:T(8,128)(2,1)S(1)}, u32[]{:S(2)}, u32[]{:S(2)}) collective-permute-start(bf16[128,256]{1,0:T(8,128)(2,1)S(1)} %get-tuple-element.66), channel_id=1, source_target_pairs={{0,6},{2,4},{4,2},{6,0},{8,14},{10,12},{12,10},{14,8},{1,7},{3,5},... | collective-permute-start | bytes 196616 | tf_op jit(solution)/shard_map/ppermute | solution.py:35
  45.7 0.4 collective-permute-start.22
  46.2 0.4 collective-permute-start.21
  46.6 1.2 %collective-permute-done.15 = bf16[224,256]{1,0:T(8,128)(2,1)S(1)} collective-permute-done((bf16[224,256]{1,0:T(8,128)(2,1)S(1)}, bf16[224,256]{1,0:T(8,128)(2,1)S(1)}, u32[]{:S(2)}, u32[]{:S(2)}) %collective-permute-start.15) | collective-permute-done | bytes 114720 | tf_op jit(solution)/shard_map/ppermute | solution.py:27
  47.9 0.6 collective-permute-start.18
  48.5 0.0 copy-start.2
  48.5 2.0 %collective-permute-start.14 = (bf16[448,256]{1,0:T(8,128)(2,1)S(1)}, bf16[448,256]{1,0:T(8,128)(2,1)S(1)}, u32[]{:S(2)}, u32[]{:S(2)}) collective-permute-start(bf16[448,256]{1,0:T(8,128)(2,1)S(1)} %add_convert_fusion.5), channel_id=1, source_target_pairs={{2,6},{6,10},{10,14},{14,12},{12,8},{8,4},{4,0},{0,2},{3,7},{7,11}... | collective-permute-start | bytes 688136 | tf_op jit(solution)/shard_map/ppermute | solution.py:27
  50.5 1.0 %shard_map.118 = (f32[448,256]{1,0:T(8,128)S(1)}, bf16[448,256]{1,0:T(8,128)(2,1)S(1)}, bf16[448,256]{1,0:T(8,128)(2,1)S(1)}, bf16[448,256]{1,0:T(8,128)(2,1)S(1)}, bf16[448,256]{1,0:T(8,128)(2,1)S(1)}) custom-call(s32[2]{0:T(128)S(1)} %pad_add_fusion.1.place, s32[2,1]{1,0:T(2,128)S(1)} %pad_add_fusion.own_table, ...), custom_call_target="tpu_custom_call" | custom-call | bytes 2293760 | tf_op jit(solution)/shard_map/pallas_call | solution.py:42
  51.5 0.4 collective-permute-done.21
  51.9 1.9 %collective-permute-start.24 = (bf16[128,256]{1,0:T(8,128)(2,1)S(1)}, bf16[128,256]{1,0:T(8,128)(2,1)S(1)}, u32[]{:S(2)}, u32[]{:S(2)}) collective-permute-start(bf16[128,256]{1,0:T(8,128)(2,1)S(1)} %add_convert_fusion.6), channel_id=1, source_target_pairs={{0,8},{2,10},{4,12},{6,14},{8,0},{10,2},{12,4},{14,6},{1,9},{3,11}... | collective-permute-start | bytes 196616 | tf_op jit(solution)/shard_map/ppermute | solution.py:35
  53.8 2.3 %collective-permute-done.18 = bf16[448,256]{1,0:T(8,128)(2,1)S(1)} collective-permute-done((bf16[448,256]{1,0:T(8,128)(2,1)S(1)}, bf16[448,256]{1,0:T(8,128)(2,1)S(1)}, u32[]{:S(2)}, u32[]{:S(2)}) %collective-permute-start.18) | collective-permute-done | bytes 229408 | tf_op jit(solution)/shard_map/ppermute | solution.py:27
  56.1 0.1 add_convert_fusion.1
  56.1 0.7 collective-permute-start.19
  56.8 0.1 add_convert_fusion.4
  56.9 1.4 %collective-permute-start.16 = (bf16[448,256]{1,0:T(8,128)(2,1)S(1)}, bf16[448,256]{1,0:T(8,128)(2,1)S(1)}, u32[]{:S(2)}, u32[]{:S(2)}) collective-permute-start(bf16[448,256]{1,0:T(8,128)(2,1)S(1)} %add_convert_fusion.4), channel_id=1, source_target_pairs={{2,6},{6,10},{10,14},{14,12},{12,8},{8,4},{4,0},{0,2},{3,7},{7,11}... | collective-permute-start | bytes 688136 | tf_op jit(solution)/shard_map/ppermute | solution.py:27
  58.3 4.6 %collective-permute-done.19 = bf16[448,256]{1,0:T(8,128)(2,1)S(1)} collective-permute-done((bf16[448,256]{1,0:T(8,128)(2,1)S(1)}, bf16[448,256]{1,0:T(8,128)(2,1)S(1)}, u32[]{:S(2)}, u32[]{:S(2)}) %collective-permute-start.19) | collective-permute-done | bytes 229408 | tf_op jit(solution)/shard_map/ppermute | solution.py:27
  63.0 0.1 add_convert_fusion
  63.0 0.3 collective-permute-start.20
  63.4 0.0 collective-permute-done.16
  63.4 0.1 add_convert_fusion.3
  63.4 1.8 %collective-permute-start.17 = (bf16[448,256]{1,0:T(8,128)(2,1)S(1)}, bf16[448,256]{1,0:T(8,128)(2,1)S(1)}, u32[]{:S(2)}, u32[]{:S(2)}) collective-permute-start(bf16[448,256]{1,0:T(8,128)(2,1)S(1)} %add_convert_fusion.3), channel_id=1, source_target_pairs={{2,6},{6,10},{10,14},{14,12},{12,8},{8,4},{4,0},{0,2},{3,7},{7,11}... | collective-permute-start | bytes 688136 | tf_op jit(solution)/shard_map/ppermute | solution.py:27
  65.2 0.1 collective-permute-start.25
  65.3 0.0 copy-start.5
  65.3 1.8 %shard_map.117 = bf16[448,256]{1,0:T(8,128)(2,1)} custom-call(bf16[8,448,256]{2,1,0:T(8,128)(2,1)S(1)} %get-tuple-element.41.mask, bf16[448,512]{1,0:T(8,128)(2,1)S(1)} %get-tuple-element.56.hidden, bf16[8,512,256]{2,1,0:T(8,128)(2,1)S(1)} %copy-done.2, bf16[448,256]{1,0:T(8,128)(2,1)S(1)} %constant_dynamic-slice_fusion.refs_0_.feats), custom_call_target="tpu_custom_call" | custom-call | flops 939524096 | bytes 4849664 | tf_op jit(solution)/shard_map/pallas_call | solution.py:42
  67.2 1.3 %shard_map.120 = f32[256,256]{1,0:T(8,128)} custom-call(s32[2]{0:T(128)S(1)} %pad_add_fusion.1.place, f32[128,256]{1,0:T(8,128)S(1)} %convert_add_fusion.own_total, f32[128,256]{1,0:T(8,128)S(1)} %collective-permute-done.25.other_total), custom_call_target="tpu_custom_call" | custom-call | bytes 524288 | tf_op jit(solution)/shard_map/pallas_call | solution.py:42
  68.5 0.6 collective-permute-done.20.down
  69.1 0.4 collective-permute-done.17.up
  69.5 1.0 %shard_map.119 = bf16[448,256]{1,0:T(8,128)(2,1)} custom-call(f32[448,256]{1,0:T(8,128)S(1)} %get-tuple-element.60.own, bf16[448,256]{1,0:T(8,128)(2,1)S(1)} %collective-permute-done.17.up, bf16[448,256]{1,0:T(8,128)(2,1)S(1)} %collective-permute-done.20.down, bf16[256,256]{1,0:T(8,128)(2,1)S(1)} %copy-done.6, bf16[448,256]{1,0:T(8,128)(2,1)S(1)} %copy-done.5), custom_call_target="tpu_custom_call" | custom-call | flops 58720256 | bytes 1507328 | tf_op jit(solution)/shard_map/pallas_call | solution.py:42
  (28 shorter events, 0.2 us)
Async XLA Ops:
  0.6 1.0 %copy-start = (bf16[896,256]{1,0:T(8,128)(2,1)S(1)}, bf16[896,256]{1,0:T(8,128)(2,1)}, u32[]{:S(2)}) copy-start(bf16[896,256]{1,0:T(8,128)(2,1)} %param.9) | copy-start | bytes 1376260
  1.7 8.6 %collective-permute-start.1 = (bf16[448,256]{1,0:T(8,128)(2,1)S(1)}, bf16[448,256]{1,0:T(8,128)(2,1)S(1)}, u32[]{:S(2)}, u32[]{:S(2)}) collective-permute-start(bf16[448,256]{1,0:T(8,128)(2,1)S(1)} %constant_dynamic-slice_fusion.refs_0_.feats), channel_id=1, source_target_pairs={{2,0},{6,2},{10,6},{14,10},{12,14},{8,12},{4,8},{0,4},{3,1},{7,3},... | collective-permute-start | bytes 688136 | tf_op jit(solution)/shard_map/ppermute | solution.py:27
  4.7 7.1 %collective-permute-start = (bf16[448,256]{1,0:T(8,128)(2,1)S(1)}, bf16[448,256]{1,0:T(8,128)(2,1)S(1)}, u32[]{:S(2)}, u32[]{:S(2)}) collective-permute-start(bf16[448,256]{1,0:T(8,128)(2,1)S(1)} %constant_dynamic-slice_fusion.refs_0_.feats), channel_id=1, source_target_pairs={{2,6},{6,10},{10,14},{14,12},{12,8},{8,4},{4,0},{0,2},{3,7},{7,11}... | collective-permute-start | bytes 688136 | tf_op jit(solution)/shard_map/ppermute | solution.py:27
  6.1 1.2 %collective-permute-start.2 = (s32[2,1]{1,0:T(2,128)S(1)}, s32[2,1]{1,0:T(2,128)S(1)}, u32[]{:S(2)}, u32[]{:S(2)}) collective-permute-start(s32[2,1]{1,0:T(2,128)S(1)} %pad_add_fusion.own_table), channel_id=1, source_target_pairs={{0,1},{1,0},{2,3},{3,2},{4,5},{5,4},{6,7},{7,6},{8,9},{9,8},{10,11... | collective-permute-start | bytes 32 | tf_op jit(solution)/shard_map/ppermute | solution.py:31
  11.8 7.4 %collective-permute-start.3 = (bf16[448,256]{1,0:T(8,128)(2,1)S(1)}, bf16[448,256]{1,0:T(8,128)(2,1)S(1)}, u32[]{:S(2)}, u32[]{:S(2)}) collective-permute-start(bf16[448,256]{1,0:T(8,128)(2,1)S(1)} %collective-permute-done.refs_1_), channel_id=1, source_target_pairs={{2,6},{6,10},{10,14},{14,12},{12,8},{8,4},{4,0},{0,2},{3,7},{7,11}... | collective-permute-start | bytes 688136 | tf_op jit(solution)/shard_map/ppermute | solution.py:27
  12.1 7.1 %collective-permute-start.4 = (bf16[448,256]{1,0:T(8,128)(2,1)S(1)}, bf16[448,256]{1,0:T(8,128)(2,1)S(1)}, u32[]{:S(2)}, u32[]{:S(2)}) collective-permute-start(bf16[448,256]{1,0:T(8,128)(2,1)S(1)} %collective-permute-done.1.refs_2_), channel_id=1, source_target_pairs={{2,0},{6,2},{10,6},{14,10},{12,14},{8,12},{4,8},{0,4},{3,1},{7,3},... | collective-permute-start | bytes 688136 | tf_op jit(solution)/shard_map/ppermute | solution.py:27
  13.9 1.6 %copy-start.1 = (bf16[8,512,256]{2,1,0:T(8,128)(2,1)S(1)}, bf16[8,512,256]{2,1,0:T(8,128)(2,1)}, u32[]{:S(2)}) copy-start(bf16[8,512,256]{2,1,0:T(8,128)(2,1)} %down.3) | copy-start | bytes 6291460
  15.5 0.9 %copy-start.4 = (bf16[448,256]{1,0:T(8,128)(2,1)S(1)}, bf16[448,256]{1,0:T(8,128)(2,1)}, u32[]{:S(2)}) copy-start(bf16[448,256]{1,0:T(8,128)(2,1)} %out_grad.3) | copy-start | bytes 688132
  16.4 0.7 copy-start.8
  17.1 4.2 %copy-start.3 = (bf16[1,1,1,896,896]{4,3,2,1,0:T(8,128)(2,1)S(1)}, bf16[1,1,1,896,896]{4,3,2,1,0:T(8,128)(2,1)}, u32[]{:S(2)}) copy-start(bf16[1,1,1,896,896]{4,3,2,1,0:T(8,128)(2,1)} %param.11) | copy-start | bytes 4816900
  19.3 6.1 %collective-permute-start.6 = (bf16[448,256]{1,0:T(8,128)(2,1)S(1)}, bf16[448,256]{1,0:T(8,128)(2,1)S(1)}, u32[]{:S(2)}, u32[]{:S(2)}) collective-permute-start(bf16[448,256]{1,0:T(8,128)(2,1)S(1)} %collective-permute-done.3.refs_3_), channel_id=1, source_target_pairs={{2,6},{6,10},{10,14},{14,12},{12,8},{8,4},{4,0},{0,2},{3,7},{7,11}... | collective-permute-start | bytes 688136 | tf_op jit(solution)/shard_map/ppermute | solution.py:27
  19.8 6.1 %collective-permute-start.7 = (bf16[448,256]{1,0:T(8,128)(2,1)S(1)}, bf16[448,256]{1,0:T(8,128)(2,1)S(1)}, u32[]{:S(2)}, u32[]{:S(2)}) collective-permute-start(bf16[448,256]{1,0:T(8,128)(2,1)S(1)} %collective-permute-done.4.refs_4_), channel_id=1, source_target_pairs={{2,0},{6,2},{10,6},{14,10},{12,14},{8,12},{4,8},{0,4},{3,1},{7,3},... | collective-permute-start | bytes 688136 | tf_op jit(solution)/shard_map/ppermute | solution.py:27
  21.3 12.1 %copy-start.6 = (bf16[256,256]{1,0:T(8,128)(2,1)S(1)}, bf16[256,256]{1,0:T(8,128)(2,1)}, u32[]{:S(2)}) copy-start(bf16[256,256]{1,0:T(8,128)(2,1)} %weight.3) | copy-start | bytes 393220
  21.3 12.1 %copy-start.7 = (bf16[8,256,512]{2,1,0:T(8,128)(2,1)S(1)}, bf16[8,256,512]{2,1,0:T(8,128)(2,1)}, u32[]{:S(2)}) copy-start(bf16[8,256,512]{2,1,0:T(8,128)(2,1)} %up.1) | copy-start | bytes 6291460
  22.5 10.9 %collective-permute-start.5 = (bf16[1,448,896]{2,1,0:T(8,128)(2,1)S(1)}, bf16[1,448,896]{2,1,0:T(8,128)(2,1)S(1)}, u32[]{:S(2)}, u32[]{:S(2)}) collective-permute-start(bf16[1,448,896]{2,1,0:T(8,128)(2,1)S(1)} %get-tuple-element.46), channel_id=1, source_target_pairs={{0,1},{1,0},{2,3},{3,2},{4,5},{5,4},{6,7},{7,6},{8,9},{9,8},{10,11... | collective-permute-start | bytes 2408456 | tf_op jit(solution)/shard_map/ppermute | solution.py:31
  25.3 4.8 %collective-permute-start.9 = (bf16[224,256]{1,0:T(8,128)(2,1)S(1)}, bf16[224,256]{1,0:T(8,128)(2,1)S(1)}, u32[]{:S(2)}, u32[]{:S(2)}) collective-permute-start(bf16[224,256]{1,0:T(8,128)(2,1)S(1)} %slice.9), channel_id=1, source_target_pairs={{2,6},{6,10},{10,14},{14,12},{12,8},{8,4},{4,0},{0,2},{3,7},{7,11}... | collective-permute-start | bytes 344072 | tf_op jit(solution)/shard_map/ppermute | solution.py:27
  25.9 4.8 %collective-permute-start.8 = (bf16[224,256]{1,0:T(8,128)(2,1)S(1)}, bf16[224,256]{1,0:T(8,128)(2,1)S(1)}, u32[]{:S(2)}, u32[]{:S(2)}) collective-permute-start(bf16[224,256]{1,0:T(8,128)(2,1)S(1)} %slice.8), channel_id=1, source_target_pairs={{2,0},{6,2},{10,6},{14,10},{12,14},{8,12},{4,8},{0,4},{3,1},{7,3},... | collective-permute-start | bytes 344072 | tf_op jit(solution)/shard_map/ppermute | solution.py:27
  31.5 1.9 %collective-permute-start.10 = (bf16[2,448,256]{2,1,0:T(8,128)(2,1)S(1)}, bf16[2,448,256]{2,1,0:T(8,128)(2,1)S(1)}, u32[]{:S(2)}, u32[]{:S(2)}) collective-permute-start(bf16[2,448,256]{2,1,0:T(8,128)(2,1)S(1)} %shard_map.114.own_rows), channel_id=1, source_target_pairs={{0,1},{1,0},{2,3},{3,2},{4,5},{5,4},{6,7},{7,6},{8,9},{9,8},{10,11... | collective-permute-start | bytes 1376264 | tf_op jit(solution)/shard_map/ppermute | solution.py:31
  33.3 6.2 %collective-permute-start.11 = (bf16[1,448,896]{2,1,0:T(8,128)(2,1)S(1)}, bf16[1,448,896]{2,1,0:T(8,128)(2,1)S(1)}, u32[]{:S(2)}, u32[]{:S(2)}) collective-permute-start(bf16[1,448,896]{2,1,0:T(8,128)(2,1)S(1)} %get-tuple-element.51), channel_id=1, source_target_pairs={{0,1},{1,0},{2,3},{3,2},{4,5},{5,4},{6,7},{7,6},{8,9},{9,8},{10,11... | collective-permute-start | bytes 2408456 | tf_op jit(solution)/shard_map/ppermute | solution.py:31
  37.8 1.7 %collective-permute-start.12 = (bf16[704,256]{1,0:T(8,128)(2,1)S(1)}, bf16[704,256]{1,0:T(8,128)(2,1)S(1)}, u32[]{:S(2)}, u32[]{:S(2)}) collective-permute-start(bf16[704,256]{1,0:T(8,128)(2,1)S(1)} %get-tuple-element.52.own_packed), channel_id=1, source_target_pairs={{0,1},{1,0},{2,3},{3,2},{4,5},{5,4},{6,7},{7,6},{8,9},{9,8},{10,11... | collective-permute-start | bytes 1081352 | tf_op jit(solution)/shard_map/ppermute | solution.py:31
  41.1 5.6 %collective-permute-start.13 = (bf16[224,256]{1,0:T(8,128)(2,1)S(1)}, bf16[224,256]{1,0:T(8,128)(2,1)S(1)}, u32[]{:S(2)}, u32[]{:S(2)}) collective-permute-start(bf16[224,256]{1,0:T(8,128)(2,1)S(1)} %get-tuple-element.54), channel_id=1, source_target_pairs={{2,6},{6,10},{10,14},{14,12},{12,8},{8,4},{4,0},{0,2},{3,7},{7,11}... | collective-permute-start | bytes 344072 | tf_op jit(solution)/shard_map/ppermute | solution.py:27
  42.7 5.1 %collective-permute-start.15 = (bf16[224,256]{1,0:T(8,128)(2,1)S(1)}, bf16[224,256]{1,0:T(8,128)(2,1)S(1)}, u32[]{:S(2)}, u32[]{:S(2)}) collective-permute-start(bf16[224,256]{1,0:T(8,128)(2,1)S(1)} %get-tuple-element.58), channel_id=1, source_target_pairs={{2,0},{6,2},{10,6},{14,10},{12,14},{8,12},{4,8},{0,4},{3,1},{7,3},... | collective-permute-start | bytes 344072 | tf_op jit(solution)/shard_map/ppermute | solution.py:27
  43.2 8.3 %collective-permute-start.23 = (bf16[128,256]{1,0:T(8,128)(2,1)S(1)}, bf16[128,256]{1,0:T(8,128)(2,1)S(1)}, u32[]{:S(2)}, u32[]{:S(2)}) collective-permute-start(bf16[128,256]{1,0:T(8,128)(2,1)S(1)} %get-tuple-element.66), channel_id=1, source_target_pairs={{0,6},{2,4},{4,2},{6,0},{8,14},{10,12},{12,10},{14,8},{1,7},{3,5},... | collective-permute-start | bytes 196616 | tf_op jit(solution)/shard_map/ppermute | solution.py:35
  45.7 5.7 %collective-permute-start.22 = (bf16[128,256]{1,0:T(8,128)(2,1)S(1)}, bf16[128,256]{1,0:T(8,128)(2,1)S(1)}, u32[]{:S(2)}, u32[]{:S(2)}) collective-permute-start(bf16[128,256]{1,0:T(8,128)(2,1)S(1)} %get-tuple-element.66), channel_id=1, source_target_pairs={{0,4},{2,6},{4,0},{6,2},{8,12},{10,14},{12,8},{14,10},{1,5},{3,7},... | collective-permute-start | bytes 196616 | tf_op jit(solution)/shard_map/ppermute | solution.py:35
  46.2 5.6 %collective-permute-start.21 = (bf16[128,256]{1,0:T(8,128)(2,1)S(1)}, bf16[128,256]{1,0:T(8,128)(2,1)S(1)}, u32[]{:S(2)}, u32[]{:S(2)}) collective-permute-start(bf16[128,256]{1,0:T(8,128)(2,1)S(1)} %get-tuple-element.66), channel_id=1, source_target_pairs={{0,2},{2,0},{4,6},{6,4},{8,10},{10,8},{12,14},{14,12},{1,3},{3,1},... | collective-permute-start | bytes 196616 | tf_op jit(solution)/shard_map/ppermute | solution.py:35
  47.9 8.2 %collective-permute-start.18 = (bf16[448,256]{1,0:T(8,128)(2,1)S(1)}, bf16[448,256]{1,0:T(8,128)(2,1)S(1)}, u32[]{:S(2)}, u32[]{:S(2)}) collective-permute-start(bf16[448,256]{1,0:T(8,128)(2,1)S(1)} %add_convert_fusion.2), channel_id=1, source_target_pairs={{2,0},{6,2},{10,6},{14,10},{12,14},{8,12},{4,8},{0,4},{3,1},{7,3},... | collective-permute-start | bytes 688136 | tf_op jit(solution)/shard_map/ppermute | solution.py:27
  48.5 16.8 %copy-start.2 = (bf16[8,512,256]{2,1,0:T(8,128)(2,1)S(1)}, bf16[8,512,256]{2,1,0:T(8,128)(2,1)}, u32[]{:S(2)}) copy-start(bf16[8,512,256]{2,1,0:T(8,128)(2,1)} %down.3) | copy-start | bytes 6291460
  48.5 8.3 %collective-permute-start.14 = (bf16[448,256]{1,0:T(8,128)(2,1)S(1)}, bf16[448,256]{1,0:T(8,128)(2,1)S(1)}, u32[]{:S(2)}, u32[]{:S(2)}) collective-permute-start(bf16[448,256]{1,0:T(8,128)(2,1)S(1)} %add_convert_fusion.5), channel_id=1, source_target_pairs={{2,6},{6,10},{10,14},{14,12},{12,8},{8,4},{4,0},{0,2},{3,7},{7,11}... | collective-permute-start | bytes 688136 | tf_op jit(solution)/shard_map/ppermute | solution.py:27
  51.9 13.3 %collective-permute-start.24 = (bf16[128,256]{1,0:T(8,128)(2,1)S(1)}, bf16[128,256]{1,0:T(8,128)(2,1)S(1)}, u32[]{:S(2)}, u32[]{:S(2)}) collective-permute-start(bf16[128,256]{1,0:T(8,128)(2,1)S(1)} %add_convert_fusion.6), channel_id=1, source_target_pairs={{0,8},{2,10},{4,12},{6,14},{8,0},{10,2},{12,4},{14,6},{1,9},{3,11}... | collective-permute-start | bytes 196616 | tf_op jit(solution)/shard_map/ppermute | solution.py:35
  56.1 6.8 %collective-permute-start.19 = (bf16[448,256]{1,0:T(8,128)(2,1)S(1)}, bf16[448,256]{1,0:T(8,128)(2,1)S(1)}, u32[]{:S(2)}, u32[]{:S(2)}) collective-permute-start(bf16[448,256]{1,0:T(8,128)(2,1)S(1)} %add_convert_fusion.1), channel_id=1, source_target_pairs={{2,0},{6,2},{10,6},{14,10},{12,14},{8,12},{4,8},{0,4},{3,1},{7,3},... | collective-permute-start | bytes 688136 | tf_op jit(solution)/shard_map/ppermute | solution.py:27
  56.9 6.5 %collective-permute-start.16 = (bf16[448,256]{1,0:T(8,128)(2,1)S(1)}, bf16[448,256]{1,0:T(8,128)(2,1)S(1)}, u32[]{:S(2)}, u32[]{:S(2)}) collective-permute-start(bf16[448,256]{1,0:T(8,128)(2,1)S(1)} %add_convert_fusion.4), channel_id=1, source_target_pairs={{2,6},{6,10},{10,14},{14,12},{12,8},{8,4},{4,0},{0,2},{3,7},{7,11}... | collective-permute-start | bytes 688136 | tf_op jit(solution)/shard_map/ppermute | solution.py:27
  63.0 6.1 %collective-permute-start.20 = (bf16[448,256]{1,0:T(8,128)(2,1)S(1)}, bf16[448,256]{1,0:T(8,128)(2,1)S(1)}, u32[]{:S(2)}, u32[]{:S(2)}) collective-permute-start(bf16[448,256]{1,0:T(8,128)(2,1)S(1)} %add_convert_fusion), channel_id=1, source_target_pairs={{2,0},{6,2},{10,6},{14,10},{12,14},{8,12},{4,8},{0,4},{3,1},{7,3},... | collective-permute-start | bytes 688136 | tf_op jit(solution)/shard_map/ppermute | solution.py:27
  63.4 6.1 %collective-permute-start.17 = (bf16[448,256]{1,0:T(8,128)(2,1)S(1)}, bf16[448,256]{1,0:T(8,128)(2,1)S(1)}, u32[]{:S(2)}, u32[]{:S(2)}) collective-permute-start(bf16[448,256]{1,0:T(8,128)(2,1)S(1)} %add_convert_fusion.3), channel_id=1, source_target_pairs={{2,6},{6,10},{10,14},{14,12},{12,8},{8,4},{4,0},{0,2},{3,7},{7,11}... | collective-permute-start | bytes 688136 | tf_op jit(solution)/shard_map/ppermute | solution.py:27
  65.2 2.0 %collective-permute-start.25 = (f32[128,256]{1,0:T(8,128)S(1)}, f32[128,256]{1,0:T(8,128)S(1)}, u32[]{:S(2)}, u32[]{:S(2)}) collective-permute-start(f32[128,256]{1,0:T(8,128)S(1)} %convert_add_fusion.own_total), channel_id=1, source_target_pairs={{0,1},{1,0},{2,3},{3,2},{4,5},{5,4},{6,7},{7,6},{8,9},{9,8},{10,11... | collective-permute-start | bytes 393224 | tf_op jit(solution)/shard_map/ppermute | solution.py:31
  65.3 4.2 %copy-start.5 = (bf16[448,256]{1,0:T(8,128)(2,1)S(1)}, bf16[448,256]{1,0:T(8,128)(2,1)}, u32[]{:S(2)}) copy-start(bf16[448,256]{1,0:T(8,128)(2,1)} %out_grad.3) | copy-start | bytes 688132
